TPU v7x, 256 devices: a whole 4x4x8 slice. The times are simulated.
256 devices in a mesh: dp: 8 (over y, core), feat: 32 (over x, z).
Axes of the slice: x: 4, y: 4, z: 8, core: 2. Of those that a mesh axis runs over, the one named last changes fastest.
Arguments:
- node_features: bfloat16 [1024, 65536], P('feat', 'dp'), may hold values from -6 to 6
- edge_tiles: bfloat16 [512, 4, 128, 128], P('dp'), may hold values from 0.019897461 to 1
- tile_source: int32 [512, 4], P('dp'), may hold values from 0 to 63, all different within a row
- tile_count: int32 [512], P('dp'), may hold values from 1 to 4, as said below
- drop_bits: int32 [512, 16], P(('dp', 'feat')), may hold values from -2147483648 to 2147483647, as said below
- cotangent: bfloat16 [65536, 512], P(('dp', 'feat')), may hold values from -0.0625 to 0.0625
- self_first: bfloat16 [1024, 512], replicated, may hold values from -0.1875 to 0.1875
- neigh_first: bfloat16 [1024, 512], replicated, may hold values from -0.1875 to 0.1875
- self_second: bfloat16 [512, 512], replicated, may hold values from -0.25 to 0.25
- neigh_second: bfloat16 [512, 512], replicated, may hold values from -0.25 to 0.25
Outputs:
- grad_self_first: float32 [1024, 512], P('feat')
- grad_neigh_first: float32 [1024, 512], P('feat')
- grad_self_second: float32 [512, 512], P('feat')
- grad_neigh_second: float32 [512, 512], P('feat')
Inputs may be any that keep to these rules, and one draw needn't show every extreme that they name: `tile_source`: each row names 4 different source blocks; every block is named somewhere. `tile_count`: every draw has rows with one slot used and rows with all 4 used. `drop_bits`: any 32-bit pattern.
All inputs are finite; a program needn't handle non-finite values.
Results may differ from a plain program's by a relative error of at most 0.0085.
Values may be sent and summed in bfloat16 or wider, within the bound.
No kernel may reach another device: no remote copies, remote signals or barrier semaphores. Data moves between devices by JAX's collectives and lax.ppermute only.
A program may use at most 128 MiB of HBM per device.

v0:
```python
import jax
import jax.numpy as jnp
from jax import lax
from jax.sharding import PartitionSpec as P


def unpack_keep(words):
    shifts = jnp.arange(32, dtype=jnp.int32)
    flags = jnp.bitwise_and(jnp.right_shift(words[:, :, None], shifts[None, None, :]), 1)
    return flags.reshape(words.shape[0], -1).astype(jnp.float32)


def local(
    node_features,
    edge_tiles,
    tile_source,
    tile_count,
    drop_bits,
    cotangent,
    self_first,
    neigh_first,
    self_second,
    neigh_second,
):
    blocks, slots, tile_side, _ = edge_tiles.shape
    feat_cols, node_count = node_features.shape
    own_blocks = drop_bits.shape[0]
    own_rows = own_blocks * tile_side
    hidden_width = self_first.shape[1]
    block_ids = jnp.arange(blocks, dtype=jnp.int32)
    live_slot = jnp.arange(slots)[None, :] < tile_count[:, None]
    live_half = live_slot.astype(jnp.bfloat16)
    degree = jnp.einsum("btrc,bt->br", edge_tiles, live_half, preferred_element_type=jnp.float32)
    scaling = lax.rsqrt(degree)
    slot_pick = (
        (tile_source[:, :, None] == block_ids[None, None, :]) & live_slot[:, :, None]
    ).astype(jnp.bfloat16)
    source_cols = jnp.einsum(
        "fbc,kb->fkc",
        node_features.reshape(feat_cols, blocks, tile_side),
        slot_pick.reshape(blocks * slots, blocks),
        preferred_element_type=jnp.float32,
    ).astype(jnp.bfloat16)
    source_cols = source_cols.reshape(feat_cols, blocks, slots, tile_side)
    neigh_sum = jnp.einsum(
        "fbtc,btrc->fbr", source_cols, edge_tiles, preferred_element_type=jnp.float32
    )
    neigh_cols = (neigh_sum * scaling[None]).reshape(feat_cols, node_count).astype(jnp.bfloat16)
    agg_own, self_own = (
        lax.all_to_all(neigh_cols, "feat", split_axis=1, concat_axis=0, tiled=True),
        lax.all_to_all(node_features, "feat", split_axis=1, concat_axis=0, tiled=True),
    )
    contract_first = (((0,), (0,)), ((), ()))
    pre_first = lax.dot_general(
        self_own, self_first, contract_first, preferred_element_type=jnp.float32
    )
    pre_first = pre_first + lax.dot_general(
        agg_own, neigh_first, contract_first, preferred_element_type=jnp.float32
    )
    keep_mask = jnp.repeat(unpack_keep(drop_bits), tile_side, axis=0)
    sigma = jax.nn.sigmoid(pre_first)
    hidden_own = (pre_first * sigma * keep_mask * 2.0).astype(jnp.bfloat16)
    hidden_all = lax.all_gather(hidden_own, "feat", axis=0, tiled=True)
    first_block = lax.axis_index("feat") * own_blocks
    own_tiles = lax.dynamic_slice_in_dim(edge_tiles, first_block, own_blocks, 0)
    own_scaling = lax.dynamic_slice_in_dim(scaling, first_block, own_blocks, 0)
    own_pick = lax.dynamic_slice_in_dim(slot_pick, first_block, own_blocks, 0).reshape(
        own_blocks * slots, blocks
    )
    hidden_src = jnp.dot(
        own_pick,
        hidden_all.reshape(blocks, tile_side * hidden_width),
        preferred_element_type=jnp.float32,
    ).astype(jnp.bfloat16)
    hidden_src = hidden_src.reshape(own_blocks, slots, tile_side, hidden_width)
    agg_two = jnp.einsum(
        "btrc,btch->brh", own_tiles, hidden_src, preferred_element_type=jnp.float32
    )
    agg_two = (
        (agg_two * own_scaling[:, :, None]).reshape(own_rows, hidden_width).astype(jnp.bfloat16)
    )
    grad_self_second = lax.dot_general(
        hidden_own, cotangent, contract_first, preferred_element_type=jnp.float32
    )
    grad_neigh_second = lax.dot_general(
        agg_two, cotangent, contract_first, preferred_element_type=jnp.float32
    )
    contract_last = (((1,), (1,)), ((), ()))
    back_scaled = lax.dot_general(
        cotangent, neigh_second, contract_last, preferred_element_type=jnp.float32
    )
    back_scaled = (back_scaled * own_scaling.reshape(own_rows)[:, None]).astype(jnp.bfloat16)
    own_ids = first_block + jnp.arange(own_blocks, dtype=jnp.int32)
    block_select = (
        (tile_source[:, :, None] == own_ids[None, None, :]) & live_slot[:, :, None]
    ).astype(jnp.bfloat16)
    tile_lines_all = edge_tiles.transpose(0, 2, 1, 3).reshape(node_count, slots, tile_side)
    shard_rows = lax.all_gather(back_scaled, "feat", axis=0, tiled=True)
    piece_len = shard_rows.shape[0]
    row_block = jnp.arange(piece_len, dtype=jnp.int32) // tile_side
    row_hot = (row_block[:, None] == block_ids[None, :]).astype(jnp.bfloat16)
    chosen = jnp.einsum(
        "pb,bts->pts", row_hot, block_select, preferred_element_type=jnp.float32
    ).astype(jnp.bfloat16)
    weights = jnp.einsum(
        "ptc,pts->psc", tile_lines_all, chosen, preferred_element_type=jnp.float32
    ).astype(jnp.bfloat16)
    added = jnp.einsum("psc,ph->sch", weights, shard_rows, preferred_element_type=jnp.float32)
    back = added.reshape(own_rows, hidden_width)
    d_hidden = (
        lax.dot_general(cotangent, self_second, contract_last, preferred_element_type=jnp.float32)
        + back
    )
    d_pre = (d_hidden * sigma * (1.0 + pre_first * (1.0 - sigma)) * keep_mask * 2.0).astype(
        jnp.bfloat16
    )
    grad_self_first = jnp.dot(self_own, d_pre, preferred_element_type=jnp.float32)
    grad_neigh_first = jnp.dot(agg_own, d_pre, preferred_element_type=jnp.float32)
    shares = (
        lax.psum_scatter(grad_self_first, "feat", scatter_dimension=0, tiled=True),
        lax.psum_scatter(grad_neigh_first, "feat", scatter_dimension=0, tiled=True),
        lax.psum_scatter(grad_self_second, "feat", scatter_dimension=0, tiled=True),
        lax.psum_scatter(grad_neigh_second, "feat", scatter_dimension=0, tiled=True),
    )
    summed = lax.psum((shares[0], shares[1], shares[2], shares[3]), "dp")
    return (summed[0], summed[1], summed[2], summed[3])


def solution(mesh):
    return jax.shard_map(
        local,
        mesh=mesh,
        in_specs=(
            P("feat", "dp"),
            P("dp", None, None, None),
            P("dp", None),
            P("dp"),
            P(("dp", "feat"), None),
            P(("dp", "feat"), None),
            P(),
            P(),
            P(),
            P(),
        ),
        out_specs=(P("feat", None), P("feat", None), P("feat", None), P("feat", None)),
        check_vma=False,
    )
```

profile of v0, /device:TPU:1, one launch (start us, length us, event | category | flops | bytes accessed | tf_op | source)
XLA Modules:
  0.0 1229.4 jit_solution(5655088159161348213)
XLA Ops:
  7.3 5.8 convert_reduce_fusion
  15.4 11.9 all-to-all-start
  28.5 6.1 fusion.21
  36.1 6.2 all-to-all-done
  42.3 9.8 all-to-all-start.1
  52.4 1.7 fusion.54
  54.1 14.1 %all-to-all-done.1 = bf16[32,32,256]{2,0,1:T(8,128)(2,1)S(1)} async-done(((bf16[32,32,256]{2,0,1:T(8,128)(2,1)}), bf16[32,32,256]{2,0,1:T(8,128)(2,1)S(1)}, u32[]{:S(2)}, u32[]{:S(2)}) %all-to-all-start.1) | async-done | bytes 524320 | tf_op jit(solution)/shard_map/all_to_all | solution.py:50
  68.2 1.3 fusion.34
  69.8 10.4 copy.39
  80.8 6.9 copy.40
  87.7 31.4 %fusion.4 = bf16[8192,2,128]{2,1,0:T(2,128)(2,1)} fusion(bf16[8192,4,2]{1,2,0:T(2,128)(2,1)} %copy.40, bf16[8192,4,128]{2,0,1:T(8,128)(2,1)} %bitcast.89), kind=kOutput, calls=%fused_computation.7 | convolution fusion | flops 18874368 | bytes 12713984 | tf_op jit(solution)/shard_map/ptc,pts->psc/dot_general | solution.py:105
  119.1 2.4 all-gather.3.cloned.1.call-done
  121.4 7.0 fusion
  130.2 1.8 copy.54
  132.4 1.7 fusion.55
  134.2 1.3 fusion.56
  135.7 83.7 %all-gather.5.cloned.1.call-done = bf16[8192,512]{1,0:T(8,128)(2,1)} async-done(((bf16[256,512]{1,0:T(8,128)(2,1)}), bf16[8192,512]{1,0:T(8,128)(2,1)}) %all-gather.5.cloned.1.call-update) | async-done | bytes 8388624 | tf_op jit(solution)/shard_map/all_gather | solution.py:63
  219.4 10.6 reshape.102
  230.0 4.7 convolution_convert_fusion
  235.0 1.3 fusion.29
  236.3 1.3 fusion.57
  237.7 194.0 %reduce-scatter.13.cloned.1.call-done = f32[32,512]{1,0:T(8,128)} async-done(((f32[1024,512]{1,0:T(8,128)}), f32[32,512]{1,0:T(8,128)}) %reduce-scatter.13.cloned.1.call-update) | async-done | bytes 65552
  431.7 1.7 copy.55
  433.4 217.2 %reduce-scatter.7.cloned.1.call-done = f32[32,512]{1,0:T(8,128)} async-done(((f32[1024,512]{1,0:T(8,128)}), f32[32,512]{1,0:T(8,128)}) %reduce-scatter.7.cloned.1.call-update) | async-done | bytes 65552 | tf_op jit(solution)/shard_map/reduce_scatter | solution.py:121
  650.7 216.0 %reduce-scatter.9.cloned.1.call-done = f32[16,512]{1,0:T(8,128)} async-done(((f32[512,512]{1,0:T(8,128)}), f32[16,512]{1,0:T(8,128)}) %reduce-scatter.9.cloned.1.call-update) | async-done | bytes 32784 | tf_op jit(solution)/shard_map/reduce_scatter | solution.py:122
  866.7 216.4 %reduce-scatter.11.cloned.1.call-done = f32[16,512]{1,0:T(8,128)} async-done(((f32[512,512]{1,0:T(8,128)}), f32[16,512]{1,0:T(8,128)}) %reduce-scatter.11.cloned.1.call-update) | async-done | bytes 32784 | tf_op jit(solution)/shard_map/reduce_scatter | solution.py:123
  1083.1 69.6 %all-reduce.7.cloned.1.call-done = (f32[32,512]{0,1:T(8,128)}, f32[32,512]{1,0:T(8,128)}) async-done(((f32[32,512]{0,1:T(8,128)}, f32[32,512]{1,0:T(8,128)}), (f32[32,512]{0,1:T(8,128)}, f32[32,512]{1,0:T(8,128)})) %all-reduce.7.cloned.1.call-update) | async-done | bytes 131088 | tf_op jit(solution)/shard_map/psum | solution.py:125
  1152.7 1.7 copy.49
  1154.3 64.0 %all-reduce.5.cloned.1.call-done = (f32[16,512]{1,0:T(8,128)}, f32[16,512]{1,0:T(8,128)}) async-done(((f32[16,512]{1,0:T(8,128)}, f32[16,512]{1,0:T(8,128)}), (f32[16,512]{1,0:T(8,128)}, f32[16,512]{1,0:T(8,128)})) %all-reduce.5.cloned.1.call-update) | async-done | bytes 65552 | tf_op jit(solution)/shard_map/psum | solution.py:125
  1218.3 1.5 copy.84
  1219.8 1.4 copy.85
  1221.2 1.4 copy.86
  (79 shorter events, 8.8 us)
Async XLA Ops:
  7.2 61.1 %copy-start = (bf16[1024,512]{1,0:T(8,128)(2,1)S(1)}, bf16[1024,512]{1,0:T(8,128)(2,1)}, u32[]{:S(2)}) copy-start(bf16[1024,512]{1,0:T(8,128)(2,1)} %param.17) | copy-start | bytes 3145732
  7.2 114.3 %all-gather.3.cloned.1.call-start = ((), (), s32[]{:S(2)}) async-start(), calls=%async_computation.6 | async-start | bytes 8650752 | tf_op jit(solution)/shard_map/all_gather | solution.py:98
  7.2 5.9 copy-start.14
  7.2 6.2 copy-start.6
  7.3 6.2 copy-start.11
  7.3 7.3 copy-start.8
  13.1 14.3 %copy-start.12 = (s32[64,4]{0,1:T(4,128)S(1)}, s32[64,4]{0,1:T(4,128)}, u32[]{:S(2)}) copy-start(s32[64,4]{0,1:T(4,128)} %param.12) | copy-start | bytes 3076
  15.4 26.9 %all-to-all-start = ((bf16[32,32,256]{2,0,1:T(8,128)(2,1)}), bf16[32,32,256]{2,0,1:T(8,128)(2,1)S(1)}, u32[]{:S(2)}, u32[]{:S(2)}) async-start(bf16[32,32,256]{2,0,1:T(8,128)(2,1)} %bitcast.88), calls=%async_computation | async-start | bytes 1048576 | tf_op jit(solution)/shard_map/all_to_all | solution.py:51
  34.6 17.5 %copy-start.13 = (s32[2,16]{1,0:T(2,128)S(1)}, s32[2,16]{1,0:T(2,128)}, u32[]{:S(2)}) copy-start(s32[2,16]{1,0:T(2,128)} %param.14) | copy-start | bytes 388
  42.3 38.0 %copy-start.2 = (bf16[32,32,256]{2,0,1:T(8,128)(2,1)}, bf16[32,32,256]{2,0,1:T(8,128)(2,1)S(1)}, u32[]{:S(2)}) copy-start(bf16[32,32,256]{2,0,1:T(8,128)(2,1)S(1)} %all-to-all-done) | copy-start | bytes 1572868
  42.3 25.9 %all-to-all-start.1 = ((bf16[32,32,256]{2,0,1:T(8,128)(2,1)}), bf16[32,32,256]{2,0,1:T(8,128)(2,1)S(1)}, u32[]{:S(2)}, u32[]{:S(2)}) async-start(bf16[32,32,256]{2,0,1:T(8,128)(2,1)} %copy.47), calls=%async_computation.1 | async-start | bytes 1048576 | tf_op jit(solution)/shard_map/all_to_all | solution.py:50
  52.1 167.4 %all-gather.5.cloned.1.call-start = ((), (), s32[]{:S(2)}) async-start(), calls=%async_computation.9 | async-start | bytes 8650752 | tf_op jit(solution)/shard_map/all_gather | solution.py:63
  68.2 12.0 copy-start.4
  69.5 362.2 %reduce-scatter.13.cloned.1.call-start = ((), (), s32[]{:S(2)}) async-start(), calls=%async_computation.11 | async-start | bytes 2162688
  119.1 9.5 copy-start.15
  128.5 1.3 copy-start.3
  129.0 0.7 copy-start.9
  129.7 2.6 copy-start.5
  130.2 2.2 copy-start.10
  132.0 2.1 copy-start.7
  132.1 518.6 %reduce-scatter.7.cloned.1.call-start = ((), (), s32[]{:S(2)}) async-start(), calls=%async_computation.7 | async-start | bytes 2162688 | tf_op jit(solution)/shard_map/reduce_scatter | solution.py:121
  134.1 732.6 %reduce-scatter.9.cloned.1.call-start = ((), (), s32[]{:S(2)}) async-start(), calls=%async_computation.8 | async-start | bytes 1081344 | tf_op jit(solution)/shard_map/reduce_scatter | solution.py:122
  135.5 947.5 %reduce-scatter.11.cloned.1.call-start = ((), (), s32[]{:S(2)}) async-start(), calls=%async_computation.10 | async-start | bytes 1081344 | tf_op jit(solution)/shard_map/reduce_scatter | solution.py:123
  230.0 992.5 %copy-start.1 = (bf16[1024,512]{1,0:T(8,128)(2,1)S(1)}, bf16[1024,512]{1,0:T(8,128)(2,1)}, u32[]{:S(2)}) copy-start(bf16[1024,512]{1,0:T(8,128)(2,1)} %param.17) | copy-start | bytes 3145732
  237.7 915.0 %all-reduce.7.cloned.1.call-start = ((), (), s32[]{:S(2)}) async-start(), calls=%async_computation.13 | async-start | bytes 655360 | tf_op jit(solution)/shard_map/psum | solution.py:125
  650.7 567.7 %all-reduce.5.cloned.1.call-start = ((), (), s32[]{:S(2)}) async-start(), calls=%async_computation.12 | async-start | bytes 131072 | tf_op jit(solution)/shard_map/psum | solution.py:125
Sparse Core Ops, SparseCore 0:
  14.7 106.7 all-gather.2
  124.0 95.3 all-gather.4
  223.3 208.3 reduce-scatter.12
  435.9 214.6 reduce-scatter.6
  654.3 212.3 reduce-scatter.8
  870.4 212.6 reduce-scatter.10
  1085.5 67.0 all-reduce.6
  1155.2 63.1 all-reduce.4
where the time goes:
time: 1230 us
  waiting for transfers between devices  1080 us (88%)
  matrix products  61.2 us (5%)
  local copies, waits for them, and re-layouts  41.6 us (3%)
  starting transfers between devices  22.4 us (2%)
  between operations  14.5 us (1%)
    reduce_scatter x1, waiting for transfers between devices, local(): lax.psum_scatter(grad_neigh_first, 'feat', scatter_dimension=0, tiled=True)  217 us
    reduce_scatter x1, waiting for transfers between devices, local(): lax.psum_scatter(grad_neigh_second, 'feat', scatter_dimension=0, tiled=True)  216 us
    reduce_scatter x1, waiting for transfers between devices, local(): lax.psum_scatter(grad_self_second, 'feat', scatter_dimension=0, tiled=True)  216 us
    unnamed x9, waiting for transfers between devices  194 us
    psum x2, waiting for transfers between devices, local(): summed = lax.psum((shares[0], shares[1], shares[2], shares[3]), 'dp')  134 us
    all_gather x1, waiting for transfers between devices, local(): hidden_all = lax.all_gather(hidden_own, 'feat', axis=0, tiled=True)  83.7 us
    dot_general x1, matrix products, local(): jnp.einsum('ptc,pts->psc', tile_lines_all, chosen, preferred_element_type...  31.4 us
  transfers between devices with their start and end apart: 10, of which 10 were waited for; matrix products, arithmetic and copies ran while one was open for 8% of the time, Pallas kernels for 0%

commit v1 on v0

v1 whole, which is shorter than its diff:
```python
import functools

import jax
import jax.numpy as jnp
from jax import lax
from jax.experimental import pallas as pl
from jax.experimental.pallas import tpu as pltpu
from jax.sharding import PartitionSpec as P

BF = jnp.bfloat16
F32 = jnp.float32
STEP = 8
LAST = (((1,), (1,)), ((), ()))


def alive(count, slot):
    return jnp.where(slot < count, 1.0, 0.0).astype(F32)


def agg_kernel(source_ref, count_ref, x_ref, tiles_ref, agg_ref, scale_ref):
    slots, side = tiles_ref.shape[1], tiles_ref.shape[2]
    rows = x_ref.shape[0]
    for j in range(STEP):
        b = pl.program_id(0) * STEP + j
        count = count_ref[b]
        parts = []
        for t in range(slots):
            start = pl.multiple_of(source_ref[b, t] * side, side)
            x = x_ref[:, pl.ds(start, side)]
            x = jnp.concatenate([x, jnp.ones((16, side), BF)], axis=0)
            parts.append(x * jnp.full((rows + 16, side), alive(count, t), F32).astype(BF))
        lhs = jnp.concatenate(parts, axis=1)
        rhs = jnp.concatenate([tiles_ref[j, t] for t in range(slots)], axis=1)
        out = lax.dot_general(lhs, rhs, LAST, preferred_element_type=F32)
        scale = lax.rsqrt(out[rows : rows + 1])
        agg_ref[j // 2, :, (j % 2) * side : (j % 2 + 1) * side] = (out[:rows] * scale).astype(BF)
        scale_ref[j : j + 1] = scale


def back_kernel(source_ref, count_ref, g_ref, scale_ref, tiles_ref, agg_ref, out_ref, acc_ref):
    slots, side = tiles_ref.shape[1], tiles_ref.shape[2]
    rows = g_ref.shape[1]
    feats = agg_ref.shape[1]

    @pl.when(pl.program_id(0) == 0)
    def _():
        acc_ref[...] = jnp.zeros_like(acc_ref)

    for j in range(STEP):
        b = pl.program_id(0) * STEP + j
        count = count_ref[b]
        g = g_ref[j // 2, :, (j % 2) * side : (j % 2 + 1) * side].astype(F32)
        g = (g * scale_ref[j : j + 1]).astype(BF)
        rhs = jnp.concatenate([tiles_ref[j, t] for t in range(slots)], axis=1)
        out = jnp.dot(g, rhs, preferred_element_type=F32)
        for t in range(slots):
            src = source_ref[b, t]
            acc_ref[src] = acc_ref[src] + out[:, t * side : (t + 1) * side] * alive(count, t)

    @pl.when(pl.program_id(0) == pl.num_programs(0) - 1)
    def _():
        out_ref[:, :feats, :] = agg_ref[...]
        for o in range(out_ref.shape[0]):
            out_ref[o, feats:, :side] = acc_ref[2 * o].astype(BF)
            out_ref[o, feats:, side:] = acc_ref[2 * o + 1].astype(BF)


def grad_kernel(core_ref, one_ref, two_ref, g_ref, keep_ref, wsf_ref, wnf_ref, wss_ref, wns_ref, out_ref):
    owners, _, width = one_ref.shape
    feats = 32
    cols = two_ref.shape[1] - feats
    side = width // 2
    xt = one_ref[:, :feats, :].reshape(owners * feats, width)
    at = two_ref[:, :feats, :].reshape(owners * feats, width)
    qt = two_ref[:, feats:, :].reshape(owners * cols, width)
    g = g_ref[...]
    pre = jnp.dot(wsf_ref[...], xt, preferred_element_type=F32)
    pre = pre + jnp.dot(wnf_ref[...], at, preferred_element_type=F32)
    hidden_width = pre.shape[0]
    keep = jnp.concatenate(
        [
            jnp.broadcast_to(keep_ref[:, 0:1], (hidden_width, side)),
            jnp.broadcast_to(keep_ref[:, 1:2], (hidden_width, side)),
        ],
        axis=1,
    )
    sigma = jax.nn.sigmoid(pre)
    hidden = (pre * sigma * keep).astype(BF)
    back = lax.dot_general(wss_ref[...], g, LAST, preferred_element_type=F32)
    back = back + jnp.dot(wns_ref[...], qt, preferred_element_type=F32)
    d_pre = (back * sigma * (1.0 + pre * (1.0 - sigma)) * keep).astype(BF)
    core = core_ref[0]
    ys = out_ref.shape[1]
    for half in range(2):
        place = jnp.bitwise_xor(core, half)
        first = lax.dot_general(at if half else xt, d_pre, LAST, preferred_element_type=F32).astype(BF)
        if half:
            second = lax.dot_general(hidden, qt, LAST, preferred_element_type=F32).astype(BF)
        else:
            second = jnp.dot(hidden, g, preferred_element_type=F32).astype(BF)
        for y in range(ys):
            cut = slice(y * 128, (y + 1) * 128)
            out_ref[place, y, :, :feats, :] = first[:, cut].reshape(owners, feats, 128)
            out_ref[place, y, :, feats:, :] = second[:, cut].reshape(owners, cols, 128)


def params():
    return pltpu.CompilerParams(vmem_limit_bytes=48 * 1024 * 1024)


def smem():
    return pl.BlockSpec(memory_space=pltpu.SMEM)


def vmem():
    return pl.BlockSpec(memory_space=pltpu.VMEM)


def local(
    node_features,
    edge_tiles,
    tile_source,
    tile_count,
    drop_bits,
    cotangent,
    self_first,
    neigh_first,
    self_second,
    neigh_second,
    owners,
    replicas,
):
    blocks, slots, side, _ = edge_tiles.shape
    feats, nodes = node_features.shape
    width = nodes // owners
    hidden_width = self_first.shape[1]
    cols = hidden_width // owners
    steps = blocks // STEP
    own = STEP * side // width

    send = jnp.concatenate(
        [
            node_features.reshape(feats, owners, width).transpose(1, 0, 2),
            cotangent.T.reshape(owners, cols, width),
        ],
        axis=1,
    )
    one = lax.all_to_all(send, "feat", split_axis=0, concat_axis=0, tiled=True)

    tiles_spec = pl.BlockSpec((STEP, slots, side, side), lambda i: (i, 0, 0, 0))
    agg, scaling = pl.pallas_call(
        agg_kernel,
        grid=(steps,),
        in_specs=[smem(), smem(), pl.BlockSpec((feats, nodes), lambda i: (0, 0)), tiles_spec],
        out_specs=[
            pl.BlockSpec((own, feats, width), lambda i: (i, 0, 0)),
            pl.BlockSpec((STEP, side), lambda i: (i, 0)),
        ],
        out_shape=[
            jax.ShapeDtypeStruct((owners, feats, width), BF),
            jax.ShapeDtypeStruct((blocks, side), F32),
        ],
        compiler_params=params(),
        cost_estimate=pl.CostEstimate(flops=2 * 48 * 512 * 8192, bytes_accessed=10 << 20, transcendentals=0),
        name="agg",
    )(tile_source, tile_count, node_features, edge_tiles)

    send = pl.pallas_call(
        back_kernel,
        grid=(steps,),
        in_specs=[
            smem(),
            smem(),
            pl.BlockSpec((own, cols, width), lambda i: (i, 0, 0)),
            pl.BlockSpec((STEP, side), lambda i: (i, 0)),
            tiles_spec,
            pl.BlockSpec((owners, feats, width), lambda i: (0, 0, 0)),
        ],
        out_specs=pl.BlockSpec((owners, feats + cols, width), lambda i: (0, 0, 0)),
        out_shape=jax.ShapeDtypeStruct((owners, feats + cols, width), BF),
        scratch_shapes=[pltpu.VMEM((blocks, cols, side), F32)],
        compiler_params=params(),
        cost_estimate=pl.CostEstimate(flops=2 * 16 * 512 * 8192, bytes_accessed=10 << 20, transcendentals=0),
        name="back",
    )(tile_source, tile_count, one[:, feats:, :], scaling, edge_tiles, agg)
    two = lax.all_to_all(send, "feat", split_axis=0, concat_axis=0, tiled=True)

    shifts = jnp.arange(32, dtype=jnp.int32)
    bits = jnp.bitwise_and(jnp.right_shift(drop_bits[:, :, None], shifts), 1)
    keep = (bits.reshape(drop_bits.shape[0], hidden_width).astype(F32) * 2.0).T
    where = lax.axis_index("dp")
    core = where % 2
    ys = replicas // 2
    rows = feats + cols
    partial = pl.pallas_call(
        grad_kernel,
        in_specs=[smem()] + [vmem()] * 8,
        out_specs=vmem(),
        out_shape=jax.ShapeDtypeStruct((2, ys, owners, rows, 128), BF),
        compiler_params=params(),
        cost_estimate=pl.CostEstimate(flops=1600 << 20, bytes_accessed=9 << 20, transcendentals=1 << 17),
        name="grads",
    )(
        core.reshape(1),
        one,
        two,
        cotangent,
        keep,
        self_first.T,
        neigh_first.T,
        self_second,
        neigh_second,
    )

    other = lax.ppermute(partial[1], "dp", [(i, i ^ 1) for i in range(replicas)])
    pair = partial[0].astype(F32) + other.astype(F32)
    y = where // 2

    def of(k):
        return lax.dynamic_index_in_dim(pair, (y + k) % ys, 0, keepdims=False).astype(BF)

    def to(k):
        return [(i, ((i // 2 + k) % ys) * 2 + i % 2) for i in range(replicas)]

    total = of(0).astype(F32)
    for k in range(1, ys):
        total = total + lax.ppermute(of(k), "dp", to(k)).astype(F32)
    shares = lax.all_to_all(total.astype(BF), "feat", split_axis=0, concat_axis=0, tiled=True)
    share = jnp.sum(shares.astype(F32), axis=0)
    spread = jnp.broadcast_to(share[None], (replicas, rows, 128))
    spread = lax.all_to_all(spread, "dp", split_axis=0, concat_axis=0, tiled=True)
    spread = spread.reshape(ys, 2, rows, 128).transpose(1, 2, 0, 3).reshape(2, rows, hidden_width)
    return (spread[0, :feats], spread[1, :feats], spread[0, feats:], spread[1, feats:])


def solution(mesh):
    return jax.shard_map(
        functools.partial(local, owners=mesh.shape["feat"], replicas=mesh.shape["dp"]),
        mesh=mesh,
        in_specs=(
            P("feat", "dp"),
            P("dp", None, None, None),
            P("dp", None),
            P("dp"),
            P(("dp", "feat"), None),
            P(("dp", "feat"), None),
            P(),
            P(),
            P(),
            P(),
        ),
        out_specs=(P("feat", None), P("feat", None), P("feat", None), P("feat", None)),
        check_vma=False,
    )
```

time: 1230 us -> 145 us (0.12)
  waiting for transfers between devices: 1080 us -> 49 us
  matrix products: 61.2 us -> 0 us
  local copies, waits for them, and re-layouts: 41.6 us -> 12.1 us
  blocking collectives: 0 us -> 28 us
  Pallas kernels: 0 us -> 20.6 us
  between operations: 14.5 us -> 0.81 us
    reduce_scatter x3 -> x0, waiting for transfers between devices: 650 us -> none  [the longest x1 217 us: local(): lax.psum_scatter(grad_neigh_first, 'feat', scatter_dimension=0, tiled=True)]
    unnamed x9 -> x0, waiting for transfers between devices: 194 us -> none
    psum x2 -> x0, waiting for transfers between devices: 134 us -> none  [local(): summed = lax.psum((shares[0], shares[1], shares[2], shares[3]), 'dp')]
    all_gather x2 -> x0, waiting for transfers between devices: 86.1 us -> none  [the longest x1 83.7 us: local(): hidden_all = lax.all_gather(hidden_own, 'feat', axis=0, tiled=True)]
    dot_general x16 -> x0, matrix products: 61.2 us -> none  [the longest x1 31.4 us: local(): jnp.einsum('ptc,pts->psc', tile_lines_all, chosen, preferred_element_type...]
    all_to_all x0 -> x2, blocking collectives: none -> 28 us  [the longest x1 15 us: local(): lax.all_to_all(total.astype(BF), 'feat', split_axis=0, concat_axis=0, til...]
    pallas_call x0 -> x3, Pallas kernels: none -> 20.6 us  [the longest x1 7.69 us: local(): pl.pallas_call(back_kernel, grid=(steps,), in_specs=[smem(), smem(), pl.B...]
    ppermute x0 -> x4, waiting for transfers between devices: none -> 20.2 us  [the longest x3 16.8 us: local(): total = total + lax.ppermute(of(k), 'dp', to(k)).astype(F32)]
  transfers between devices with their start and end apart: 10 -> 6, of which waited for: 10 -> 5; matrix products, arithmetic and copies ran while one was open for 8% -> 2% of each run, Pallas kernels for 0% -> 5%
where the time goes in v1:
time: 145 us; the launch traced here: 144 us
  waiting for transfers between devices  49 us (34%)
  starting transfers between devices  29.4 us (20%)
  blocking collectives  28 us (19%)
  Pallas kernels  20.6 us (14%)
  local copies, waits for them, and re-layouts  12.1 us (8%)
  other arithmetic  4.16 us (3%)
    all_to_all x1, waiting for transfers between devices, local(): two = lax.all_to_all(send, 'feat', split_axis=0, concat_axis=0, tiled=True)  17.4 us
    ppermute x3, waiting for transfers between devices, local(): total = total + lax.ppermute(of(k), 'dp', to(k)).astype(F32)  16.8 us
    all_to_all x1, blocking collectives, local(): lax.all_to_all(total.astype(BF), 'feat', split_axis=0, concat_axis=0, til...  15 us
    all_to_all x1, blocking collectives, local(): lax.all_to_all(spread, 'dp', split_axis=0, concat_axis=0, tiled=True)  13 us
    all_to_all x1, starting transfers between devices, local(): one = lax.all_to_all(send, 'feat', split_axis=0, concat_axis=0, tiled=True)  11.9 us
    all_to_all x1, waiting for transfers between devices, local(): one = lax.all_to_all(send, 'feat', split_axis=0, concat_axis=0, tiled=True)  11.5 us
    all_to_all x1, starting transfers between devices, local(): two = lax.all_to_all(send, 'feat', split_axis=0, concat_axis=0, tiled=True)  8.6 us
    pallas_call x1, Pallas kernels, local(): pl.pallas_call(back_kernel, grid=(steps,), in_specs=[smem(), smem(), pl.B...  7.69 us
  transfers between devices with their start and end apart: 6, of which 5 were waited for; matrix products, arithmetic and copies ran while one was open for 2% of the time, Pallas kernels for 5%

profile of v1, /device:TPU:1, one launch (start us, length us, event | category | flops | bytes accessed | tf_op | source)
XLA Modules:
  0.0 144.1 jit_solution(8069777975993870624)
XLA Ops:
  0.6 1.1 copy.36
  1.7 1.1 copy.48
  2.9 0.9 pad_maximum_fusion
  3.8 11.9 %all-to-all-start = ((bf16[32,48,256]{2,1,0:T(8,128)(2,1)}), bf16[32,48,256]{2,1,0:T(8,128)(2,1)S(1)}, u32[]{:S(2)}, u32[]{:S(2)}) async-start(bf16[32,48,256]{2,1,0:T(8,128)(2,1)} %pad_maximum_fusion), calls=%async_computation | async-start | bytes 1572864 | tf_op jit(solution)/shard_map/all_to_all | solution.py:148
  15.7 0.1 copy.38.source_ref
  15.8 7.7 %agg.1 = (bf16[32,32,256]{2,1,0:T(8,128)(2,1)S(1)}, f32[64,128]{1,0:T(8,128)S(1)}) custom-call(s32[64,4]{1,0:T(8,128)S(1)} %copy.38.source_ref, s32[64]{0:T(128)S(1)} %copy-done.4, bf16[32,8192]{1,0:T(8,128)(2,1)S(1)} %copy-done, bf16[64,4,128,128]{3,2,1,0:T(8,128)(2,1)} %tiles_ref.3), custom_call_target="tpu_custom_call" | custom-call | flops 402653184 | bytes 10485760 | tf_op jit(solution)/shard_map/agg/pallas_call | solution.py:151
  23.5 11.5 %all-to-all-done.one_ref = bf16[32,48,256]{2,1,0:T(8,128)(2,1)S(1)} async-done(((bf16[32,48,256]{2,1,0:T(8,128)(2,1)}), bf16[32,48,256]{2,1,0:T(8,128)(2,1)S(1)}, u32[]{:S(2)}, u32[]{:S(2)}) %all-to-all-start) | async-done | bytes 786464 | tf_op jit(solution)/shard_map/all_to_all | solution.py:148
  35.0 7.7 %back.1 = bf16[32,48,256]{2,1,0:T(8,128)(2,1)} custom-call(s32[64,4]{1,0:T(8,128)S(1)} %copy.38.source_ref, s32[64]{0:T(128)S(1)} %copy-done.4, bf16[32,16,256]{2,1,0:T(8,128)(2,1)S(1)} %slice.28.g_ref, f32[64,128]{1,0:T(8,128)S(1)} %get-tuple-element.6.scale_ref, bf16[64,4,128,128]{3,2,1,0:T(8,128)(2,1)} %tiles_ref.3, ...), custom_call_target="tpu_custom_call" | custom-call | flops 134217728 | bytes 10485760 | tf_op jit(solution)/shard_map/back/pallas_call | solution.py:168
  42.6 8.6 %all-to-all-start.1 = ((bf16[32,48,256]{2,1,0:T(8,128)(2,1)}), bf16[32,48,256]{2,1,0:T(8,128)(2,1)}, u32[]{:S(2)}, u32[]{:S(2)}) async-start(bf16[32,48,256]{2,1,0:T(8,128)(2,1)} %back.1), calls=%async_computation.1 | async-start | bytes 1572864 | tf_op jit(solution)/shard_map/all_to_all | solution.py:186
  51.3 0.1 copy.39
  51.5 0.5 copy.41
  52.0 1.5 %copy.42 = bf16[1024,512]{0,1:T(8,128)(2,1)S(1)} copy(bf16[1024,512]{1,0:T(8,128)(2,1)} %param.17) | data formatting | bytes 2097152 | tf_op args[7]
  53.5 0.1 fusion.9
  53.7 17.4 %all-to-all-done.1.two_ref = bf16[32,48,256]{2,1,0:T(8,128)(2,1)} async-done(((bf16[32,48,256]{2,1,0:T(8,128)(2,1)}), bf16[32,48,256]{2,1,0:T(8,128)(2,1)}, u32[]{:S(2)}, u32[]{:S(2)}) %all-to-all-start.1) | async-done | bytes 786464 | tf_op jit(solution)/shard_map/all_to_all | solution.py:186
  71.0 1.0 copy-done.2
  72.1 1.0 copy-done.3
  73.1 5.3 %grads.1 = bf16[2,4,32,48,128]{4,3,2,1,0:T(8,128)(2,1)} custom-call(s32[1]{0:T(128)} %bitcast.core_ref, bf16[32,48,256]{2,1,0:T(8,128)(2,1)S(1)} %all-to-all-done.one_ref, bf16[32,48,256]{2,1,0:T(8,128)(2,1)} %all-to-all-done.1.two_ref, bf16[256,512]{1,0:T(8,128)(2,1)S(1)} %copy-done.1, f32[512,2]{1,0:T(8,128)S(1)} %bitcast.58, ...), custom_call_target="tpu_custom_call" | custom-call | flops 1677721600 | bytes 9437184 | tf_op jit(solution)/shard_map/grads/pallas_call | solution.py:195
  78.4 2.9 %slice_bitcast_fusion = bf16[4,32,48,128]{3,2,1,0:T(8,128)(2,1)} fusion(bf16[2,4,32,48,128]{4,3,2,1,0:T(8,128)(2,1)} %grads.1), kind=kLoop, calls=%fused_computation.1 | loop fusion | bytes 3145728 | tf_op jit(solution)/shard_map/squeeze | solution.py:215
  81.3 4.5 %collective-permute-start = (bf16[4,32,48,128]{3,2,1,0:T(8,128)(2,1)}, bf16[4,32,48,128]{3,2,1,0:T(8,128)(2,1)}, u32[]{:S(2)}, u32[]{:S(2)}) collective-permute-start(bf16[4,32,48,128]{3,2,1,0:T(8,128)(2,1)} %slice_bitcast_fusion), channel_id=1, source_target_pairs={{0,32},{32,0},{64,96},{96,64},{128,160},{160,128},{192,224},{224,1... | collective-permute-start | bytes 4718600 | tf_op jit(solution)/shard_map/ppermute | solution.py:215
  85.8 3.4 %collective-permute-done = bf16[4,32,48,128]{3,2,1,0:T(8,128)(2,1)} collective-permute-done((bf16[4,32,48,128]{3,2,1,0:T(8,128)(2,1)}, bf16[4,32,48,128]{3,2,1,0:T(8,128)(2,1)}, u32[]{:S(2)}, u32[]{:S(2)}) %collective-permute-start) | collective-permute-done | bytes 1572896 | tf_op jit(solution)/shard_map/ppermute | solution.py:215
  89.2 1.8 %convert_add_fusion = bf16[4,32,48,128]{3,2,1,0:T(8,128)(2,1)S(1)} fusion(bf16[4,32,48,128]{3,2,1,0:T(8,128)(2,1)} %collective-permute-done, bf16[2,4,32,48,128]{4,3,2,1,0:T(8,128)(2,1)S(1)} %copy-done.5), kind=kLoop, calls=%fused_computation | loop fusion | flops 3145728 | bytes 4718592 | tf_op jit(solution)/shard_map/add | solution.py:216
  91.0 1.2 copy-done.6
  92.2 1.4 collective-permute-start.1
  93.6 1.5 %collective-permute-start.3 = (bf16[32,48,128]{2,1,0:T(8,128)(2,1)S(1)}, bf16[32,48,128]{2,1,0:T(8,128)(2,1)S(1)}, u32[]{:S(2)}, u32[]{:S(2)}) collective-permute-start(bf16[32,48,128]{2,1,0:T(8,128)(2,1)S(1)} %get-tuple-element.9), channel_id=1, source_target_pairs={{0,192},{32,224},{64,0},{96,32},{128,64},{160,96},{192,128},{224,1... | collective-permute-start | bytes 1179656 | tf_op jit(solution)/shard_map/ppermute | solution.py:227
  95.1 1.6 %collective-permute-start.2 = (bf16[32,48,128]{2,1,0:T(8,128)(2,1)S(1)}, bf16[32,48,128]{2,1,0:T(8,128)(2,1)S(1)}, u32[]{:S(2)}, u32[]{:S(2)}) collective-permute-start(bf16[32,48,128]{2,1,0:T(8,128)(2,1)S(1)} %get-tuple-element.10), channel_id=1, source_target_pairs={{0,128},{32,160},{64,192},{96,224},{128,0},{160,32},{192,64},{224,... | collective-permute-start | bytes 1179656 | tf_op jit(solution)/shard_map/ppermute | solution.py:227
  96.7 7.3 %collective-permute-done.1 = bf16[32,48,128]{2,1,0:T(8,128)(2,1)S(1)} collective-permute-done((bf16[32,48,128]{2,1,0:T(8,128)(2,1)S(1)}, bf16[32,48,128]{2,1,0:T(8,128)(2,1)S(1)}, u32[]{:S(2)}, u32[]{:S(2)}) %collective-permute-start.1) | collective-permute-done | bytes 393248 | tf_op jit(solution)/shard_map/ppermute | solution.py:227
  104.0 9.5 %collective-permute-done.2 = bf16[32,48,128]{2,1,0:T(8,128)(2,1)S(1)} collective-permute-done((bf16[32,48,128]{2,1,0:T(8,128)(2,1)S(1)}, bf16[32,48,128]{2,1,0:T(8,128)(2,1)S(1)}, u32[]{:S(2)}, u32[]{:S(2)}) %collective-permute-start.2) | collective-permute-done | bytes 393248 | tf_op jit(solution)/shard_map/ppermute | solution.py:227
  113.5 1.2 fusion.2
  114.7 15.0 %all_to_all.20 = bf16[32,48,128]{2,1,0:T(8,128)(2,1)S(1)} all-to-all(bf16[32,48,128]{2,1,0:T(8,128)(2,1)S(1)} %fusion.2), channel_id=1, replica_groups=mesh['dp'=8,'feat'=32] {'feat'}, dimensions={0} | all-to-all | bytes 786432 | tf_op jit(solution)/shard_map/all_to_all | solution.py:228
  129.8 13.0 %all_to_all.21 = f32[8,48,128]{2,1,0:T(8,128)S(1)} all-to-all(f32[8,48,128]{2,1,0:T(8,128)S(1)} %broadcast_in_dim.2), channel_id=1, replica_groups=mesh['dp'=8,'feat'=32] {'dp'}, dimensions={0} | all-to-all | bytes 393216 | tf_op jit(solution)/shard_map/all_to_all | solution.py:231
  142.8 0.6 slice_bitcast_fusion.4
  143.4 0.7 slice_bitcast_fusion.2
  (25 shorter events, 0.3 us)
Async XLA Ops:
  2.8 12.9 %copy-start.8 = (s32[64,4]{0,1:T(4,128)S(1)}, s32[64,4]{0,1:T(4,128)}, u32[]{:S(2)}) copy-start(s32[64,4]{0,1:T(4,128)} %param.12) | copy-start | bytes 3076
  2.8 12.9 %copy-start = (bf16[32,8192]{1,0:T(8,128)(2,1)S(1)}, bf16[32,8192]{1,0:T(8,128)(2,1)}, u32[]{:S(2)}) copy-start(bf16[32,8192]{1,0:T(8,128)(2,1)} %x_ref.1) | copy-start | bytes 1572868
  2.8 12.9 %copy-start.4 = (s32[64]{0:T(128)S(1)}, s32[64]{0:T(128)}, u32[]{:S(2)}) copy-start(s32[64]{0:T(128)} %count_ref.3) | copy-start | bytes 772
  3.8 31.1 %all-to-all-start = ((bf16[32,48,256]{2,1,0:T(8,128)(2,1)}), bf16[32,48,256]{2,1,0:T(8,128)(2,1)S(1)}, u32[]{:S(2)}, u32[]{:S(2)}) async-start(bf16[32,48,256]{2,1,0:T(8,128)(2,1)} %pad_maximum_fusion), calls=%async_computation | async-start | bytes 1572864 | tf_op jit(solution)/shard_map/all_to_all | solution.py:148
  42.6 8.6 %copy-start.9 = (s32[2,16]{1,0:T(2,128)S(1)}, s32[2,16]{1,0:T(2,128)}, u32[]{:S(2)}) copy-start(s32[2,16]{1,0:T(2,128)} %param.14) | copy-start | bytes 388
  42.6 8.8 %copy-start.7 = (bf16[1024,512]{1,0:T(8,128)(2,1)S(1)}, bf16[1024,512]{1,0:T(8,128)(2,1)}, u32[]{:S(2)}) copy-start(bf16[1024,512]{1,0:T(8,128)(2,1)} %param.16) | copy-start | bytes 3145732
  42.6 28.4 %all-to-all-start.1 = ((bf16[32,48,256]{2,1,0:T(8,128)(2,1)}), bf16[32,48,256]{2,1,0:T(8,128)(2,1)}, u32[]{:S(2)}, u32[]{:S(2)}) async-start(bf16[32,48,256]{2,1,0:T(8,128)(2,1)} %back.1), calls=%async_computation.1 | async-start | bytes 1572864 | tf_op jit(solution)/shard_map/all_to_all | solution.py:186
  52.0 19.1 %copy-start.1 = (bf16[256,512]{1,0:T(8,128)(2,1)S(1)}, bf16[256,512]{1,0:T(8,128)(2,1)}, u32[]{:S(2)}) copy-start(bf16[256,512]{1,0:T(8,128)(2,1)} %g_ref.1) | copy-start | bytes 786436
  71.0 1.0 copy-start.2
  72.1 1.0 copy-start.3
  78.4 10.8 %copy-start.5 = (bf16[2,4,32,48,128]{4,3,2,1,0:T(8,128)(2,1)S(1)}, bf16[2,4,32,48,128]{4,3,2,1,0:T(8,128)(2,1)}, u32[]{:S(2)}) copy-start(bf16[2,4,32,48,128]{4,3,2,1,0:T(8,128)(2,1)} %grads.1) | copy-start | bytes 9437188
  81.3 7.9 %collective-permute-start = (bf16[4,32,48,128]{3,2,1,0:T(8,128)(2,1)}, bf16[4,32,48,128]{3,2,1,0:T(8,128)(2,1)}, u32[]{:S(2)}, u32[]{:S(2)}) collective-permute-start(bf16[4,32,48,128]{3,2,1,0:T(8,128)(2,1)} %slice_bitcast_fusion), channel_id=1, source_target_pairs={{0,32},{32,0},{64,96},{96,64},{128,160},{160,128},{192,224},{224,1... | collective-permute-start | bytes 4718600 | tf_op jit(solution)/shard_map/ppermute | solution.py:215
  91.0 1.2 copy-start.6
  92.2 11.7 %collective-permute-start.1 = (bf16[32,48,128]{2,1,0:T(8,128)(2,1)S(1)}, bf16[32,48,128]{2,1,0:T(8,128)(2,1)S(1)}, u32[]{:S(2)}, u32[]{:S(2)}) collective-permute-start(bf16[32,48,128]{2,1,0:T(8,128)(2,1)S(1)} %get-tuple-element.8), channel_id=1, source_target_pairs={{0,64},{32,96},{64,128},{96,160},{128,192},{160,224},{192,0},{224,... | collective-permute-start | bytes 1179656 | tf_op jit(solution)/shard_map/ppermute | solution.py:227
  93.6 10.4 %collective-permute-start.3 = (bf16[32,48,128]{2,1,0:T(8,128)(2,1)S(1)}, bf16[32,48,128]{2,1,0:T(8,128)(2,1)S(1)}, u32[]{:S(2)}, u32[]{:S(2)}) collective-permute-start(bf16[32,48,128]{2,1,0:T(8,128)(2,1)S(1)} %get-tuple-element.9), channel_id=1, source_target_pairs={{0,192},{32,224},{64,0},{96,32},{128,64},{160,96},{192,128},{224,1... | collective-permute-start | bytes 1179656 | tf_op jit(solution)/shard_map/ppermute | solution.py:227
  95.1 18.4 %collective-permute-start.2 = (bf16[32,48,128]{2,1,0:T(8,128)(2,1)S(1)}, bf16[32,48,128]{2,1,0:T(8,128)(2,1)S(1)}, u32[]{:S(2)}, u32[]{:S(2)}) collective-permute-start(bf16[32,48,128]{2,1,0:T(8,128)(2,1)S(1)} %get-tuple-element.10), channel_id=1, source_target_pairs={{0,128},{32,160},{64,192},{96,224},{128,0},{160,32},{192,64},{224,... | collective-permute-start | bytes 1179656 | tf_op jit(solution)/shard_map/ppermute | solution.py:227

commit v2 on v0

v2 whole, which is shorter than its diff:
```python
import functools

import jax
import jax.numpy as jnp
from jax import lax
from jax.experimental import pallas as pl
from jax.experimental.pallas import tpu as pltpu
from jax.sharding import PartitionSpec as P

BF = jnp.bfloat16
F32 = jnp.float32
STEP = 8
FEATS = 32
LAST = (((1,), (1,)), ((), ()))


def alive(count, slot):
    return jnp.where(slot < count, 1.0, 0.0).astype(F32)


def begin(pairs, sems):
    copies = [pltpu.make_async_copy(src, dst, sems.at[i]) for i, (src, dst) in enumerate(pairs)]
    for copy in copies:
        copy.start()
    return copies


def chunk(tiles_ref, held_ref, sems, i):
    part = pl.ds(i * STEP, STEP)
    return pltpu.make_async_copy(tiles_ref.at[part], held_ref.at[part], sems.at[i])


def prep_kernel(x_ref, g_ref, out_ref, x_held, g_held, sems):
    owners, rows, width = out_ref.shape
    copies = begin([(g_ref, g_held), (x_ref, x_held)], sems)
    copies[0].wait()
    out_ref[:, FEATS:, :] = g_held[...].T.reshape(owners, rows - FEATS, width)
    copies[1].wait()
    for o in range(owners):
        out_ref[o, :FEATS, :] = x_held[:, o * width : (o + 1) * width]


def agg_kernel(source_ref, count_ref, x_ref, tiles_ref, agg_ref, scale_ref, x_held, held_ref, x_sem, sems):
    blocks, slots, side, _ = held_ref.shape
    steps = blocks // STEP
    copies = begin([(x_ref, x_held)], x_sem)
    for i in range(steps):
        chunk(tiles_ref, held_ref, sems, i).start()
    copies[0].wait()

    @pl.loop(0, steps)
    def _(i):
        chunk(tiles_ref, held_ref, sems, i).wait()
        for j in range(STEP):
            b = i * STEP + j
            count = count_ref[b]
            parts = []
            for t in range(slots):
                start = pl.multiple_of(source_ref[b, t] * side, side)
                x = jnp.concatenate([x_held[:, pl.ds(start, side)], jnp.ones((16, side), BF)], axis=0)
                parts.append(x * jnp.full((FEATS + 16, side), alive(count, t), F32).astype(BF))
            lhs = jnp.concatenate(parts, axis=1)
            rhs = jnp.concatenate([held_ref[b, t] for t in range(slots)], axis=1)
            out = lax.dot_general(lhs, rhs, LAST, preferred_element_type=F32)
            scale = lax.rsqrt(out[FEATS : FEATS + 1])
            agg_ref[b // 2, :, (j % 2) * side : (j % 2 + 1) * side] = (out[:FEATS] * scale).astype(BF)
            scale_ref[pl.ds(b, 1)] = scale


def back_kernel(source_ref, count_ref, one_ref, scale_ref, tiles_ref, agg_ref, out_ref, acc_ref, held_ref, sems):
    blocks, slots, side, _ = held_ref.shape
    steps = blocks // STEP
    for i in range(steps):
        chunk(tiles_ref, held_ref, sems, i).start()
    acc_ref[...] = jnp.zeros_like(acc_ref)
    out_ref[:, :FEATS, :] = agg_ref[...]

    @pl.loop(0, steps)
    def _(i):
        chunk(tiles_ref, held_ref, sems, i).wait()
        for j in range(STEP):
            b = i * STEP + j
            count = count_ref[b]
            g = one_ref[b // 2, FEATS:, (j % 2) * side : (j % 2 + 1) * side].astype(F32)
            g = (g * scale_ref[pl.ds(b, 1)]).astype(BF)
            rhs = jnp.concatenate([held_ref[b, t] for t in range(slots)], axis=1)
            out = jnp.dot(g, rhs, preferred_element_type=F32)
            for t in range(slots):
                src = source_ref[b, t]
                acc_ref[src] = acc_ref[src] + out[:, t * side : (t + 1) * side] * alive(count, t)

    for o in range(out_ref.shape[0]):
        out_ref[o, FEATS:, :side] = acc_ref[2 * o].astype(BF)
        out_ref[o, FEATS:, side:] = acc_ref[2 * o + 1].astype(BF)


def upper(ref):
    owners, _, width = ref.shape
    return ref[:, :FEATS, :].reshape(owners * FEATS, width)


def lower(ref):
    owners, rows, width = ref.shape
    return ref[:, FEATS:, :].reshape(owners * (rows - FEATS), width)


def early_kernel(mine_ref, one_ref, wsf_ref, wss_ref, pre_ref, back_ref):
    pre_ref[...] = jnp.dot(wsf_ref[...], upper(one_ref), preferred_element_type=F32)
    back_ref[...] = jnp.dot(wss_ref[...], lower(mine_ref), preferred_element_type=F32)


def write_half(half, gt_ref, one_ref, two_ref, hidden, d_pre, out_ref):
    owners, rows, width = out_ref.shape
    if half:
        left, right = upper(two_ref), lower(two_ref)
    else:
        left, right = upper(one_ref), gt_ref[...].reshape(hidden.shape)
    first = lax.dot_general(left, d_pre, LAST, preferred_element_type=F32).astype(BF)
    out_ref[:, :FEATS, :] = first.reshape(owners, FEATS, width)
    second = lax.dot_general(hidden, right, LAST, preferred_element_type=F32).astype(BF)
    out_ref[:, FEATS:, :] = second.reshape(owners, rows - FEATS, width)


def send_kernel(
    core_ref,
    mine_ref,
    one_ref,
    two_ref,
    pre_ref,
    back_ref,
    keep_ref,
    wnf_ref,
    wns_ref,
    send_ref,
    hidden_ref,
    d_pre_ref,
    gt_held,
    pre_held,
    back_held,
    wnf_held,
    wns_held,
    sems,
):
    copies = begin(
        [
            (wnf_ref, wnf_held),
            (pre_ref, pre_held),
            (wns_ref, wns_held),
            (back_ref, back_held),
            (mine_ref.at[:, FEATS:, :], gt_held),
        ],
        sems,
    )
    copies[0].wait()
    pre = jnp.dot(wnf_held[...], upper(two_ref), preferred_element_type=F32)
    copies[1].wait()
    pre = pre + pre_held[...]
    hidden_width, width = pre.shape
    side = width // 2
    keep = jnp.concatenate(
        [
            jnp.broadcast_to(keep_ref[:, 0:1], (hidden_width, side)),
            jnp.broadcast_to(keep_ref[:, 1:2], (hidden_width, side)),
        ],
        axis=1,
    )
    sigma = jax.nn.sigmoid(pre)
    hidden_ref[...] = (pre * sigma * keep).astype(BF)
    slope = sigma * (1.0 + pre * (1.0 - sigma)) * keep
    copies[2].wait()
    back = jnp.dot(wns_held[...], lower(two_ref), preferred_element_type=F32)
    copies[3].wait()
    d_pre_ref[...] = ((back + back_held[...]) * slope).astype(BF)
    copies[4].wait()
    for core in range(2):

        @pl.when(core_ref[0] == core)
        def _():
            write_half(1 - core, gt_held, one_ref, two_ref, hidden_ref[...], d_pre_ref[...], send_ref)


def keep_kernel(core_ref, mine_ref, one_ref, two_ref, hidden_ref, d_pre_ref, keep_ref, gt_held, hidden, d_pre, sems):
    copies = begin(
        [(d_pre_ref, d_pre), (hidden_ref, hidden), (mine_ref.at[:, FEATS:, :], gt_held)], sems
    )
    for copy in copies:
        copy.wait()
    for core in range(2):

        @pl.when(core_ref[0] == core)
        def _():
            write_half(core, gt_held, one_ref, two_ref, hidden[...], d_pre[...], keep_ref)


def sum_one_kernel(x_ref, keep_ref, other_ref, send_a, send_b, own_a, own_b):
    x = x_ref[0]
    zs = keep_ref.shape[1] // 2
    for lo, send, own, first, later in ((0, send_a, own_a, 1, 3), (zs, send_b, own_b, 3, 1)):
        for out, slots in ((send, (first, 2)), (own, (0, later))):
            for i, slot in enumerate(slots):
                at = jnp.bitwise_xor(x, slot)
                a = keep_ref[at, lo : lo + zs].astype(F32)
                out[i] = (a + other_ref[at, lo : lo + zs].astype(F32)).astype(BF)


def sum_two_kernel(own_a, own_b, got_a, got_b, send_a, send_b, out_ref):
    zs = own_a.shape[1]
    for own, got, send, lo in ((own_a, got_a, send_a, 0), (own_b, got_b, send_b, zs)):
        send[...] = (own[1].astype(F32) + got[1].astype(F32)).astype(BF)
        out_ref[lo : lo + zs] = (own[0].astype(F32) + got[0].astype(F32)).astype(BF)


def sum_three_kernel(own_ref, got_a, got_b, out_ref):
    zs = got_a.shape[0]
    for got, lo in ((got_a, 0), (got_b, zs)):
        out_ref[lo : lo + zs] = (own_ref[lo : lo + zs].astype(F32) + got[...].astype(F32)).astype(BF)


def place_kernel(core_ref, own_ref, other_ref, *outs):
    for core in range(2):

        @pl.when(core_ref[0] == core)
        def _():
            for half in range(2):
                src = own_ref if half == core else other_ref
                outs[half][...] = src[:FEATS]
                outs[2 + half][...] = src[FEATS:]


SMEM = pl.BlockSpec(memory_space=pltpu.SMEM)
VMEM = pl.BlockSpec(memory_space=pltpu.VMEM)
HBM = pl.BlockSpec(memory_space=pltpu.HBM)
DMA = pltpu.SemaphoreType.DMA


def call(kernel, name, ins, outs, scratch=(), flops=0, size=1 << 20):
    run = pl.pallas_call(
        kernel,
        in_specs=list(ins),
        out_specs=[VMEM] * len(outs),
        out_shape=[jax.ShapeDtypeStruct(*o) for o in outs],
        scratch_shapes=list(scratch),
        compiler_params=pltpu.CompilerParams(vmem_limit_bytes=24 << 20),
        cost_estimate=pl.CostEstimate(flops=flops, bytes_accessed=size, transcendentals=0),
        name=name,
    )

    def apply(*args):
        return run(
            *(
                pltpu.with_memory_space_constraint(a, pltpu.HBM) if spec is HBM else a
                for a, spec in zip(args, ins, strict=True)
            )
        )

    return apply


def local(
    node_features,
    edge_tiles,
    tile_source,
    tile_count,
    drop_bits,
    cotangent,
    self_first,
    neigh_first,
    self_second,
    neigh_second,
    owners,
    replicas,
):
    blocks, slots, side, _ = edge_tiles.shape
    feats, nodes = node_features.shape
    width = nodes // owners
    hidden_width = self_first.shape[1]
    cols = hidden_width // owners
    rows = feats + cols
    steps = blocks // STEP
    exchange = functools.partial(lax.all_to_all, axis_name="feat", split_axis=0, concat_axis=0, tiled=True)

    (mine,) = call(
        prep_kernel,
        "prep",
        [HBM] * 2,
        [((owners, rows, width), BF)],
        [pltpu.VMEM((feats, nodes), BF), pltpu.VMEM((width, hidden_width), BF), DMA((2,))],
    )(node_features, cotangent)
    one = exchange(mine)
    held = pltpu.VMEM((blocks, slots, side, side), BF)
    agg, scaling = call(
        agg_kernel,
        "agg",
        [SMEM, SMEM, HBM, HBM],
        [((owners, feats, width), BF), ((blocks, side), F32)],
        [pltpu.VMEM((feats, nodes), BF), held, DMA((1,)), DMA((steps,))],
        flops=2 * 48 * 512 * 8192,
        size=9 << 20,
    )(tile_source, tile_count, node_features, edge_tiles)
    (send,) = call(
        back_kernel,
        "back",
        [SMEM, SMEM, VMEM, VMEM, HBM, VMEM],
        [((owners, rows, width), BF)],
        [pltpu.VMEM((blocks, cols, side), F32), held, DMA((steps,))],
        flops=2 * 16 * 512 * 8192,
        size=9 << 20,
    )(tile_source, tile_count, one, scaling, edge_tiles, agg)
    two = exchange(send)

    shifts = jnp.arange(32, dtype=jnp.int32)
    bits = jnp.bitwise_and(jnp.right_shift(drop_bits[:, :, None], shifts), 1)
    keep = (bits.reshape(drop_bits.shape[0], hidden_width).astype(F32) * 2.0).T
    core = (lax.axis_index("dp") % 2).reshape(1)
    wide = (hidden_width, width)
    pre, back = call(
        early_kernel, "early", [VMEM, VMEM, VMEM, VMEM], [(wide, F32), (wide, F32)], flops=400 << 20, size=4 << 20
    )(mine, one, self_first.T, self_second)
    gt = pltpu.VMEM((owners, cols, width), BF)
    send, hidden, d_pre = call(
        send_kernel,
        "send",
        [SMEM, HBM, VMEM, VMEM, HBM, HBM, VMEM, HBM, HBM],
        [((owners, rows, hidden_width), BF), (wide, BF), (wide, BF)],
        [
            gt,
            pltpu.VMEM(wide, F32),
            pltpu.VMEM(wide, F32),
            pltpu.VMEM((hidden_width, self_first.shape[0]), BF),
            pltpu.VMEM((hidden_width, hidden_width), BF),
            DMA((5,)),
        ],
        flops=800 << 20,
        size=6 << 20,
    )(core, mine, one, two, pre, back, keep, neigh_first.T, neigh_second)
    swap = [(i, i ^ 1) for i in range(replicas)]
    other = lax.ppermute(send, "dp", swap)
    (kept,) = call(
        keep_kernel,
        "keep",
        [SMEM, HBM, VMEM, VMEM, HBM, HBM],
        [((owners, rows, hidden_width), BF)],
        [gt, pltpu.VMEM(wide, BF), pltpu.VMEM(wide, BF), DMA((3,))],
        flops=400 << 20,
        size=3 << 20,
    )(core, mine, one, two, hidden, d_pre)

    xs, zs = 4, owners // 4
    x = lax.axis_index("feat") // zs

    def along_x(value, flip):
        return lax.ppermute(value, "feat", [(i, i ^ (flip * zs)) for i in range(owners)])

    by_x = (xs, zs, rows, hidden_width)
    two_slots = ((2, zs // 2, rows, hidden_width), BF)
    send_a, send_b, own_a, own_b = call(
        sum_one_kernel, "sum_one", [SMEM, VMEM, VMEM], [two_slots] * 4, size=4 << 20
    )(x.reshape(1), kept.reshape(by_x), other.reshape(by_x))
    got_a, got_b = along_x(send_a, 1), along_x(send_b, 3)
    one_slot = ((zs // 2, rows, hidden_width), BF)
    all_z = ((zs, rows, hidden_width), BF)
    send_a, send_b, own = call(sum_two_kernel, "sum_two", [VMEM] * 4, [one_slot, one_slot, all_z])(
        own_a, own_b, got_a, got_b
    )
    got_a, got_b = along_x(send_a, 3), along_x(send_b, 1)
    (own,) = call(sum_three_kernel, "sum_three", [VMEM] * 3, [all_z])(own, got_a, got_b)
    shares = exchange(own, axis_index_groups=[[a * zs + b for b in range(zs)] for a in range(xs)])
    share = jnp.sum(shares.astype(F32), axis=0).astype(BF)
    ys = replicas // 2
    total = share.astype(F32)
    for k in (1, 3, 2):
        to = [(i, ((i // 2 + k) % ys) * 2 + i % 2) for i in range(replicas)]
        total = total + lax.ppermute(share, "dp", to).astype(F32)
    return tuple(
        call(
            place_kernel,
            "place",
            [SMEM, VMEM, VMEM],
            [((r, hidden_width), F32) for r in (feats, feats, cols, cols)],
        )(core, total, lax.ppermute(total, "dp", swap))
    )


def solution(mesh):
    return jax.shard_map(
        functools.partial(local, owners=mesh.shape["feat"], replicas=mesh.shape["dp"]),
        mesh=mesh,
        in_specs=(
            P("feat", "dp"),
            P("dp", None, None, None),
            P("dp", None),
            P("dp"),
            P(("dp", "feat"), None),
            P(("dp", "feat"), None),
            P(),
            P(),
            P(),
            P(),
        ),
        out_specs=(P("feat", None), P("feat", None), P("feat", None), P("feat", None)),
        check_vma=False,
    )
```

time: 1230 us -> 130 us (0.11)
  waiting for transfers between devices: 1080 us -> 46 us
  matrix products: 61.2 us -> 0 us
  local copies, waits for them, and re-layouts: 41.6 us -> 7.04 us
  Pallas kernels: 0 us -> 25.1 us
  starting transfers between devices: 22.4 us -> 36.7 us
  blocking collectives: 0 us -> 13.8 us
  between operations: 14.5 us -> 0.83 us
    reduce_scatter x3 -> x0, waiting for transfers between devices: 650 us -> none  [the longest x1 217 us: local(): lax.psum_scatter(grad_neigh_first, 'feat', scatter_dimension=0, tiled=True)]
    unnamed x9 -> x0, waiting for transfers between devices: 194 us -> none
    psum x2 -> x0, waiting for transfers between devices: 134 us -> none  [local(): summed = lax.psum((shares[0], shares[1], shares[2], shares[3]), 'dp')]
    all_gather x2 -> x0, waiting for transfers between devices: 86.1 us -> none  [the longest x1 83.7 us: local(): hidden_all = lax.all_gather(hidden_own, 'feat', axis=0, tiled=True)]
    dot_general x16 -> x0, matrix products: 61.2 us -> none  [the longest x1 31.4 us: local(): jnp.einsum('ptc,pts->psc', tile_lines_all, chosen, preferred_element_type...]
    pallas_call x0 -> x10, Pallas kernels: none -> 25.1 us  [apply(): run(*(pltpu.with_memory_space_constraint(a, pltpu.HBM) if spec is HBM els...]
    ppermute x0 -> x9, waiting for transfers between devices: none -> 22.8 us  [the longest x4 16.9 us: along_x(): lax.ppermute(value, 'feat', [(i, i ^ flip * zs) for i in range(owners)])]
    ppermute x0 -> x9, starting transfers between devices: none -> 16.4 us  [the longest x1 6.15 us: local(): lax.ppermute(total, 'dp', swap)]
  transfers between devices with their start and end apart: 10 -> 11, of which waited for: 10 -> 10; matrix products, arithmetic and copies ran while one was open for 8% -> 3% of each run, Pallas kernels for 0% -> 9%
where the time goes in v2:
time: 130 us
  waiting for transfers between devices  46 us (35%)
  starting transfers between devices  36.7 us (28%)
  Pallas kernels  25.1 us (19%)
  blocking collectives  13.8 us (11%)
  local copies, waits for them, and re-layouts  7.04 us (5%)
    pallas_call x10, Pallas kernels, apply(): run(*(pltpu.with_memory_space_constraint(a, pltpu.HBM) if spec is HBM els...  25.1 us
    ppermute x4, waiting for transfers between devices, along_x(): lax.ppermute(value, 'feat', [(i, i ^ flip * zs) for i in range(owners)])  16.9 us
    all_to_all x1, blocking collectives, local(): exchange(own, axis_index_groups=[[a * zs + b for b in range(zs)] for a in...  13.8 us
    all_to_all x1, waiting for transfers between devices, local(): two = exchange(send)  12.3 us
    all_to_all x1, starting transfers between devices, local(): one = exchange(mine)  11.9 us
    all_to_all x1, waiting for transfers between devices, local(): one = exchange(mine)  10.9 us
    all_to_all x1, starting transfers between devices, local(): two = exchange(send)  8.37 us
    unnamed x20, local copies, waits for them, and re-layouts  6.96 us
  transfers between devices with their start and end apart: 11, of which 10 were waited for; matrix products, arithmetic and copies ran while one was open for 3% of the time, Pallas kernels for 9%

profile of v2, /device:TPU:1, one launch (start us, length us, event | category | flops | bytes accessed | tf_op | source)
XLA Modules:
  0.0 129.7 jit_solution(11218455545727579000)
XLA Ops:
  0.7 2.1 %prep.1.mine_ref = bf16[32,48,256]{2,1,0:T(8,128)(2,1)} custom-call(bf16[32,8192]{1,0:T(8,128)(2,1)} %x_ref.3, bf16[256,512]{1,0:T(8,128)(2,1)} %g_ref.1), custom_call_target="tpu_custom_call" | custom-call | bytes 1048576 | tf_op jit(solution)/shard_map/prep/pallas_call | solution.py:249
  2.7 11.9 %all-to-all-start = ((bf16[32,48,256]{2,1,0:T(8,128)(2,1)}), bf16[32,48,256]{2,1,0:T(8,128)(2,1)S(1)}, u32[]{:S(2)}, u32[]{:S(2)}) async-start(bf16[32,48,256]{2,1,0:T(8,128)(2,1)} %prep.1.mine_ref), calls=%async_computation | async-start | bytes 1572864 | tf_op jit(solution)/shard_map/all_to_all | solution.py:289
  14.7 8.3 %agg.1 = (bf16[32,32,256]{2,1,0:T(8,128)(2,1)S(1)}, f32[64,128]{1,0:T(8,128)S(1)}) custom-call(s32[64,4]{1,0:T(8,128)S(1)} %copy.20.source_ref, s32[64]{0:T(128)S(1)} %copy-done.5, bf16[32,8192]{1,0:T(8,128)(2,1)} %x_ref.3, bf16[64,4,128,128]{3,2,1,0:T(8,128)(2,1)} %tiles_ref.3), custom_call_target="tpu_custom_call" | custom-call | flops 402653184 | bytes 9437184 | tf_op jit(solution)/shard_map/agg/pallas_call | solution.py:249
  23.0 10.9 %all-to-all-done.one_ref = bf16[32,48,256]{2,1,0:T(8,128)(2,1)S(1)} async-done(((bf16[32,48,256]{2,1,0:T(8,128)(2,1)}), bf16[32,48,256]{2,1,0:T(8,128)(2,1)S(1)}, u32[]{:S(2)}, u32[]{:S(2)}) %all-to-all-start) | async-done | bytes 786464 | tf_op jit(solution)/shard_map/all_to_all | solution.py:289
  33.9 5.7 %back.1 = bf16[32,48,256]{2,1,0:T(8,128)(2,1)} custom-call(s32[64,4]{1,0:T(8,128)S(1)} %copy.20.source_ref, s32[64]{0:T(128)S(1)} %copy-done.5, bf16[32,48,256]{2,1,0:T(8,128)(2,1)S(1)} %all-to-all-done.one_ref, f32[64,128]{1,0:T(8,128)S(1)} %get-tuple-element.18.scale_ref, bf16[64,4,128,128]{3,2,1,0:T(8,128)(2,1)} %tiles_ref.3, ...), custom_call_target="tpu_custom_call" | custom-call | flops 134217728 | bytes 9437184 | tf_op jit(solution)/shard_map/back/pallas_call | solution.py:249
  39.6 8.4 %all-to-all-start.1 = ((bf16[32,48,256]{2,1,0:T(8,128)(2,1)}), bf16[32,48,256]{2,1,0:T(8,128)(2,1)S(1)}, u32[]{:S(2)}, u32[]{:S(2)}) async-start(bf16[32,48,256]{2,1,0:T(8,128)(2,1)} %back.1), calls=%async_computation.1 | async-start | bytes 1572864 | tf_op jit(solution)/shard_map/all_to_all | solution.py:309
  48.2 1.5 %copy.21 = bf16[1024,512]{0,1:T(8,128)(2,1)S(1)} copy(bf16[1024,512]{1,0:T(8,128)(2,1)} %param.16) | data formatting | bytes 2097152 | tf_op args[6]
  49.7 2.3 %copy.24 = bf16[1024,512]{0,1:T(8,128)(2,1)} copy(bf16[1024,512]{1,0:T(8,128)(2,1)} %param.17) | data formatting | bytes 2097152 | tf_op args[7]
  52.2 1.7 %early.1 = (f32[512,256]{1,0:T(8,128)S(1)}, f32[512,256]{1,0:T(8,128)S(1)}) custom-call(bf16[32,48,256]{2,1,0:T(8,128)(2,1)} %prep.1.mine_ref, bf16[32,48,256]{2,1,0:T(8,128)(2,1)S(1)} %all-to-all-done.one_ref, bf16[512,1024]{1,0:T(8,128)(2,1)S(1)} %bitcast.16, bf16[512,512]{1,0:T(8,128)(2,1)S(1)} %copy-done), custom_call_target="tpu_custom_call" | custom-call | flops 419430400 | bytes 4194304 | tf_op jit(solution)/shard_map/early/pallas_call | solution.py:249
  53.9 0.8 copy-done.1
  54.7 0.8 copy-done.2
  55.5 12.3 %all-to-all-done.1.two_ref = bf16[32,48,256]{2,1,0:T(8,128)(2,1)S(1)} async-done(((bf16[32,48,256]{2,1,0:T(8,128)(2,1)}), bf16[32,48,256]{2,1,0:T(8,128)(2,1)S(1)}, u32[]{:S(2)}, u32[]{:S(2)}) %all-to-all-start.1) | async-done | bytes 786464 | tf_op jit(solution)/shard_map/all_to_all | solution.py:309
  67.8 4.3 %send.1 = (bf16[32,48,512]{2,1,0:T(8,128)(2,1)}, bf16[512,256]{1,0:T(8,128)(2,1)S(1)}, bf16[512,256]{1,0:T(8,128)(2,1)S(1)}) custom-call(s32[1]{0:T(128)} %bitcast.core_ref, bf16[32,48,256]{2,1,0:T(8,128)(2,1)} %prep.1.mine_ref, bf16[32,48,256]{2,1,0:T(8,128)(2,1)S(1)} %all-to-all-done.one_ref, bf16[32,48,256]{2,1,0:T(8,128)(2,1)S(1)} %all-to-all-done.1.two_ref, ...), custom_call_target="tpu_custom_call" | custom-call | flops 838860800 | bytes 6291456 | tf_op jit(solution)/shard_map/send/pallas_call | solution.py:249
  72.1 0.7 copy-done.3
  72.8 0.7 copy-done.4
  73.5 4.5 %collective-permute-start = (bf16[32,48,512]{2,1,0:T(8,128)(2,1)}, bf16[32,48,512]{2,1,0:T(8,128)(2,1)S(1)}, u32[]{:S(2)}, u32[]{:S(2)}) collective-permute-start(bf16[32,48,512]{2,1,0:T(8,128)(2,1)} %get-tuple-element.24), channel_id=1, source_target_pairs={{0,32},{32,0},{64,96},{96,64},{128,160},{160,128},{192,224},{224,1... | collective-permute-start | bytes 4718600 | tf_op jit(solution)/shard_map/ppermute | solution.py:337
  78.0 1.7 %keep.1 = bf16[32,48,512]{2,1,0:T(8,128)(2,1)S(1)} custom-call(s32[1]{0:T(128)} %bitcast.core_ref, bf16[32,48,256]{2,1,0:T(8,128)(2,1)} %prep.1.mine_ref, bf16[32,48,256]{2,1,0:T(8,128)(2,1)S(1)} %all-to-all-done.one_ref, bf16[32,48,256]{2,1,0:T(8,128)(2,1)S(1)} %all-to-all-done.1.two_ref, bf16[512,256]{1,0:T(8,128)(2,1)} %copy-done.3, ...), custom_call_target="tpu_custom_call" | custom-call | flops 419430400 | bytes 3145728 | tf_op jit(solution)/shard_map/keep/pallas_call | solution.py:249
  79.7 1.5 %collective-permute-done = bf16[32,48,512]{2,1,0:T(8,128)(2,1)S(1)} collective-permute-done((bf16[32,48,512]{2,1,0:T(8,128)(2,1)}, bf16[32,48,512]{2,1,0:T(8,128)(2,1)S(1)}, u32[]{:S(2)}, u32[]{:S(2)}) %collective-permute-start) | collective-permute-done | bytes 1572896 | tf_op jit(solution)/shard_map/ppermute | solution.py:337
  81.7 0.8 collective-permute-start.2
  82.5 9.5 %collective-permute-done.1.got_a = bf16[2,4,48,512]{3,2,1,0:T(8,128)(2,1)S(1)} collective-permute-done((bf16[2,4,48,512]{3,2,1,0:T(8,128)(2,1)S(1)}, bf16[2,4,48,512]{3,2,1,0:T(8,128)(2,1)S(1)}, u32[]{:S(2)}, u32[]{:S(2)}) %collective-permute-start.1) | collective-permute-done | bytes 393248 | tf_op jit(solution)/shard_map/ppermute | solution.py:352
  92.0 1.3 %collective-permute-done.2.got_b = bf16[2,4,48,512]{3,2,1,0:T(8,128)(2,1)S(1)} collective-permute-done((bf16[2,4,48,512]{3,2,1,0:T(8,128)(2,1)S(1)}, bf16[2,4,48,512]{3,2,1,0:T(8,128)(2,1)S(1)}, u32[]{:S(2)}, u32[]{:S(2)}) %collective-permute-start.2) | collective-permute-done | bytes 393248 | tf_op jit(solution)/shard_map/ppermute | solution.py:352
  93.5 0.4 collective-permute-start.3
  94.0 6.0 %collective-permute-done.3.got_a = bf16[4,48,512]{2,1,0:T(8,128)(2,1)S(1)} collective-permute-done((bf16[4,48,512]{2,1,0:T(8,128)(2,1)S(1)}, bf16[4,48,512]{2,1,0:T(8,128)(2,1)S(1)}, u32[]{:S(2)}, u32[]{:S(2)}) %collective-permute-start.3) | collective-permute-done | bytes 196640 | tf_op jit(solution)/shard_map/ppermute | solution.py:352
  100.1 13.8 %all_to_all.15 = bf16[8,48,512]{2,1,0:T(8,128)(2,1)S(1)} all-to-all(bf16[8,48,512]{2,1,0:T(8,128)(2,1)S(1)} %sum_three.1), channel_id=1, replica_groups={{0,1,2,3,4,5,6,7},{8,9,10,11,12,13,14,15},{16,17,18,19,20,21,22,23},{24..., dimensions={0} | all-to-all | bytes 786432 | tf_op jit(solution)/shard_map/all_to_all | solution.py:367
  114.0 3.0 %collective-permute-start.7 = (bf16[48,512]{1,0:T(8,128)(2,1)S(1)}, bf16[48,512]{1,0:T(8,128)(2,1)S(1)}, u32[]{:S(2)}, u32[]{:S(2)}) collective-permute-start(bf16[48,512]{1,0:T(8,128)(2,1)S(1)} %reduce_sum.12), channel_id=1, source_target_pairs={{0,128},{32,160},{64,192},{96,224},{128,0},{160,32},{192,64},{224,... | collective-permute-start | bytes 147464 | tf_op jit(solution)/shard_map/ppermute | solution.py:373
  117.0 0.8 collective-permute-start.6
  117.8 0.7 collective-permute-start.5
  118.5 1.4 %collective-permute-done.6 = bf16[48,512]{1,0:T(8,128)(2,1)S(1)} collective-permute-done((bf16[48,512]{1,0:T(8,128)(2,1)S(1)}, bf16[48,512]{1,0:T(8,128)(2,1)S(1)}, u32[]{:S(2)}, u32[]{:S(2)}) %collective-permute-start.6) | collective-permute-done | bytes 49184 | tf_op jit(solution)/shard_map/ppermute | solution.py:373
  119.9 2.0 %collective-permute-done.5 = bf16[48,512]{1,0:T(8,128)(2,1)S(1)} collective-permute-done((bf16[48,512]{1,0:T(8,128)(2,1)S(1)}, bf16[48,512]{1,0:T(8,128)(2,1)S(1)}, u32[]{:S(2)}, u32[]{:S(2)}) %collective-permute-start.5) | collective-permute-done | bytes 49184 | tf_op jit(solution)/shard_map/ppermute | solution.py:373
  122.0 6.1 %collective-permute-start.8 = (f32[48,512]{1,0:T(8,128)S(1)}, f32[48,512]{1,0:T(8,128)S(1)}, u32[]{:S(2)}, u32[]{:S(2)}) collective-permute-start(f32[48,512]{1,0:T(8,128)S(1)} %convert_add_fusion.own_ref), channel_id=1, source_target_pairs={{0,32},{32,0},{64,96},{96,64},{128,160},{160,128},{192,224},{224,1... | collective-permute-start | bytes 294920 | tf_op jit(solution)/shard_map/ppermute | solution.py:380
  128.1 0.9 collective-permute-done.8.other_ref
  129.0 0.7 place.1
  (26 shorter events, 1.3 us)
Async XLA Ops:
  0.6 14.0 %copy-start.6 = (s32[64,4]{0,1:T(4,128)S(1)}, s32[64,4]{0,1:T(4,128)}, u32[]{:S(2)}) copy-start(s32[64,4]{0,1:T(4,128)} %param.12) | copy-start | bytes 3076
  0.6 14.1 %copy-start.5 = (s32[64]{0:T(128)S(1)}, s32[64]{0:T(128)}, u32[]{:S(2)}) copy-start(s32[64]{0:T(128)} %count_ref.3) | copy-start | bytes 772
  2.7 31.1 %all-to-all-start = ((bf16[32,48,256]{2,1,0:T(8,128)(2,1)}), bf16[32,48,256]{2,1,0:T(8,128)(2,1)S(1)}, u32[]{:S(2)}, u32[]{:S(2)}) async-start(bf16[32,48,256]{2,1,0:T(8,128)(2,1)} %prep.1.mine_ref), calls=%async_computation | async-start | bytes 1572864 | tf_op jit(solution)/shard_map/all_to_all | solution.py:289
  39.6 8.4 %copy-start.7 = (s32[2,16]{1,0:T(2,128)S(1)}, s32[2,16]{1,0:T(2,128)}, u32[]{:S(2)}) copy-start(s32[2,16]{1,0:T(2,128)} %param.14) | copy-start | bytes 388
  39.6 28.2 %all-to-all-start.1 = ((bf16[32,48,256]{2,1,0:T(8,128)(2,1)}), bf16[32,48,256]{2,1,0:T(8,128)(2,1)S(1)}, u32[]{:S(2)}, u32[]{:S(2)}) async-start(bf16[32,48,256]{2,1,0:T(8,128)(2,1)} %back.1), calls=%async_computation.1 | async-start | bytes 1572864 | tf_op jit(solution)/shard_map/all_to_all | solution.py:309
  49.7 2.5 %copy-start = (bf16[512,512]{1,0:T(8,128)(2,1)S(1)}, bf16[512,512]{1,0:T(8,128)(2,1)}, u32[]{:S(2)}) copy-start(bf16[512,512]{1,0:T(8,128)(2,1)} %wss_ref.1) | copy-start | bytes 1572868
  53.9 0.8 copy-start.1
  54.7 0.8 copy-start.2
  72.1 0.7 copy-start.3
  72.8 0.7 copy-start.4
  73.5 7.8 %collective-permute-start = (bf16[32,48,512]{2,1,0:T(8,128)(2,1)}, bf16[32,48,512]{2,1,0:T(8,128)(2,1)S(1)}, u32[]{:S(2)}, u32[]{:S(2)}) collective-permute-start(bf16[32,48,512]{2,1,0:T(8,128)(2,1)} %get-tuple-element.24), channel_id=1, source_target_pairs={{0,32},{32,0},{64,96},{96,64},{128,160},{160,128},{192,224},{224,1... | collective-permute-start | bytes 4718600 | tf_op jit(solution)/shard_map/ppermute | solution.py:337
  81.6 10.4 %collective-permute-start.1 = (bf16[2,4,48,512]{3,2,1,0:T(8,128)(2,1)S(1)}, bf16[2,4,48,512]{3,2,1,0:T(8,128)(2,1)S(1)}, u32[]{:S(2)}, u32[]{:S(2)}) collective-permute-start(bf16[2,4,48,512]{3,2,1,0:T(8,128)(2,1)S(1)} %get-tuple-element.27), channel_id=1, source_target_pairs={{0,8},{1,9},{2,10},{3,11},{4,12},{5,13},{6,14},{7,15},{8,0},{9,1},... | collective-permute-start | bytes 1179656 | tf_op jit(solution)/shard_map/ppermute | solution.py:352
  81.7 11.6 %collective-permute-start.2 = (bf16[2,4,48,512]{3,2,1,0:T(8,128)(2,1)S(1)}, bf16[2,4,48,512]{3,2,1,0:T(8,128)(2,1)S(1)}, u32[]{:S(2)}, u32[]{:S(2)}) collective-permute-start(bf16[2,4,48,512]{3,2,1,0:T(8,128)(2,1)S(1)} %get-tuple-element.28), channel_id=1, source_target_pairs={{0,24},{1,25},{2,26},{3,27},{4,28},{5,29},{6,30},{7,31},{8,16},{9,... | collective-permute-start | bytes 1179656 | tf_op jit(solution)/shard_map/ppermute | solution.py:352
  93.5 6.5 %collective-permute-start.3 = (bf16[4,48,512]{2,1,0:T(8,128)(2,1)S(1)}, bf16[4,48,512]{2,1,0:T(8,128)(2,1)S(1)}, u32[]{:S(2)}, u32[]{:S(2)}) collective-permute-start(bf16[4,48,512]{2,1,0:T(8,128)(2,1)S(1)} %get-tuple-element.30), channel_id=1, source_target_pairs={{0,24},{1,25},{2,26},{3,27},{4,28},{5,29},{6,30},{7,31},{8,16},{9,... | collective-permute-start | bytes 589832 | tf_op jit(solution)/shard_map/ppermute | solution.py:352
  94.0 6.0 %collective-permute-start.4 = (bf16[4,48,512]{2,1,0:T(8,128)(2,1)S(1)}, bf16[4,48,512]{2,1,0:T(8,128)(2,1)S(1)}, u32[]{:S(2)}, u32[]{:S(2)}) collective-permute-start(bf16[4,48,512]{2,1,0:T(8,128)(2,1)S(1)} %get-tuple-element.31), channel_id=1, source_target_pairs={{0,8},{1,9},{2,10},{3,11},{4,12},{5,13},{6,14},{7,15},{8,0},{9,1},... | collective-permute-start | bytes 589832 | tf_op jit(solution)/shard_map/ppermute | solution.py:352
  114.0 4.5 %collective-permute-start.7 = (bf16[48,512]{1,0:T(8,128)(2,1)S(1)}, bf16[48,512]{1,0:T(8,128)(2,1)S(1)}, u32[]{:S(2)}, u32[]{:S(2)}) collective-permute-start(bf16[48,512]{1,0:T(8,128)(2,1)S(1)} %reduce_sum.12), channel_id=1, source_target_pairs={{0,128},{32,160},{64,192},{96,224},{128,0},{160,32},{192,64},{224,... | collective-permute-start | bytes 147464 | tf_op jit(solution)/shard_map/ppermute | solution.py:373
  117.0 2.9 %collective-permute-start.6 = (bf16[48,512]{1,0:T(8,128)(2,1)S(1)}, bf16[48,512]{1,0:T(8,128)(2,1)S(1)}, u32[]{:S(2)}, u32[]{:S(2)}) collective-permute-start(bf16[48,512]{1,0:T(8,128)(2,1)S(1)} %reduce_sum.12), channel_id=1, source_target_pairs={{0,192},{32,224},{64,0},{96,32},{128,64},{160,96},{192,128},{224,1... | collective-permute-start | bytes 147464 | tf_op jit(solution)/shard_map/ppermute | solution.py:373
  117.8 4.2 %collective-permute-start.5 = (bf16[48,512]{1,0:T(8,128)(2,1)S(1)}, bf16[48,512]{1,0:T(8,128)(2,1)S(1)}, u32[]{:S(2)}, u32[]{:S(2)}) collective-permute-start(bf16[48,512]{1,0:T(8,128)(2,1)S(1)} %reduce_sum.12), channel_id=1, source_target_pairs={{0,64},{32,96},{64,128},{96,160},{128,192},{160,224},{192,0},{224,... | collective-permute-start | bytes 147464 | tf_op jit(solution)/shard_map/ppermute | solution.py:373
  122.0 7.1 %collective-permute-start.8 = (f32[48,512]{1,0:T(8,128)S(1)}, f32[48,512]{1,0:T(8,128)S(1)}, u32[]{:S(2)}, u32[]{:S(2)}) collective-permute-start(f32[48,512]{1,0:T(8,128)S(1)} %convert_add_fusion.own_ref), channel_id=1, source_target_pairs={{0,32},{32,0},{64,96},{96,64},{128,160},{160,128},{192,224},{224,1... | collective-permute-start | bytes 294920 | tf_op jit(solution)/shard_map/ppermute | solution.py:380

commit v3 on v2

--- a/solution.py
+++ b/solution.py
@@ -63,17 +63,16 @@
             rhs = jnp.concatenate([held_ref[b, t] for t in range(slots)], axis=1)
             out = lax.dot_general(lhs, rhs, LAST, preferred_element_type=F32)
             scale = lax.rsqrt(out[FEATS : FEATS + 1])
-            agg_ref[b // 2, :, (j % 2) * side : (j % 2 + 1) * side] = (out[:FEATS] * scale).astype(BF)
+            agg_ref[b // 2, :FEATS, (j % 2) * side : (j % 2 + 1) * side] = (out[:FEATS] * scale).astype(BF)
             scale_ref[pl.ds(b, 1)] = scale
 
 
-def back_kernel(source_ref, count_ref, one_ref, scale_ref, tiles_ref, agg_ref, out_ref, acc_ref, held_ref, sems):
+def back_kernel(source_ref, count_ref, one_ref, scale_ref, tiles_ref, agg_ref, out_ref, acc_ref, q_ref, held_ref, sems, out_sem):
     blocks, slots, side, _ = held_ref.shape
     steps = blocks // STEP
     for i in range(steps):
         chunk(tiles_ref, held_ref, sems, i).start()
     acc_ref[...] = jnp.zeros_like(acc_ref)
-    out_ref[:, :FEATS, :] = agg_ref[...]
 
     @pl.loop(0, steps)
     def _(i):
@@ -89,9 +88,10 @@
                 src = source_ref[b, t]
                 acc_ref[src] = acc_ref[src] + out[:, t * side : (t + 1) * side] * alive(count, t)
 
-    for o in range(out_ref.shape[0]):
-        out_ref[o, FEATS:, :side] = acc_ref[2 * o].astype(BF)
-        out_ref[o, FEATS:, side:] = acc_ref[2 * o + 1].astype(BF)
+    for o in range(q_ref.shape[0]):
+        q_ref[o, :, :side] = acc_ref[2 * o].astype(BF)
+        q_ref[o, :, side:] = acc_ref[2 * o + 1].astype(BF)
+    begin([(q_ref, out_ref.at[:, FEATS:, :])], out_sem)[0].wait()
 
 
 def upper(ref):
@@ -110,15 +110,17 @@
 
 
 def write_half(half, gt_ref, one_ref, two_ref, hidden, d_pre, out_ref):
-    owners, rows, width = out_ref.shape
+    ys, owners, rows, lanes = out_ref.shape
     if half:
         left, right = upper(two_ref), lower(two_ref)
     else:
         left, right = upper(one_ref), gt_ref[...].reshape(hidden.shape)
     first = lax.dot_general(left, d_pre, LAST, preferred_element_type=F32).astype(BF)
-    out_ref[:, :FEATS, :] = first.reshape(owners, FEATS, width)
     second = lax.dot_general(hidden, right, LAST, preferred_element_type=F32).astype(BF)
-    out_ref[:, FEATS:, :] = second.reshape(owners, rows - FEATS, width)
+    for y in range(ys):
+        cut = slice(y * lanes, (y + 1) * lanes)
+        out_ref[y, :, :FEATS, :] = first[:, cut].reshape(owners, FEATS, lanes)
+        out_ref[y, :, FEATS:, :] = second[:, cut].reshape(owners, rows - FEATS, lanes)
 
 
 def send_kernel(
@@ -132,14 +134,17 @@
     wnf_ref,
     wns_ref,
     send_ref,
-    hidden_ref,
-    d_pre_ref,
+    hidden_out,
+    d_pre_out,
     gt_held,
     pre_held,
     back_held,
     wnf_held,
     wns_held,
+    hidden_ref,
+    d_pre_ref,
     sems,
+    out_sems,
 ):
     copies = begin(
         [
@@ -172,12 +177,16 @@
     copies[3].wait()
     d_pre_ref[...] = ((back + back_held[...]) * slope).astype(BF)
     copies[4].wait()
+    leaving = begin([(hidden_ref, hidden_out), (d_pre_ref, d_pre_out)], out_sems)
     for core in range(2):
 
         @pl.when(core_ref[0] == core)
         def _():
             write_half(1 - core, gt_held, one_ref, two_ref, hidden_ref[...], d_pre_ref[...], send_ref)
 
+    for copy in leaving:
+        copy.wait()
+
 
 def keep_kernel(core_ref, mine_ref, one_ref, two_ref, hidden_ref, d_pre_ref, keep_ref, gt_held, hidden, d_pre, sems):
     copies = begin(
@@ -192,39 +201,30 @@
             write_half(core, gt_held, one_ref, two_ref, hidden[...], d_pre[...], keep_ref)
 
 
-def sum_one_kernel(x_ref, keep_ref, other_ref, send_a, send_b, own_a, own_b):
-    x = x_ref[0]
-    zs = keep_ref.shape[1] // 2
-    for lo, send, own, first, later in ((0, send_a, own_a, 1, 3), (zs, send_b, own_b, 3, 1)):
-        for out, slots in ((send, (first, 2)), (own, (0, later))):
-            for i, slot in enumerate(slots):
-                at = jnp.bitwise_xor(x, slot)
-                a = keep_ref[at, lo : lo + zs].astype(F32)
-                out[i] = (a + other_ref[at, lo : lo + zs].astype(F32)).astype(BF)
-
-
-def sum_two_kernel(own_a, own_b, got_a, got_b, send_a, send_b, out_ref):
-    zs = own_a.shape[1]
-    for own, got, send, lo in ((own_a, got_a, send_a, 0), (own_b, got_b, send_b, zs)):
-        send[...] = (own[1].astype(F32) + got[1].astype(F32)).astype(BF)
-        out_ref[lo : lo + zs] = (own[0].astype(F32) + got[0].astype(F32)).astype(BF)
-
-
-def sum_three_kernel(own_ref, got_a, got_b, out_ref):
-    zs = got_a.shape[0]
-    for got, lo in ((got_a, 0), (got_b, zs)):
-        out_ref[lo : lo + zs] = (own_ref[lo : lo + zs].astype(F32) + got[...].astype(F32)).astype(BF)
-
-
-def place_kernel(core_ref, own_ref, other_ref, *outs):
+def pair_kernel(keep_ref, other_ref, out_ref):
+    out_ref[...] = (keep_ref[...].astype(F32) + other_ref[...].astype(F32)).astype(BF)
+
+
+def gather_kernel(got_ref, out_ref):
+    total = got_ref[0].astype(F32)
+    for i in range(1, got_ref.shape[0]):
+        total = total + got_ref[i].astype(F32)
+    out_ref[...] = total.astype(BF)
+
+
+def place_kernel(where_ref, *refs):
+    ins, outs = refs[:4], refs[4:]
+    ys = len(ins)
     for core in range(2):
 
-        @pl.when(core_ref[0] == core)
+        @pl.when(where_ref[0] == core)
         def _():
-            for half in range(2):
-                src = own_ref if half == core else other_ref
-                outs[half][...] = src[:FEATS]
-                outs[2 + half][...] = src[FEATS:]
+            for k in range(ys):
+                start = pl.multiple_of(lax.rem(where_ref[1] + ys - k, ys) * 128, 128)
+                for r in range(2):
+                    half = core ^ r
+                    outs[half][:, pl.ds(start, 128)] = ins[k][r, :FEATS]
+                    outs[2 + half][:, pl.ds(start, 128)] = ins[k][r, FEATS:]
 
 
 SMEM = pl.BlockSpec(memory_space=pltpu.SMEM)
@@ -233,13 +233,14 @@
 DMA = pltpu.SemaphoreType.DMA
 
 
-def call(kernel, name, ins, outs, scratch=(), flops=0, size=1 << 20):
+def call(kernel, name, ins, outs, scratch=(), flops=0, size=1 << 20, aliases=None):
     run = pl.pallas_call(
         kernel,
         in_specs=list(ins),
-        out_specs=[VMEM] * len(outs),
-        out_shape=[jax.ShapeDtypeStruct(*o) for o in outs],
+        out_specs=[HBM if len(o) > 2 else VMEM for o in outs],
+        out_shape=[(pltpu.HBM if len(o) > 2 else jax.ShapeDtypeStruct)(*o[:2]) for o in outs],
         scratch_shapes=list(scratch),
+        input_output_aliases=aliases or {},
         compiler_params=pltpu.CompilerParams(vmem_limit_bytes=24 << 20),
         cost_estimate=pl.CostEstimate(flops=flops, bytes_accessed=size, transcendentals=0),
         name=name,
@@ -292,7 +293,7 @@
         agg_kernel,
         "agg",
         [SMEM, SMEM, HBM, HBM],
-        [((owners, feats, width), BF), ((blocks, side), F32)],
+        [((owners, rows, width), BF), ((blocks, side), F32)],
         [pltpu.VMEM((feats, nodes), BF), held, DMA((1,)), DMA((steps,))],
         flops=2 * 48 * 512 * 8192,
         size=9 << 20,
@@ -300,11 +301,12 @@
     (send,) = call(
         back_kernel,
         "back",
-        [SMEM, SMEM, VMEM, VMEM, HBM, VMEM],
-        [((owners, rows, width), BF)],
-        [pltpu.VMEM((blocks, cols, side), F32), held, DMA((steps,))],
+        [SMEM, SMEM, VMEM, VMEM, HBM, HBM],
+        [((owners, rows, width), BF, HBM)],
+        [pltpu.VMEM((blocks, cols, side), F32), pltpu.VMEM((owners, cols, width), BF), held, DMA((steps,)), DMA((1,))],
         flops=2 * 16 * 512 * 8192,
         size=9 << 20,
+        aliases={5: 0},
     )(tile_source, tile_count, one, scaling, edge_tiles, agg)
     two = exchange(send)
 
@@ -317,18 +319,24 @@
         early_kernel, "early", [VMEM, VMEM, VMEM, VMEM], [(wide, F32), (wide, F32)], flops=400 << 20, size=4 << 20
     )(mine, one, self_first.T, self_second)
     gt = pltpu.VMEM((owners, cols, width), BF)
+    ys, xs = replicas // 2, 4
+    zs = owners // xs
+    half = ((ys, owners, rows, 128), BF)
     send, hidden, d_pre = call(
         send_kernel,
         "send",
         [SMEM, HBM, VMEM, VMEM, HBM, HBM, VMEM, HBM, HBM],
-        [((owners, rows, hidden_width), BF), (wide, BF), (wide, BF)],
+        [half, (wide, BF, HBM), (wide, BF, HBM)],
         [
             gt,
             pltpu.VMEM(wide, F32),
             pltpu.VMEM(wide, F32),
             pltpu.VMEM((hidden_width, self_first.shape[0]), BF),
             pltpu.VMEM((hidden_width, hidden_width), BF),
+            pltpu.VMEM(wide, BF),
+            pltpu.VMEM(wide, BF),
             DMA((5,)),
+            DMA((2,)),
         ],
         flops=800 << 20,
         size=6 << 20,
@@ -339,45 +347,34 @@
         keep_kernel,
         "keep",
         [SMEM, HBM, VMEM, VMEM, HBM, HBM],
-        [((owners, rows, hidden_width), BF)],
+        [half],
         [gt, pltpu.VMEM(wide, BF), pltpu.VMEM(wide, BF), DMA((3,))],
         flops=400 << 20,
         size=3 << 20,
     )(core, mine, one, two, hidden, d_pre)
 
-    xs, zs = 4, owners // 4
-    x = lax.axis_index("feat") // zs
-
-    def along_x(value, flip):
-        return lax.ppermute(value, "feat", [(i, i ^ (flip * zs)) for i in range(owners)])
-
-    by_x = (xs, zs, rows, hidden_width)
-    two_slots = ((2, zs // 2, rows, hidden_width), BF)
-    send_a, send_b, own_a, own_b = call(
-        sum_one_kernel, "sum_one", [SMEM, VMEM, VMEM], [two_slots] * 4, size=4 << 20
-    )(x.reshape(1), kept.reshape(by_x), other.reshape(by_x))
-    got_a, got_b = along_x(send_a, 1), along_x(send_b, 3)
-    one_slot = ((zs // 2, rows, hidden_width), BF)
-    all_z = ((zs, rows, hidden_width), BF)
-    send_a, send_b, own = call(sum_two_kernel, "sum_two", [VMEM] * 4, [one_slot, one_slot, all_z])(
-        own_a, own_b, got_a, got_b
-    )
-    got_a, got_b = along_x(send_a, 3), along_x(send_b, 1)
-    (own,) = call(sum_three_kernel, "sum_three", [VMEM] * 3, [all_z])(own, got_a, got_b)
+    (pair,) = call(pair_kernel, "pair", [VMEM] * 2, [half], size=5 << 20)(kept, other)
+    planes = [
+        [(2 * y + c) * owners + x * zs + z for y in range(ys) for x in range(xs)] for c in range(2) for z in range(zs)
+    ]
+    got = lax.all_to_all(
+        pair.reshape(ys * xs, zs, rows, 128), ("dp", "feat"), 0, 0, tiled=True, axis_index_groups=planes
+    )
+    (own,) = call(gather_kernel, "gather", [VMEM], [((zs, rows, 128), BF)], size=2 << 20)(got)
     shares = exchange(own, axis_index_groups=[[a * zs + b for b in range(zs)] for a in range(xs)])
-    share = jnp.sum(shares.astype(F32), axis=0).astype(BF)
-    ys = replicas // 2
-    total = share.astype(F32)
+    share = jnp.sum(shares.astype(F32), axis=0)
+    both = jnp.stack([share, lax.ppermute(share, "dp", swap)])
+    moved = {0: both}
     for k in (1, 3, 2):
-        to = [(i, ((i // 2 + k) % ys) * 2 + i % 2) for i in range(replicas)]
-        total = total + lax.ppermute(share, "dp", to).astype(F32)
+        moved[k] = lax.ppermute(both, "dp", [(i, ((i // 2 + k) % ys) * 2 + i % 2) for i in range(replicas)])
+    where = jnp.concatenate([core, (lax.axis_index("dp") // 2).reshape(1)])
     return tuple(
         call(
             place_kernel,
             "place",
-            [SMEM, VMEM, VMEM],
+            [SMEM] + [VMEM] * ys,
             [((r, hidden_width), F32) for r in (feats, feats, cols, cols)],
-        )(core, total, lax.ppermute(total, "dp", swap))
+        )(where, *(moved[k] for k in range(ys)))
     )
 
 

time: 130 us -> 128 us (0.985)
  blocking collectives: 13.8 us -> 37.6 us
  waiting for transfers between devices: 46 us -> 28.4 us
  starting transfers between devices: 36.7 us -> 29.5 us
    all_to_all x0 -> x1, blocking collectives: none -> 26.3 us  [local(): lax.all_to_all(pair.reshape(ys * xs, zs, rows, 128), ('dp', 'feat'), 0, 0...]
    ppermute x8 -> x4, waiting for transfers between devices: 21.3 us -> 4.85 us  [the longest x3 4 us: local(): lax.ppermute(both, 'dp', [(i, (i // 2 + k) % ys * 2 + i % 2) for i in ran...]
    ppermute x8 -> x4, starting transfers between devices: 11.9 us -> 4.65 us  [the longest x1 3.18 us: local(): both = jnp.stack([share, lax.ppermute(share, 'dp', swap)])]
    all_to_all x1, blocking collectives: 13.8 us -> 11.3 us  [local(): exchange(own, axis_index_groups=[[a * zs + b for b in range(zs)] for a in...]
    pallas_call x10 -> x9, Pallas kernels: 25.1 us -> 24.5 us  [apply(): run(*(pltpu.with_memory_space_constraint(a, pltpu.HBM) if spec is HBM els...]
    unnamed x20 -> x18, local copies, waits for them, and re-layouts: 6.96 us -> 6.53 us
  transfers between devices with their start and end apart: 11 -> 7, of which waited for: 10 -> 7; matrix products, arithmetic and copies ran while one was open for 3% -> 3% of each run, Pallas kernels for 9% -> 9%
where the time goes in v3:
time: 128 us
  blocking collectives  37.6 us (29%)
  starting transfers between devices  29.5 us (23%)
  waiting for transfers between devices  28.4 us (22%)
  Pallas kernels  24.5 us (19%)
  local copies, waits for them, and re-layouts  6.62 us (5%)
    all_to_all x1, blocking collectives, local(): lax.all_to_all(pair.reshape(ys * xs, zs, rows, 128), ('dp', 'feat'), 0, 0...  26.3 us
    pallas_call x9, Pallas kernels, apply(): run(*(pltpu.with_memory_space_constraint(a, pltpu.HBM) if spec is HBM els...  24.5 us
    all_to_all x1, waiting for transfers between devices, local(): two = exchange(send)  12.3 us
    all_to_all x1, starting transfers between devices, local(): one = exchange(mine)  11.9 us
    all_to_all x1, blocking collectives, local(): exchange(own, axis_index_groups=[[a * zs + b for b in range(zs)] for a in...  11.3 us
    all_to_all x1, waiting for transfers between devices, local(): one = exchange(mine)  9.94 us
    all_to_all x1, starting transfers between devices, local(): two = exchange(send)  8.37 us
    unnamed x18, local copies, waits for them, and re-layouts  6.53 us
  transfers between devices with their start and end apart: 7, of which 7 were waited for; matrix products, arithmetic and copies ran while one was open for 3% of the time, Pallas kernels for 9%

profile of v3, /device:TPU:1, one launch (start us, length us, event | category | flops | bytes accessed | tf_op | source)
XLA Modules:
  0.0 127.7 jit_solution(17740596671390156442)
XLA Ops:
  0.7 2.1 %prep.1.mine_ref = bf16[32,48,256]{2,1,0:T(8,128)(2,1)} custom-call(bf16[32,8192]{1,0:T(8,128)(2,1)} %x_ref.3, bf16[256,512]{1,0:T(8,128)(2,1)} %g_ref.1), custom_call_target="tpu_custom_call" | custom-call | bytes 1048576 | tf_op jit(solution)/shard_map/prep/pallas_call | solution.py:250
  2.8 11.9 %all-to-all-start = ((bf16[32,48,256]{2,1,0:T(8,128)(2,1)}), bf16[32,48,256]{2,1,0:T(8,128)(2,1)S(1)}, u32[]{:S(2)}, u32[]{:S(2)}) async-start(bf16[32,48,256]{2,1,0:T(8,128)(2,1)} %prep.1.mine_ref), calls=%async_computation | async-start | bytes 1572864 | tf_op jit(solution)/shard_map/all_to_all | solution.py:290
  14.7 0.1 copy.21.source_ref
  14.8 8.3 %agg.1 = (bf16[32,48,256]{2,1,0:T(8,128)(2,1)S(1)}, f32[64,128]{1,0:T(8,128)S(1)}) custom-call(s32[64,4]{1,0:T(8,128)S(1)} %copy.21.source_ref, s32[64]{0:T(128)S(1)} %copy-done.4, bf16[32,8192]{1,0:T(8,128)(2,1)} %x_ref.3, bf16[64,4,128,128]{3,2,1,0:T(8,128)(2,1)} %tiles_ref.3), custom_call_target="tpu_custom_call" | custom-call | flops 402653184 | bytes 9437184 | tf_op jit(solution)/shard_map/agg/pallas_call | solution.py:250
  23.1 0.9 copy-done
  24.0 9.9 %all-to-all-done.one_ref = bf16[32,48,256]{2,1,0:T(8,128)(2,1)S(1)} async-done(((bf16[32,48,256]{2,1,0:T(8,128)(2,1)}), bf16[32,48,256]{2,1,0:T(8,128)(2,1)S(1)}, u32[]{:S(2)}, u32[]{:S(2)}) %all-to-all-start) | async-done | bytes 786464 | tf_op jit(solution)/shard_map/all_to_all | solution.py:290
  33.9 5.6 %back.1 = bf16[32,48,256]{2,1,0:T(8,128)(2,1)} custom-call(s32[64,4]{1,0:T(8,128)S(1)} %copy.21.source_ref, s32[64]{0:T(128)S(1)} %copy-done.4, bf16[32,48,256]{2,1,0:T(8,128)(2,1)S(1)} %all-to-all-done.one_ref, f32[64,128]{1,0:T(8,128)S(1)} %get-tuple-element.11.scale_ref, bf16[64,4,128,128]{3,2,1,0:T(8,128)(2,1)} %tiles_ref.3, ...), custom_call_target="tpu_custom_call", output_to_operand_aliasing={{}: (5, {})} | custom-call | flops 134217728 | bytes 9437184 | tf_op jit(solution)/shard_map/back/pallas_call | solution.py:250
  39.5 8.4 %all-to-all-start.1 = ((bf16[32,48,256]{2,1,0:T(8,128)(2,1)}), bf16[32,48,256]{2,1,0:T(8,128)(2,1)S(1)}, u32[]{:S(2)}, u32[]{:S(2)}) async-start(bf16[32,48,256]{2,1,0:T(8,128)(2,1)} %back.1), calls=%async_computation.1 | async-start | bytes 1572864 | tf_op jit(solution)/shard_map/all_to_all | solution.py:311
  48.1 1.5 %copy.22 = bf16[1024,512]{0,1:T(8,128)(2,1)S(1)} copy(bf16[1024,512]{1,0:T(8,128)(2,1)} %param.16) | data formatting | bytes 2097152 | tf_op args[6]
  49.6 2.3 %copy.25 = bf16[1024,512]{0,1:T(8,128)(2,1)} copy(bf16[1024,512]{1,0:T(8,128)(2,1)} %param.17) | data formatting | bytes 2097152 | tf_op args[7]
  51.9 0.1 fusion.2
  52.1 1.7 %early.1 = (f32[512,256]{1,0:T(8,128)S(1)}, f32[512,256]{1,0:T(8,128)S(1)}) custom-call(bf16[32,48,256]{2,1,0:T(8,128)(2,1)} %prep.1.mine_ref, bf16[32,48,256]{2,1,0:T(8,128)(2,1)S(1)} %all-to-all-done.one_ref, bf16[512,1024]{1,0:T(8,128)(2,1)S(1)} %bitcast.17, bf16[512,512]{1,0:T(8,128)(2,1)S(1)} %copy-done.1), custom_call_target="tpu_custom_call" | custom-call | flops 419430400 | bytes 4194304 | tf_op jit(solution)/shard_map/early/pallas_call | solution.py:250
  53.8 0.8 copy-done.2
  54.6 0.8 copy-done.3
  55.4 12.3 %all-to-all-done.1.two_ref = bf16[32,48,256]{2,1,0:T(8,128)(2,1)S(1)} async-done(((bf16[32,48,256]{2,1,0:T(8,128)(2,1)}), bf16[32,48,256]{2,1,0:T(8,128)(2,1)S(1)}, u32[]{:S(2)}, u32[]{:S(2)}) %all-to-all-start.1) | async-done | bytes 786464 | tf_op jit(solution)/shard_map/all_to_all | solution.py:311
  67.7 3.3 %send.1 = (bf16[4,32,48,128]{3,2,1,0:T(8,128)(2,1)S(1)}, bf16[512,256]{1,0:T(8,128)(2,1)}, bf16[512,256]{1,0:T(8,128)(2,1)}) custom-call(s32[1]{0:T(128)} %bitcast.core_ref, bf16[32,48,256]{2,1,0:T(8,128)(2,1)} %prep.1.mine_ref, bf16[32,48,256]{2,1,0:T(8,128)(2,1)S(1)} %all-to-all-done.one_ref, bf16[32,48,256]{2,1,0:T(8,128)(2,1)S(1)} %all-to-all-done.1.two_ref, ...), custom_call_target="tpu_custom_call" | custom-call | flops 838860800 | bytes 6291456 | tf_op jit(solution)/shard_map/send/pallas_call | solution.py:250
  71.0 4.6 %collective-permute-start = (bf16[4,32,48,128]{3,2,1,0:T(8,128)(2,1)S(1)}, bf16[4,32,48,128]{3,2,1,0:T(8,128)(2,1)S(1)}, u32[]{:S(2)}, u32[]{:S(2)}) collective-permute-start(bf16[4,32,48,128]{3,2,1,0:T(8,128)(2,1)S(1)} %get-tuple-element.17), channel_id=1, source_target_pairs={{0,32},{32,0},{64,96},{96,64},{128,160},{160,128},{192,224},{224,1... | collective-permute-start | bytes 4718600 | tf_op jit(solution)/shard_map/ppermute | solution.py:345
  75.6 1.7 %keep.1.keep_ref = bf16[4,32,48,128]{3,2,1,0:T(8,128)(2,1)S(1)} custom-call(s32[1]{0:T(128)} %bitcast.core_ref, bf16[32,48,256]{2,1,0:T(8,128)(2,1)} %prep.1.mine_ref, bf16[32,48,256]{2,1,0:T(8,128)(2,1)S(1)} %all-to-all-done.one_ref, bf16[32,48,256]{2,1,0:T(8,128)(2,1)S(1)} %all-to-all-done.1.two_ref, bf16[512,256]{1,0:T(8,128)(2,1)} %get-tuple-element.15.hidden_ref, ...), custom_call_target="tpu_custom_call" | custom-call | flops 419430400 | bytes 3145728 | tf_op jit(solution)/shard_map/keep/pallas_call | solution.py:250
  77.3 1.3 %collective-permute-done.other_ref = bf16[4,32,48,128]{3,2,1,0:T(8,128)(2,1)S(1)} collective-permute-done((bf16[4,32,48,128]{3,2,1,0:T(8,128)(2,1)S(1)}, bf16[4,32,48,128]{3,2,1,0:T(8,128)(2,1)S(1)}, u32[]{:S(2)}, u32[]{:S(2)}) %collective-permute-start) | collective-permute-done | bytes 1572896 | tf_op jit(solution)/shard_map/ppermute | solution.py:345
  78.6 0.4 pair.1
  79.0 26.3 %all_to_all.20.got_ref = bf16[16,8,48,128]{3,2,1,0:T(8,128)(2,1)S(1)} all-to-all(bf16[16,8,48,128]{3,2,1,0:T(8,128)(2,1)S(1)} %bitcast.16), channel_id=1, replica_groups={{0,8,16,24,64,72,80,88,128,136,144,152,192,200,208,216},{1,9,17,25,65,7..., dimensions={0} | all-to-all | bytes 3145728 | tf_op jit(solution)/shard_map/all_to_all | solution.py:360
  105.3 0.2 gather.1
  105.5 11.3 %all_to_all.21 = bf16[8,48,128]{2,1,0:T(8,128)(2,1)S(1)} all-to-all(bf16[8,48,128]{2,1,0:T(8,128)(2,1)S(1)} %gather.1), channel_id=1, replica_groups={{0,1,2,3,4,5,6,7},{8,9,10,11,12,13,14,15},{16,17,18,19,20,21,22,23},{24..., dimensions={0} | all-to-all | bytes 196608 | tf_op jit(solution)/shard_map/all_to_all | solution.py:364
  116.8 3.2 %collective-permute-start.1 = (f32[48,128]{1,0:T(8,128)S(1)}, f32[48,128]{1,0:T(8,128)S(1)}, u32[]{:S(2)}, u32[]{:S(2)}) collective-permute-start(f32[48,128]{1,0:T(8,128)S(1)} %convert_reduce_fusion), channel_id=1, source_target_pairs={{0,32},{32,0},{64,96},{96,64},{128,160},{160,128},{192,224},{224,1... | collective-permute-start | bytes 73736 | tf_op jit(solution)/shard_map/ppermute | solution.py:366
  120.0 0.8 collective-permute-done.1
  120.9 0.6 collective-permute-start.4
  121.5 0.3 collective-permute-start.3
  121.7 0.6 collective-permute-start.2
  122.4 1.4 %collective-permute-done.4.refs_3_ = f32[2,48,128]{2,1,0:T(8,128)S(1)} collective-permute-done((f32[2,48,128]{2,1,0:T(8,128)S(1)}, f32[2,48,128]{2,1,0:T(8,128)S(1)}, u32[]{:S(2)}, u32[]{:S(2)}) %collective-permute-start.4) | collective-permute-done | bytes 49184 | tf_op jit(solution)/shard_map/ppermute | solution.py:369
  123.8 2.1 %collective-permute-done.3.refs_2_ = f32[2,48,128]{2,1,0:T(8,128)S(1)} collective-permute-done((f32[2,48,128]{2,1,0:T(8,128)S(1)}, f32[2,48,128]{2,1,0:T(8,128)S(1)}, u32[]{:S(2)}, u32[]{:S(2)}) %collective-permute-start.3) | collective-permute-done | bytes 49184 | tf_op jit(solution)/shard_map/ppermute | solution.py:369
  125.9 0.5 collective-permute-done.2.refs_1_
  126.4 1.2 place.1
  (17 shorter events, 0.3 us)
Async XLA Ops:
  0.6 14.0 %copy-start.5 = (s32[64,4]{0,1:T(4,128)S(1)}, s32[64,4]{0,1:T(4,128)}, u32[]{:S(2)}) copy-start(s32[64,4]{0,1:T(4,128)} %param.12) | copy-start | bytes 3076
  0.6 14.1 %copy-start.4 = (s32[64]{0:T(128)S(1)}, s32[64]{0:T(128)}, u32[]{:S(2)}) copy-start(s32[64]{0:T(128)} %count_ref.3) | copy-start | bytes 772
  2.8 31.1 %all-to-all-start = ((bf16[32,48,256]{2,1,0:T(8,128)(2,1)}), bf16[32,48,256]{2,1,0:T(8,128)(2,1)S(1)}, u32[]{:S(2)}, u32[]{:S(2)}) async-start(bf16[32,48,256]{2,1,0:T(8,128)(2,1)} %prep.1.mine_ref), calls=%async_computation | async-start | bytes 1572864 | tf_op jit(solution)/shard_map/all_to_all | solution.py:290
  23.1 0.9 copy-start
  39.5 8.4 %copy-start.6 = (s32[2,16]{1,0:T(2,128)S(1)}, s32[2,16]{1,0:T(2,128)}, u32[]{:S(2)}) copy-start(s32[2,16]{1,0:T(2,128)} %param.14) | copy-start | bytes 388
  39.5 28.2 %all-to-all-start.1 = ((bf16[32,48,256]{2,1,0:T(8,128)(2,1)}), bf16[32,48,256]{2,1,0:T(8,128)(2,1)S(1)}, u32[]{:S(2)}, u32[]{:S(2)}) async-start(bf16[32,48,256]{2,1,0:T(8,128)(2,1)} %back.1), calls=%async_computation.1 | async-start | bytes 1572864 | tf_op jit(solution)/shard_map/all_to_all | solution.py:311
  49.6 2.5 %copy-start.1 = (bf16[512,512]{1,0:T(8,128)(2,1)S(1)}, bf16[512,512]{1,0:T(8,128)(2,1)}, u32[]{:S(2)}) copy-start(bf16[512,512]{1,0:T(8,128)(2,1)} %wss_ref.1) | copy-start | bytes 1572868
  53.8 0.8 copy-start.2
  54.6 0.8 copy-start.3
  71.0 7.6 %collective-permute-start = (bf16[4,32,48,128]{3,2,1,0:T(8,128)(2,1)S(1)}, bf16[4,32,48,128]{3,2,1,0:T(8,128)(2,1)S(1)}, u32[]{:S(2)}, u32[]{:S(2)}) collective-permute-start(bf16[4,32,48,128]{3,2,1,0:T(8,128)(2,1)S(1)} %get-tuple-element.17), channel_id=1, source_target_pairs={{0,32},{32,0},{64,96},{96,64},{128,160},{160,128},{192,224},{224,1... | collective-permute-start | bytes 4718600 | tf_op jit(solution)/shard_map/ppermute | solution.py:345
  116.8 4.0 %collective-permute-start.1 = (f32[48,128]{1,0:T(8,128)S(1)}, f32[48,128]{1,0:T(8,128)S(1)}, u32[]{:S(2)}, u32[]{:S(2)}) collective-permute-start(f32[48,128]{1,0:T(8,128)S(1)} %convert_reduce_fusion), channel_id=1, source_target_pairs={{0,32},{32,0},{64,96},{96,64},{128,160},{160,128},{192,224},{224,1... | collective-permute-start | bytes 73736 | tf_op jit(solution)/shard_map/ppermute | solution.py:366
  120.9 2.9 %collective-permute-start.4 = (f32[2,48,128]{2,1,0:T(8,128)S(1)}, f32[2,48,128]{2,1,0:T(8,128)S(1)}, u32[]{:S(2)}, u32[]{:S(2)}) collective-permute-start(f32[2,48,128]{2,1,0:T(8,128)S(1)} %pad_maximum_fusion.refs_0_), channel_id=1, source_target_pairs={{0,192},{32,224},{64,0},{96,32},{128,64},{160,96},{192,128},{224,1... | collective-permute-start | bytes 147464 | tf_op jit(solution)/shard_map/ppermute | solution.py:369
  121.5 4.5 %collective-permute-start.3 = (f32[2,48,128]{2,1,0:T(8,128)S(1)}, f32[2,48,128]{2,1,0:T(8,128)S(1)}, u32[]{:S(2)}, u32[]{:S(2)}) collective-permute-start(f32[2,48,128]{2,1,0:T(8,128)S(1)} %pad_maximum_fusion.refs_0_), channel_id=1, source_target_pairs={{0,128},{32,160},{64,192},{96,224},{128,0},{160,32},{192,64},{224,... | collective-permute-start | bytes 147464 | tf_op jit(solution)/shard_map/ppermute | solution.py:369
  121.7 4.7 %collective-permute-start.2 = (f32[2,48,128]{2,1,0:T(8,128)S(1)}, f32[2,48,128]{2,1,0:T(8,128)S(1)}, u32[]{:S(2)}, u32[]{:S(2)}) collective-permute-start(f32[2,48,128]{2,1,0:T(8,128)S(1)} %pad_maximum_fusion.refs_0_), channel_id=1, source_target_pairs={{0,64},{32,96},{64,128},{96,160},{128,192},{160,224},{192,0},{224,... | collective-permute-start | bytes 147464 | tf_op jit(solution)/shard_map/ppermute | solution.py:369

commit v4 on v3

--- a/solution.py
+++ b/solution.py
@@ -10,6 +10,7 @@
 BF = jnp.bfloat16
 F32 = jnp.float32
 STEP = 8
+FRONT = 16
 FEATS = 32
 LAST = (((1,), (1,)), ((), ()))
 
@@ -40,7 +41,7 @@
         out_ref[o, :FEATS, :] = x_held[:, o * width : (o + 1) * width]
 
 
-def agg_kernel(source_ref, count_ref, x_ref, tiles_ref, agg_ref, scale_ref, x_held, held_ref, x_sem, sems):
+def agg_kernel(source_ref, count_ref, x_ref, tiles_ref, agg_ref, scale_ref, front_ref, x_held, held_ref, x_sem, sems):
     blocks, slots, side, _ = held_ref.shape
     steps = blocks // STEP
     copies = begin([(x_ref, x_held)], x_sem)
@@ -66,27 +67,38 @@
             agg_ref[b // 2, :FEATS, (j % 2) * side : (j % 2 + 1) * side] = (out[:FEATS] * scale).astype(BF)
             scale_ref[pl.ds(b, 1)] = scale
 
-
-def back_kernel(source_ref, count_ref, one_ref, scale_ref, tiles_ref, agg_ref, out_ref, acc_ref, q_ref, held_ref, sems, out_sem):
+    front_ref[...] = held_ref[: front_ref.shape[0]]
+
+
+def back_kernel(
+    source_ref, count_ref, one_ref, scale_ref, tiles_ref, front_ref, agg_ref, out_ref, acc_ref, q_ref, held_ref, sems, out_sem
+):
     blocks, slots, side, _ = held_ref.shape
-    steps = blocks // STEP
-    for i in range(steps):
+    steps, first = blocks // STEP, front_ref.shape[0] // STEP
+    for i in range(first, steps):
         chunk(tiles_ref, held_ref, sems, i).start()
     acc_ref[...] = jnp.zeros_like(acc_ref)
 
-    @pl.loop(0, steps)
-    def _(i):
-        chunk(tiles_ref, held_ref, sems, i).wait()
+    def add_up(i, tiles):
         for j in range(STEP):
             b = i * STEP + j
             count = count_ref[b]
             g = one_ref[b // 2, FEATS:, (j % 2) * side : (j % 2 + 1) * side].astype(F32)
             g = (g * scale_ref[pl.ds(b, 1)]).astype(BF)
-            rhs = jnp.concatenate([held_ref[b, t] for t in range(slots)], axis=1)
+            rhs = jnp.concatenate([tiles[b, t] for t in range(slots)], axis=1)
             out = jnp.dot(g, rhs, preferred_element_type=F32)
             for t in range(slots):
                 src = source_ref[b, t]
                 acc_ref[src] = acc_ref[src] + out[:, t * side : (t + 1) * side] * alive(count, t)
+
+    @pl.loop(0, first)
+    def _(i):
+        add_up(i, front_ref)
+
+    @pl.loop(first, steps)
+    def _(i):
+        chunk(tiles_ref, held_ref, sems, i).wait()
+        add_up(i, held_ref)
 
     for o in range(q_ref.shape[0]):
         q_ref[o, :, :side] = acc_ref[2 * o].astype(BF)
@@ -237,8 +249,10 @@
     run = pl.pallas_call(
         kernel,
         in_specs=list(ins),
-        out_specs=[HBM if len(o) > 2 else VMEM for o in outs],
-        out_shape=[(pltpu.HBM if len(o) > 2 else jax.ShapeDtypeStruct)(*o[:2]) for o in outs],
+        out_specs=[o[2] if len(o) > 2 else VMEM for o in outs],
+        out_shape=[
+            ((pltpu.HBM if o[2] is HBM else pltpu.VMEM) if len(o) > 2 else jax.ShapeDtypeStruct)(*o[:2]) for o in outs
+        ],
         scratch_shapes=list(scratch),
         input_output_aliases=aliases or {},
         compiler_params=pltpu.CompilerParams(vmem_limit_bytes=24 << 20),
@@ -289,11 +303,11 @@
     )(node_features, cotangent)
     one = exchange(mine)
     held = pltpu.VMEM((blocks, slots, side, side), BF)
-    agg, scaling = call(
+    agg, scaling, front = call(
         agg_kernel,
         "agg",
         [SMEM, SMEM, HBM, HBM],
-        [((owners, rows, width), BF), ((blocks, side), F32)],
+        [((owners, rows, width), BF), ((blocks, side), F32), ((FRONT,) + edge_tiles.shape[1:], BF, VMEM)],
         [pltpu.VMEM((feats, nodes), BF), held, DMA((1,)), DMA((steps,))],
         flops=2 * 48 * 512 * 8192,
         size=9 << 20,
@@ -301,13 +315,13 @@
     (send,) = call(
         back_kernel,
         "back",
-        [SMEM, SMEM, VMEM, VMEM, HBM, HBM],
+        [SMEM, SMEM, VMEM, VMEM, HBM, VMEM, HBM],
         [((owners, rows, width), BF, HBM)],
         [pltpu.VMEM((blocks, cols, side), F32), pltpu.VMEM((owners, cols, width), BF), held, DMA((steps,)), DMA((1,))],
         flops=2 * 16 * 512 * 8192,
         size=9 << 20,
-        aliases={5: 0},
-    )(tile_source, tile_count, one, scaling, edge_tiles, agg)
+        aliases={6: 0},
+    )(tile_source, tile_count, one, scaling, edge_tiles, front, agg)
     two = exchange(send)
 
     shifts = jnp.arange(32, dtype=jnp.int32)

time: 128 us -> 128 us (level)
  waiting for transfers between devices: 28.4 us -> 27.1 us
  transfers between devices with their start and end apart: 7 -> 7, of which waited for: 7 -> 6; matrix products, arithmetic and copies ran while one was open for 3% -> 3% of each run, Pallas kernels for 9% -> 9%
where the time goes in v4:
time: 128 us; the launch traced here: 127 us
  blocking collectives  37.6 us (29%)
  starting transfers between devices  30.7 us (24%)
  waiting for transfers between devices  27.1 us (21%)
  Pallas kernels  24 us (19%)
  local copies, waits for them, and re-layouts  6.56 us (5%)
    all_to_all x1, blocking collectives, local(): lax.all_to_all(pair.reshape(ys * xs, zs, rows, 128), ('dp', 'feat'), 0, 0...  26.3 us
    pallas_call x9, Pallas kernels, apply(): run(*(pltpu.with_memory_space_constraint(a, pltpu.HBM) if spec is HBM els...  24 us
    all_to_all x1, waiting for transfers between devices, local(): two = exchange(send)  12.4 us
    all_to_all x1, starting transfers between devices, local(): one = exchange(mine)  11.9 us
    all_to_all x1, blocking collectives, local(): exchange(own, axis_index_groups=[[a * zs + b for b in range(zs)] for a in...  11.3 us
    all_to_all x1, waiting for transfers between devices, local(): one = exchange(mine)  9.86 us
    all_to_all x1, starting transfers between devices, local(): two = exchange(send)  8.37 us
    unnamed x18, local copies, waits for them, and re-layouts  6.48 us
  transfers between devices with their start and end apart: 7, of which 6 were waited for; matrix products, arithmetic and copies ran while one was open for 3% of the time, Pallas kernels for 9%

profile of v4, /device:TPU:1, one launch (start us, length us, event | category | flops | bytes accessed | tf_op | source)
XLA Modules:
  0.0 127.1 jit_solution(6036347462610361469)
XLA Ops:
  0.7 2.1 %prep.1.mine_ref = bf16[32,48,256]{2,1,0:T(8,128)(2,1)} custom-call(bf16[32,8192]{1,0:T(8,128)(2,1)} %x_ref.3, bf16[256,512]{1,0:T(8,128)(2,1)} %g_ref.1), custom_call_target="tpu_custom_call" | custom-call | bytes 1048576 | tf_op jit(solution)/shard_map/prep/pallas_call | solution.py:264
  2.8 11.9 %all-to-all-start = ((bf16[32,48,256]{2,1,0:T(8,128)(2,1)}), bf16[32,48,256]{2,1,0:T(8,128)(2,1)S(1)}, u32[]{:S(2)}, u32[]{:S(2)}) async-start(bf16[32,48,256]{2,1,0:T(8,128)(2,1)} %prep.1.mine_ref), calls=%async_computation | async-start | bytes 1572864 | tf_op jit(solution)/shard_map/all_to_all | solution.py:304
  14.7 0.1 copy.21.source_ref
  14.8 8.4 %agg.1 = (bf16[32,48,256]{2,1,0:T(8,128)(2,1)S(1)}, f32[64,128]{1,0:T(8,128)S(1)}, bf16[16,4,128,128]{3,2,1,0:T(8,128)(2,1)S(1)}) custom-call(s32[64,4]{1,0:T(8,128)S(1)} %copy.21.source_ref, s32[64]{0:T(128)S(1)} %copy-done.4, bf16[32,8192]{1,0:T(8,128)(2,1)} %x_ref.3, bf16[64,4,128,128]{3,2,1,0:T(8,128)(2,1)} %tiles_ref.3), custom_call_target="tpu_custom_call" | custom-call | flops 402653184 | bytes 9437184 | tf_op jit(solution)/shard_map/agg/pallas_call | solution.py:264
  23.1 0.9 copy-done
  24.1 9.9 %all-to-all-done.one_ref = bf16[32,48,256]{2,1,0:T(8,128)(2,1)S(1)} async-done(((bf16[32,48,256]{2,1,0:T(8,128)(2,1)}), bf16[32,48,256]{2,1,0:T(8,128)(2,1)S(1)}, u32[]{:S(2)}, u32[]{:S(2)}) %all-to-all-start) | async-done | bytes 786464 | tf_op jit(solution)/shard_map/all_to_all | solution.py:304
  33.9 5.0 %back.1 = bf16[32,48,256]{2,1,0:T(8,128)(2,1)} custom-call(s32[64,4]{1,0:T(8,128)S(1)} %copy.21.source_ref, s32[64]{0:T(128)S(1)} %copy-done.4, bf16[32,48,256]{2,1,0:T(8,128)(2,1)S(1)} %all-to-all-done.one_ref, f32[64,128]{1,0:T(8,128)S(1)} %get-tuple-element.12.scale_ref, bf16[64,4,128,128]{3,2,1,0:T(8,128)(2,1)} %tiles_ref.3, ...), custom_call_target="tpu_custom_call", output_to_operand_aliasing={{}: (6, {})} | custom-call | flops 134217728 | bytes 9437184 | tf_op jit(solution)/shard_map/back/pallas_call | solution.py:264
  38.9 8.4 %all-to-all-start.1 = ((bf16[32,48,256]{2,1,0:T(8,128)(2,1)}), bf16[32,48,256]{2,1,0:T(8,128)(2,1)S(1)}, u32[]{:S(2)}, u32[]{:S(2)}) async-start(bf16[32,48,256]{2,1,0:T(8,128)(2,1)} %back.1), calls=%async_computation.1 | async-start | bytes 1572864 | tf_op jit(solution)/shard_map/all_to_all | solution.py:325
  47.3 1.5 %copy.22 = bf16[1024,512]{0,1:T(8,128)(2,1)S(1)} copy(bf16[1024,512]{1,0:T(8,128)(2,1)} %param.16) | data formatting | bytes 2097152 | tf_op args[6]
  48.8 0.1 shift_right_arithmetic.23
  48.9 0.1 copy.23
  49.0 2.3 %copy.25 = bf16[1024,512]{0,1:T(8,128)(2,1)} copy(bf16[1024,512]{1,0:T(8,128)(2,1)} %param.17) | data formatting | bytes 2097152 | tf_op args[7]
  51.3 0.1 fusion.2
  51.4 1.7 %early.1 = (f32[512,256]{1,0:T(8,128)S(1)}, f32[512,256]{1,0:T(8,128)S(1)}) custom-call(bf16[32,48,256]{2,1,0:T(8,128)(2,1)} %prep.1.mine_ref, bf16[32,48,256]{2,1,0:T(8,128)(2,1)S(1)} %all-to-all-done.one_ref, bf16[512,1024]{1,0:T(8,128)(2,1)S(1)} %bitcast.17, bf16[512,512]{1,0:T(8,128)(2,1)S(1)} %copy-done.1), custom_call_target="tpu_custom_call" | custom-call | flops 419430400 | bytes 4194304 | tf_op jit(solution)/shard_map/early/pallas_call | solution.py:264
  53.1 0.8 copy-done.2
  53.9 0.8 copy-done.3
  54.7 12.4 %all-to-all-done.1.two_ref = bf16[32,48,256]{2,1,0:T(8,128)(2,1)S(1)} async-done(((bf16[32,48,256]{2,1,0:T(8,128)(2,1)}), bf16[32,48,256]{2,1,0:T(8,128)(2,1)S(1)}, u32[]{:S(2)}, u32[]{:S(2)}) %all-to-all-start.1) | async-done | bytes 786464 | tf_op jit(solution)/shard_map/all_to_all | solution.py:325
  67.1 3.3 %send.1 = (bf16[4,32,48,128]{3,2,1,0:T(8,128)(2,1)S(1)}, bf16[512,256]{1,0:T(8,128)(2,1)}, bf16[512,256]{1,0:T(8,128)(2,1)}) custom-call(s32[1]{0:T(128)} %bitcast.core_ref, bf16[32,48,256]{2,1,0:T(8,128)(2,1)} %prep.1.mine_ref, bf16[32,48,256]{2,1,0:T(8,128)(2,1)S(1)} %all-to-all-done.one_ref, bf16[32,48,256]{2,1,0:T(8,128)(2,1)S(1)} %all-to-all-done.1.two_ref, ...), custom_call_target="tpu_custom_call" | custom-call | flops 838860800 | bytes 6291456 | tf_op jit(solution)/shard_map/send/pallas_call | solution.py:264
  70.4 4.6 %collective-permute-start = (bf16[4,32,48,128]{3,2,1,0:T(8,128)(2,1)S(1)}, bf16[4,32,48,128]{3,2,1,0:T(8,128)(2,1)S(1)}, u32[]{:S(2)}, u32[]{:S(2)}) collective-permute-start(bf16[4,32,48,128]{3,2,1,0:T(8,128)(2,1)S(1)} %get-tuple-element.19), channel_id=1, source_target_pairs={{0,32},{32,0},{64,96},{96,64},{128,160},{160,128},{192,224},{224,1... | collective-permute-start | bytes 4718600 | tf_op jit(solution)/shard_map/ppermute | solution.py:359
  75.0 1.7 %keep.1.keep_ref = bf16[4,32,48,128]{3,2,1,0:T(8,128)(2,1)S(1)} custom-call(s32[1]{0:T(128)} %bitcast.core_ref, bf16[32,48,256]{2,1,0:T(8,128)(2,1)} %prep.1.mine_ref, bf16[32,48,256]{2,1,0:T(8,128)(2,1)S(1)} %all-to-all-done.one_ref, bf16[32,48,256]{2,1,0:T(8,128)(2,1)S(1)} %all-to-all-done.1.two_ref, bf16[512,256]{1,0:T(8,128)(2,1)} %get-tuple-element.17.hidden_ref, ...), custom_call_target="tpu_custom_call" | custom-call | flops 419430400 | bytes 3145728 | tf_op jit(solution)/shard_map/keep/pallas_call | solution.py:264
  76.7 1.3 %collective-permute-done.other_ref = bf16[4,32,48,128]{3,2,1,0:T(8,128)(2,1)S(1)} collective-permute-done((bf16[4,32,48,128]{3,2,1,0:T(8,128)(2,1)S(1)}, bf16[4,32,48,128]{3,2,1,0:T(8,128)(2,1)S(1)}, u32[]{:S(2)}, u32[]{:S(2)}) %collective-permute-start) | collective-permute-done | bytes 1572896 | tf_op jit(solution)/shard_map/ppermute | solution.py:359
  78.0 0.4 pair.1
  78.4 26.3 %all_to_all.20.got_ref = bf16[16,8,48,128]{3,2,1,0:T(8,128)(2,1)S(1)} all-to-all(bf16[16,8,48,128]{3,2,1,0:T(8,128)(2,1)S(1)} %bitcast.16), channel_id=1, replica_groups={{0,8,16,24,64,72,80,88,128,136,144,152,192,200,208,216},{1,9,17,25,65,7..., dimensions={0} | all-to-all | bytes 3145728 | tf_op jit(solution)/shard_map/all_to_all | solution.py:374
  104.7 0.2 gather.1
  104.9 11.3 %all_to_all.21 = bf16[8,48,128]{2,1,0:T(8,128)(2,1)S(1)} all-to-all(bf16[8,48,128]{2,1,0:T(8,128)(2,1)S(1)} %gather.1), channel_id=1, replica_groups={{0,1,2,3,4,5,6,7},{8,9,10,11,12,13,14,15},{16,17,18,19,20,21,22,23},{24..., dimensions={0} | all-to-all | bytes 196608 | tf_op jit(solution)/shard_map/all_to_all | solution.py:378
  116.2 3.2 %collective-permute-start.1 = (f32[48,128]{1,0:T(8,128)S(1)}, f32[48,128]{1,0:T(8,128)S(1)}, u32[]{:S(2)}, u32[]{:S(2)}) collective-permute-start(f32[48,128]{1,0:T(8,128)S(1)} %convert_reduce_fusion), channel_id=1, source_target_pairs={{0,32},{32,0},{64,96},{96,64},{128,160},{160,128},{192,224},{224,1... | collective-permute-start | bytes 73736 | tf_op jit(solution)/shard_map/ppermute | solution.py:380
  119.4 0.8 collective-permute-done.1
  120.3 1.8 %collective-permute-start.3 = (f32[2,48,128]{2,1,0:T(8,128)S(1)}, f32[2,48,128]{2,1,0:T(8,128)S(1)}, u32[]{:S(2)}, u32[]{:S(2)}) collective-permute-start(f32[2,48,128]{2,1,0:T(8,128)S(1)} %pad_maximum_fusion.refs_0_), channel_id=1, source_target_pairs={{0,128},{32,160},{64,192},{96,224},{128,0},{160,32},{192,64},{224,... | collective-permute-start | bytes 147464 | tf_op jit(solution)/shard_map/ppermute | solution.py:383
  122.0 0.9 collective-permute-start.4
  123.0 2.3 %collective-permute-done.2.refs_1_ = f32[2,48,128]{2,1,0:T(8,128)S(1)} collective-permute-done((f32[2,48,128]{2,1,0:T(8,128)S(1)}, f32[2,48,128]{2,1,0:T(8,128)S(1)}, u32[]{:S(2)}, u32[]{:S(2)}) %collective-permute-start.2) | collective-permute-done | bytes 49184 | tf_op jit(solution)/shard_map/ppermute | solution.py:383
  125.3 0.5 collective-permute-done.4.refs_3_
  125.8 1.2 place.1
  (17 shorter events, 0.1 us)
Async XLA Ops:
  0.6 14.0 %copy-start.5 = (s32[64,4]{0,1:T(4,128)S(1)}, s32[64,4]{0,1:T(4,128)}, u32[]{:S(2)}) copy-start(s32[64,4]{0,1:T(4,128)} %param.12) | copy-start | bytes 3076
  0.6 14.1 %copy-start.4 = (s32[64]{0:T(128)S(1)}, s32[64]{0:T(128)}, u32[]{:S(2)}) copy-start(s32[64]{0:T(128)} %count_ref.3) | copy-start | bytes 772
  2.8 31.1 %all-to-all-start = ((bf16[32,48,256]{2,1,0:T(8,128)(2,1)}), bf16[32,48,256]{2,1,0:T(8,128)(2,1)S(1)}, u32[]{:S(2)}, u32[]{:S(2)}) async-start(bf16[32,48,256]{2,1,0:T(8,128)(2,1)} %prep.1.mine_ref), calls=%async_computation | async-start | bytes 1572864 | tf_op jit(solution)/shard_map/all_to_all | solution.py:304
  23.1 0.9 copy-start
  38.9 10.0 %copy-start.6 = (s32[2,16]{1,0:T(2,128)S(1)}, s32[2,16]{1,0:T(2,128)}, u32[]{:S(2)}) copy-start(s32[2,16]{1,0:T(2,128)} %param.14) | copy-start | bytes 388
  38.9 28.2 %all-to-all-start.1 = ((bf16[32,48,256]{2,1,0:T(8,128)(2,1)}), bf16[32,48,256]{2,1,0:T(8,128)(2,1)S(1)}, u32[]{:S(2)}, u32[]{:S(2)}) async-start(bf16[32,48,256]{2,1,0:T(8,128)(2,1)} %back.1), calls=%async_computation.1 | async-start | bytes 1572864 | tf_op jit(solution)/shard_map/all_to_all | solution.py:325
  48.8 2.6 %copy-start.1 = (bf16[512,512]{1,0:T(8,128)(2,1)S(1)}, bf16[512,512]{1,0:T(8,128)(2,1)}, u32[]{:S(2)}) copy-start(bf16[512,512]{1,0:T(8,128)(2,1)} %wss_ref.1) | copy-start | bytes 1572868
  53.1 0.8 copy-start.2
  53.9 0.8 copy-start.3
  70.4 7.6 %collective-permute-start = (bf16[4,32,48,128]{3,2,1,0:T(8,128)(2,1)S(1)}, bf16[4,32,48,128]{3,2,1,0:T(8,128)(2,1)S(1)}, u32[]{:S(2)}, u32[]{:S(2)}) collective-permute-start(bf16[4,32,48,128]{3,2,1,0:T(8,128)(2,1)S(1)} %get-tuple-element.19), channel_id=1, source_target_pairs={{0,32},{32,0},{64,96},{96,64},{128,160},{160,128},{192,224},{224,1... | collective-permute-start | bytes 4718600 | tf_op jit(solution)/shard_map/ppermute | solution.py:359
  116.2 4.0 %collective-permute-start.1 = (f32[48,128]{1,0:T(8,128)S(1)}, f32[48,128]{1,0:T(8,128)S(1)}, u32[]{:S(2)}, u32[]{:S(2)}) collective-permute-start(f32[48,128]{1,0:T(8,128)S(1)} %convert_reduce_fusion), channel_id=1, source_target_pairs={{0,32},{32,0},{64,96},{96,64},{128,160},{160,128},{192,224},{224,1... | collective-permute-start | bytes 73736 | tf_op jit(solution)/shard_map/ppermute | solution.py:380
  120.3 5.1 %collective-permute-start.2 = (f32[2,48,128]{2,1,0:T(8,128)S(1)}, f32[2,48,128]{2,1,0:T(8,128)S(1)}, u32[]{:S(2)}, u32[]{:S(2)}) collective-permute-start(f32[2,48,128]{2,1,0:T(8,128)S(1)} %pad_maximum_fusion.refs_0_), channel_id=1, source_target_pairs={{0,64},{32,96},{64,128},{96,160},{128,192},{160,224},{192,0},{224,... | collective-permute-start | bytes 147464 | tf_op jit(solution)/shard_map/ppermute | solution.py:383
  120.3 5.1 %collective-permute-start.3 = (f32[2,48,128]{2,1,0:T(8,128)S(1)}, f32[2,48,128]{2,1,0:T(8,128)S(1)}, u32[]{:S(2)}, u32[]{:S(2)}) collective-permute-start(f32[2,48,128]{2,1,0:T(8,128)S(1)} %pad_maximum_fusion.refs_0_), channel_id=1, source_target_pairs={{0,128},{32,160},{64,192},{96,224},{128,0},{160,32},{192,64},{224,... | collective-permute-start | bytes 147464 | tf_op jit(solution)/shard_map/ppermute | solution.py:383
  122.0 3.8 %collective-permute-start.4 = (f32[2,48,128]{2,1,0:T(8,128)S(1)}, f32[2,48,128]{2,1,0:T(8,128)S(1)}, u32[]{:S(2)}, u32[]{:S(2)}) collective-permute-start(f32[2,48,128]{2,1,0:T(8,128)S(1)} %pad_maximum_fusion.refs_0_), channel_id=1, source_target_pairs={{0,192},{32,224},{64,0},{96,32},{128,64},{160,96},{192,128},{224,1... | collective-permute-start | bytes 147464 | tf_op jit(solution)/shard_map/ppermute | solution.py:383

commit v5 on v4

--- a/solution.py
+++ b/solution.py
@@ -213,15 +213,22 @@
             write_half(core, gt_held, one_ref, two_ref, hidden[...], d_pre[...], keep_ref)
 
 
-def pair_kernel(keep_ref, other_ref, out_ref):
-    out_ref[...] = (keep_ref[...].astype(F32) + other_ref[...].astype(F32)).astype(BF)
-
-
-def gather_kernel(got_ref, out_ref):
-    total = got_ref[0].astype(F32)
-    for i in range(1, got_ref.shape[0]):
-        total = total + got_ref[i].astype(F32)
-    out_ref[...] = total.astype(BF)
+def add(*terms):
+    total = terms[0].astype(F32)
+    for term in terms[1:]:
+        total = total + term.astype(F32)
+    return total.astype(BF)
+
+
+def pair_kernel(slot_ref, keep_ref, other_ref, *outs):
+    for i, out in enumerate(outs):
+        for j in range(4):
+            slot = slot_ref[4 * i + j]
+            out[j] = add(keep_ref[slot], other_ref[slot])
+
+
+def square_kernel(own_ref, got_one, got_two, got_three, out_ref):
+    out_ref[...] = add(own_ref[...], got_one[...], got_two[...], got_three[...])
 
 
 def place_kernel(where_ref, *refs):
@@ -367,15 +374,43 @@
         size=3 << 20,
     )(core, mine, one, two, hidden, d_pre)
 
-    (pair,) = call(pair_kernel, "pair", [VMEM] * 2, [half], size=5 << 20)(kept, other)
-    planes = [
-        [(2 * y + c) * owners + x * zs + z for y in range(ys) for x in range(xs)] for c in range(2) for z in range(zs)
+    def trade(value, member):
+        flips = (1, 3)
+        pairs = []
+        for y in range(ys):
+            for c in range(2):
+                for x in range(xs):
+                    there = ((y ^ (flips[c] * (member // 2))) * 2 + c) * owners + (x ^ (flips[c] * (member % 2))) * zs
+                    here = (2 * y + c) * owners + x * zs
+                    pairs += [(here + z, there + z) for z in range(zs)]
+        return lax.ppermute(value, ("dp", "feat"), pairs)
+
+    def ordered(at, flip):
+        return jnp.stack([jnp.minimum(at, at ^ flip), jnp.maximum(at, at ^ flip)])
+
+    x, y = lax.axis_index("feat") // zs, lax.axis_index("dp") // 2
+    near = jnp.where(core[0] == 0, 1, 3)
+    slots = [
+        ordered(y ^ (near * (m // 2)), near ^ 2)[:, None] * xs + ordered(x ^ (near * (m % 2)), near ^ 2)[None]
+        for m in range(4)
     ]
-    got = lax.all_to_all(
-        pair.reshape(ys * xs, zs, rows, 128), ("dp", "feat"), 0, 0, tiled=True, axis_index_groups=planes
-    )
-    (own,) = call(gather_kernel, "gather", [VMEM], [((zs, rows, 128), BF)], size=2 << 20)(got)
-    shares = exchange(own, axis_index_groups=[[a * zs + b for b in range(zs)] for a in range(xs)])
+    parts = (ys * xs, zs, rows, 128)
+    four = ((4,) + parts[1:], BF)
+    own, *sends = call(pair_kernel, "pair", [SMEM, VMEM, VMEM], [four] * 4, size=5 << 20)(
+        jnp.stack(slots).reshape(ys * xs).astype(jnp.int32), kept.reshape(parts), other.reshape(parts)
+    )
+    got = [trade(sends[m - 1], m) for m in (1, 2, 3)]
+    (own,) = call(square_kernel, "square", [VMEM] * 4, [four], size=2 << 20)(own, *got)
+    lines = (((0, 3), (1, 2)), ((0, 1), (2, 3)))
+    groups = [
+        [(2 * y + c) * owners + x * zs + z for y in line for x in row for z in range(zs)]
+        for c in range(2)
+        for line in lines[c]
+        for row in lines[c]
+    ]
+    shares = lax.all_to_all(
+        own.reshape(4 * zs, rows, 128), ("dp", "feat"), 0, 0, tiled=True, axis_index_groups=groups
+    )
     share = jnp.sum(shares.astype(F32), axis=0)
     both = jnp.stack([share, lax.ppermute(share, "dp", swap)])
     moved = {0: both}

time: 128 us -> 126 us (0.984)
  blocking collectives: 37.6 us -> 17.8 us
  waiting for transfers between devices: 27.1 us -> 34.8 us
  starting transfers between devices: 30.7 us -> 35.8 us
  local copies, waits for them, and re-layouts: 6.56 us -> 9.53 us
  Pallas kernels: 24 us -> 25.7 us
    all_to_all x2 -> x1, blocking collectives: 37.6 us -> 17.8 us  [local(): lax.all_to_all(own.reshape(4 * zs, rows, 128), ('dp', 'feat'), 0, 0, tile...]
    ppermute x0 -> x3, waiting for transfers between devices: none -> 9.37 us  [trade(): return lax.ppermute(value, ('dp', 'feat'), pairs)]
    ppermute x0 -> x3, starting transfers between devices: none -> 5.21 us  [trade(): return lax.ppermute(value, ('dp', 'feat'), pairs)]
    unnamed x18 -> x22, local copies, waits for them, and re-layouts: 6.48 us -> 9.36 us
    pallas_call x9, Pallas kernels: 24 us -> 25.7 us  [apply(): run(*(pltpu.with_memory_space_constraint(a, pltpu.HBM) if spec is HBM els...]
    all_to_all x1, waiting for transfers between devices: 9.86 us -> 8.55 us  [local(): one = exchange(mine)]
  transfers between devices with their start and end apart: 7 -> 10, of which waited for: 6 -> 10; matrix products, arithmetic and copies ran while one was open for 3% -> 4% of each run, Pallas kernels for 9% -> 9%
where the time goes in v5:
time: 126 us; the launch traced here: 125 us
  starting transfers between devices  35.8 us (28%)
  waiting for transfers between devices  34.8 us (28%)
  Pallas kernels  25.7 us (20%)
  blocking collectives  17.8 us (14%)
  local copies, waits for them, and re-layouts  9.53 us (8%)
    pallas_call x9, Pallas kernels, apply(): run(*(pltpu.with_memory_space_constraint(a, pltpu.HBM) if spec is HBM els...  25.7 us
    all_to_all x1, blocking collectives, local(): lax.all_to_all(own.reshape(4 * zs, rows, 128), ('dp', 'feat'), 0, 0, tile...  17.8 us
    all_to_all x1, waiting for transfers between devices, local(): two = exchange(send)  12.4 us
    all_to_all x1, starting transfers between devices, local(): one = exchange(mine)  11.9 us
    ppermute x3, waiting for transfers between devices, trade(): return lax.ppermute(value, ('dp', 'feat'), pairs)  9.37 us
    unnamed x22, local copies, waits for them, and re-layouts  9.36 us
    all_to_all x1, waiting for transfers between devices, local(): one = exchange(mine)  8.55 us
    all_to_all x1, starting transfers between devices, local(): two = exchange(send)  8.37 us
  transfers between devices with their start and end apart: 10, of which 10 were waited for; matrix products, arithmetic and copies ran while one was open for 4% of the time, Pallas kernels for 9%

profile of v5, /device:TPU:1, one launch (start us, length us, event | category | flops | bytes accessed | tf_op | source)
XLA Modules:
  0.0 125.0 jit_solution(18432490539645693871)
XLA Ops:
  0.7 2.1 %prep.1.mine_ref = bf16[32,48,256]{2,1,0:T(8,128)(2,1)} custom-call(bf16[32,8192]{1,0:T(8,128)(2,1)} %x_ref.3, bf16[256,512]{1,0:T(8,128)(2,1)} %g_ref.1), custom_call_target="tpu_custom_call" | custom-call | bytes 1048576 | tf_op jit(solution)/shard_map/prep/pallas_call | solution.py:271
  2.7 11.9 %all-to-all-start = ((bf16[32,48,256]{2,1,0:T(8,128)(2,1)}), bf16[32,48,256]{2,1,0:T(8,128)(2,1)S(1)}, u32[]{:S(2)}, u32[]{:S(2)}) async-start(bf16[32,48,256]{2,1,0:T(8,128)(2,1)} %prep.1.mine_ref), calls=%async_computation | async-start | bytes 1572864 | tf_op jit(solution)/shard_map/all_to_all | solution.py:311
  14.7 8.4 %agg.1 = (bf16[32,48,256]{2,1,0:T(8,128)(2,1)S(1)}, f32[64,128]{1,0:T(8,128)S(1)}, bf16[16,4,128,128]{3,2,1,0:T(8,128)(2,1)S(1)}) custom-call(s32[64,4]{1,0:T(8,128)S(1)} %copy.26.source_ref, s32[64]{0:T(128)S(1)} %copy-done.6, bf16[32,8192]{1,0:T(8,128)(2,1)} %x_ref.3, bf16[64,4,128,128]{3,2,1,0:T(8,128)(2,1)} %tiles_ref.3), custom_call_target="tpu_custom_call" | custom-call | flops 402653184 | bytes 9437184 | tf_op jit(solution)/shard_map/agg/pallas_call | solution.py:271
  23.1 0.9 copy-done
  24.0 1.3 %copy-done.1 = bf16[16,4,128,128]{3,2,1,0:T(8,128)(2,1)} copy-done((bf16[16,4,128,128]{3,2,1,0:T(8,128)(2,1)}, bf16[16,4,128,128]{3,2,1,0:T(8,128)(2,1)S(1)}, u32[]{:S(2)}) %copy-start.1) | copy-done | bytes 2097176
  25.3 8.5 %all-to-all-done.one_ref = bf16[32,48,256]{2,1,0:T(8,128)(2,1)S(1)} async-done(((bf16[32,48,256]{2,1,0:T(8,128)(2,1)}), bf16[32,48,256]{2,1,0:T(8,128)(2,1)S(1)}, u32[]{:S(2)}, u32[]{:S(2)}) %all-to-all-start) | async-done | bytes 786464 | tf_op jit(solution)/shard_map/all_to_all | solution.py:311
  33.9 1.6 %copy-done.2 = bf16[16,4,128,128]{3,2,1,0:T(8,128)(2,1)S(1)} copy-done((bf16[16,4,128,128]{3,2,1,0:T(8,128)(2,1)S(1)}, bf16[16,4,128,128]{3,2,1,0:T(8,128)(2,1)}, u32[]{:S(2)}) %copy-start.2) | copy-done | bytes 2097176
  35.5 5.0 %back.1 = bf16[32,48,256]{2,1,0:T(8,128)(2,1)} custom-call(s32[64,4]{1,0:T(8,128)S(1)} %copy.26.source_ref, s32[64]{0:T(128)S(1)} %copy-done.6, bf16[32,48,256]{2,1,0:T(8,128)(2,1)S(1)} %all-to-all-done.one_ref, f32[64,128]{1,0:T(8,128)S(1)} %get-tuple-element.16.scale_ref, bf16[64,4,128,128]{3,2,1,0:T(8,128)(2,1)} %tiles_ref.3, ...), custom_call_target="tpu_custom_call", output_to_operand_aliasing={{}: (6, {})} | custom-call | flops 134217728 | bytes 9437184 | tf_op jit(solution)/shard_map/back/pallas_call | solution.py:271
  40.5 8.4 %all-to-all-start.1 = ((bf16[32,48,256]{2,1,0:T(8,128)(2,1)}), bf16[32,48,256]{2,1,0:T(8,128)(2,1)S(1)}, u32[]{:S(2)}, u32[]{:S(2)}) async-start(bf16[32,48,256]{2,1,0:T(8,128)(2,1)} %back.1), calls=%async_computation.1 | async-start | bytes 1572864 | tf_op jit(solution)/shard_map/all_to_all | solution.py:332
  48.9 1.5 %copy.27 = bf16[1024,512]{0,1:T(8,128)(2,1)S(1)} copy(bf16[1024,512]{1,0:T(8,128)(2,1)} %param.16) | data formatting | bytes 2097152 | tf_op args[6]
  50.5 2.3 %copy.30 = bf16[1024,512]{0,1:T(8,128)(2,1)} copy(bf16[1024,512]{1,0:T(8,128)(2,1)} %param.17) | data formatting | bytes 2097152 | tf_op args[7]
  52.9 1.7 %early.1 = (f32[512,256]{1,0:T(8,128)S(1)}, f32[512,256]{1,0:T(8,128)S(1)}) custom-call(bf16[32,48,256]{2,1,0:T(8,128)(2,1)} %prep.1.mine_ref, bf16[32,48,256]{2,1,0:T(8,128)(2,1)S(1)} %all-to-all-done.one_ref, bf16[512,1024]{1,0:T(8,128)(2,1)S(1)} %bitcast.27, bf16[512,512]{1,0:T(8,128)(2,1)S(1)} %copy-done.3), custom_call_target="tpu_custom_call" | custom-call | flops 419430400 | bytes 4194304 | tf_op jit(solution)/shard_map/early/pallas_call | solution.py:271
  54.7 0.8 copy-done.4
  56.3 12.4 %all-to-all-done.1.two_ref = bf16[32,48,256]{2,1,0:T(8,128)(2,1)S(1)} async-done(((bf16[32,48,256]{2,1,0:T(8,128)(2,1)}), bf16[32,48,256]{2,1,0:T(8,128)(2,1)S(1)}, u32[]{:S(2)}, u32[]{:S(2)}) %all-to-all-start.1) | async-done | bytes 786464 | tf_op jit(solution)/shard_map/all_to_all | solution.py:332
  68.6 4.5 %send.1 = (bf16[4,32,48,128]{3,2,1,0:T(8,128)(2,1)}, bf16[512,256]{1,0:T(8,128)(2,1)}, bf16[512,256]{1,0:T(8,128)(2,1)}) custom-call(s32[1]{0:T(128)} %bitcast.core_ref, bf16[32,48,256]{2,1,0:T(8,128)(2,1)} %prep.1.mine_ref, bf16[32,48,256]{2,1,0:T(8,128)(2,1)S(1)} %all-to-all-done.one_ref, bf16[32,48,256]{2,1,0:T(8,128)(2,1)S(1)} %all-to-all-done.1.two_ref, ...), custom_call_target="tpu_custom_call" | custom-call | flops 838860800 | bytes 6291456 | tf_op jit(solution)/shard_map/send/pallas_call | solution.py:271
  73.1 4.6 %collective-permute-start = (bf16[4,32,48,128]{3,2,1,0:T(8,128)(2,1)}, bf16[4,32,48,128]{3,2,1,0:T(8,128)(2,1)S(1)}, u32[]{:S(2)}, u32[]{:S(2)}) collective-permute-start(bf16[4,32,48,128]{3,2,1,0:T(8,128)(2,1)} %get-tuple-element.23), channel_id=1, source_target_pairs={{0,32},{32,0},{64,96},{96,64},{128,160},{160,128},{192,224},{224,1... | collective-permute-start | bytes 4718600 | tf_op jit(solution)/shard_map/ppermute | solution.py:366
  78.1 1.7 %keep.1 = bf16[4,32,48,128]{3,2,1,0:T(8,128)(2,1)S(1)} custom-call(s32[1]{0:T(128)} %bitcast.core_ref, bf16[32,48,256]{2,1,0:T(8,128)(2,1)} %prep.1.mine_ref, bf16[32,48,256]{2,1,0:T(8,128)(2,1)S(1)} %all-to-all-done.one_ref, bf16[32,48,256]{2,1,0:T(8,128)(2,1)S(1)} %all-to-all-done.1.two_ref, bf16[512,256]{1,0:T(8,128)(2,1)} %get-tuple-element.21.hidden_ref, ...), custom_call_target="tpu_custom_call" | custom-call | flops 419430400 | bytes 3145728 | tf_op jit(solution)/shard_map/keep/pallas_call | solution.py:271
  79.8 1.2 collective-permute-done
  81.0 0.9 pair.1
  82.5 2.7 %collective-permute-start.2 = (bf16[4,8,48,128]{3,2,1,0:T(8,128)(2,1)S(1)}, bf16[4,8,48,128]{3,2,1,0:T(8,128)(2,1)S(1)}, u32[]{:S(2)}, u32[]{:S(2)}) collective-permute-start(bf16[4,8,48,128]{3,2,1,0:T(8,128)(2,1)S(1)} %get-tuple-element.26), channel_id=1, source_target_pairs={{0,64},{1,65},{2,66},{3,67},{4,68},{5,69},{6,70},{7,71},{8,72},{9,... | collective-permute-start | bytes 1179656 | tf_op jit(solution)/shard_map/ppermute | solution.py:386
  85.2 1.9 %collective-permute-start.3 = (bf16[4,8,48,128]{3,2,1,0:T(8,128)(2,1)S(1)}, bf16[4,8,48,128]{3,2,1,0:T(8,128)(2,1)S(1)}, u32[]{:S(2)}, u32[]{:S(2)}) collective-permute-start(bf16[4,8,48,128]{3,2,1,0:T(8,128)(2,1)S(1)} %get-tuple-element.27), channel_id=1, source_target_pairs={{0,72},{1,73},{2,74},{3,75},{4,76},{5,77},{6,78},{7,79},{8,64},{9,... | collective-permute-start | bytes 1179656 | tf_op jit(solution)/shard_map/ppermute | solution.py:386
  87.1 2.7 %collective-permute-done.1.got_one = bf16[4,8,48,128]{3,2,1,0:T(8,128)(2,1)S(1)} collective-permute-done((bf16[4,8,48,128]{3,2,1,0:T(8,128)(2,1)S(1)}, bf16[4,8,48,128]{3,2,1,0:T(8,128)(2,1)S(1)}, u32[]{:S(2)}, u32[]{:S(2)}) %collective-permute-start.1) | collective-permute-done | bytes 393248 | tf_op jit(solution)/shard_map/ppermute | solution.py:386
  89.8 4.4 %collective-permute-done.2.got_two = bf16[4,8,48,128]{3,2,1,0:T(8,128)(2,1)S(1)} collective-permute-done((bf16[4,8,48,128]{3,2,1,0:T(8,128)(2,1)S(1)}, bf16[4,8,48,128]{3,2,1,0:T(8,128)(2,1)S(1)}, u32[]{:S(2)}, u32[]{:S(2)}) %collective-permute-start.2) | collective-permute-done | bytes 393248 | tf_op jit(solution)/shard_map/ppermute | solution.py:386
  94.2 2.3 %collective-permute-done.3.got_three = bf16[4,8,48,128]{3,2,1,0:T(8,128)(2,1)S(1)} collective-permute-done((bf16[4,8,48,128]{3,2,1,0:T(8,128)(2,1)S(1)}, bf16[4,8,48,128]{3,2,1,0:T(8,128)(2,1)S(1)}, u32[]{:S(2)}, u32[]{:S(2)}) %collective-permute-start.3) | collective-permute-done | bytes 393248 | tf_op jit(solution)/shard_map/ppermute | solution.py:386
  96.7 17.8 %all_to_all.15 = bf16[32,48,128]{2,1,0:T(8,128)(2,1)S(1)} all-to-all(bf16[32,48,128]{2,1,0:T(8,128)(2,1)S(1)} %bitcast.29), channel_id=1, replica_groups={{0,1,2,3,4,5,6,7,24,25,26,27,28,29,30,31,192,193,194,195,196,197,198,19..., dimensions={0} | all-to-all | bytes 786432 | tf_op jit(solution)/shard_map/all_to_all | solution.py:411
  114.5 2.8 %collective-permute-start.4 = (f32[48,128]{1,0:T(8,128)S(1)}, f32[48,128]{1,0:T(8,128)S(1)}, u32[]{:S(2)}, u32[]{:S(2)}) collective-permute-start(f32[48,128]{1,0:T(8,128)S(1)} %convert_reduce_fusion), channel_id=1, source_target_pairs={{0,32},{32,0},{64,96},{96,64},{128,160},{160,128},{192,224},{224,1... | collective-permute-start | bytes 73736 | tf_op jit(solution)/shard_map/ppermute | solution.py:415
  117.3 0.8 collective-permute-done.4
  118.2 2.0 %collective-permute-start.6 = (f32[2,48,128]{2,1,0:T(8,128)S(1)}, f32[2,48,128]{2,1,0:T(8,128)S(1)}, u32[]{:S(2)}, u32[]{:S(2)}) collective-permute-start(f32[2,48,128]{2,1,0:T(8,128)S(1)} %pad_maximum_fusion.refs_0_), channel_id=1, source_target_pairs={{0,128},{32,160},{64,192},{96,224},{128,0},{160,32},{192,64},{224,... | collective-permute-start | bytes 147464 | tf_op jit(solution)/shard_map/ppermute | solution.py:418
  120.2 0.9 collective-permute-start.7
  121.2 1.3 %collective-permute-done.5.refs_1_ = f32[2,48,128]{2,1,0:T(8,128)S(1)} collective-permute-done((f32[2,48,128]{2,1,0:T(8,128)S(1)}, f32[2,48,128]{2,1,0:T(8,128)S(1)}, u32[]{:S(2)}, u32[]{:S(2)}) %collective-permute-start.5) | collective-permute-done | bytes 49184 | tf_op jit(solution)/shard_map/ppermute | solution.py:418
  122.5 0.9 collective-permute-done.6.refs_2_
  123.7 1.2 place.1
  (31 shorter events, 2.8 us)
Async XLA Ops:
  0.6 14.0 %copy-start.7 = (s32[64,4]{0,1:T(4,128)S(1)}, s32[64,4]{0,1:T(4,128)}, u32[]{:S(2)}) copy-start(s32[64,4]{0,1:T(4,128)} %param.12) | copy-start | bytes 3076
  0.6 14.1 %copy-start.6 = (s32[64]{0:T(128)S(1)}, s32[64]{0:T(128)}, u32[]{:S(2)}) copy-start(s32[64]{0:T(128)} %count_ref.3) | copy-start | bytes 772
  2.7 31.1 %all-to-all-start = ((bf16[32,48,256]{2,1,0:T(8,128)(2,1)}), bf16[32,48,256]{2,1,0:T(8,128)(2,1)S(1)}, u32[]{:S(2)}, u32[]{:S(2)}) async-start(bf16[32,48,256]{2,1,0:T(8,128)(2,1)} %prep.1.mine_ref), calls=%async_computation | async-start | bytes 1572864 | tf_op jit(solution)/shard_map/all_to_all | solution.py:311
  23.1 0.9 copy-start
  24.0 1.3 %copy-start.1 = (bf16[16,4,128,128]{3,2,1,0:T(8,128)(2,1)}, bf16[16,4,128,128]{3,2,1,0:T(8,128)(2,1)S(1)}, u32[]{:S(2)}) copy-start(bf16[16,4,128,128]{3,2,1,0:T(8,128)(2,1)S(1)} %get-tuple-element.17.front_ref) | copy-start | bytes 6291460
  33.9 1.6 %copy-start.2 = (bf16[16,4,128,128]{3,2,1,0:T(8,128)(2,1)S(1)}, bf16[16,4,128,128]{3,2,1,0:T(8,128)(2,1)}, u32[]{:S(2)}) copy-start(bf16[16,4,128,128]{3,2,1,0:T(8,128)(2,1)} %copy-done.1) | copy-start | bytes 6291460
  40.5 10.0 %copy-start.8 = (s32[2,16]{1,0:T(2,128)S(1)}, s32[2,16]{1,0:T(2,128)}, u32[]{:S(2)}) copy-start(s32[2,16]{1,0:T(2,128)} %param.14) | copy-start | bytes 388
  40.5 28.2 %all-to-all-start.1 = ((bf16[32,48,256]{2,1,0:T(8,128)(2,1)}), bf16[32,48,256]{2,1,0:T(8,128)(2,1)S(1)}, u32[]{:S(2)}, u32[]{:S(2)}) async-start(bf16[32,48,256]{2,1,0:T(8,128)(2,1)} %back.1), calls=%async_computation.1 | async-start | bytes 1572864 | tf_op jit(solution)/shard_map/all_to_all | solution.py:332
  50.4 2.6 %copy-start.3 = (bf16[512,512]{1,0:T(8,128)(2,1)S(1)}, bf16[512,512]{1,0:T(8,128)(2,1)}, u32[]{:S(2)}) copy-start(bf16[512,512]{1,0:T(8,128)(2,1)} %wss_ref.1) | copy-start | bytes 1572868
  54.7 0.8 copy-start.4
  55.5 0.8 copy-start.5
  73.1 7.8 %collective-permute-start = (bf16[4,32,48,128]{3,2,1,0:T(8,128)(2,1)}, bf16[4,32,48,128]{3,2,1,0:T(8,128)(2,1)S(1)}, u32[]{:S(2)}, u32[]{:S(2)}) collective-permute-start(bf16[4,32,48,128]{3,2,1,0:T(8,128)(2,1)} %get-tuple-element.23), channel_id=1, source_target_pairs={{0,32},{32,0},{64,96},{96,64},{128,160},{160,128},{192,224},{224,1... | collective-permute-start | bytes 4718600 | tf_op jit(solution)/shard_map/ppermute | solution.py:366
  81.9 7.9 %collective-permute-start.1 = (bf16[4,8,48,128]{3,2,1,0:T(8,128)(2,1)S(1)}, bf16[4,8,48,128]{3,2,1,0:T(8,128)(2,1)S(1)}, u32[]{:S(2)}, u32[]{:S(2)}) collective-permute-start(bf16[4,8,48,128]{3,2,1,0:T(8,128)(2,1)S(1)} %get-tuple-element.25), channel_id=1, source_target_pairs={{0,8},{1,9},{2,10},{3,11},{4,12},{5,13},{6,14},{7,15},{8,0},{9,1},... | collective-permute-start | bytes 1179656 | tf_op jit(solution)/shard_map/ppermute | solution.py:386
  82.5 11.7 %collective-permute-start.2 = (bf16[4,8,48,128]{3,2,1,0:T(8,128)(2,1)S(1)}, bf16[4,8,48,128]{3,2,1,0:T(8,128)(2,1)S(1)}, u32[]{:S(2)}, u32[]{:S(2)}) collective-permute-start(bf16[4,8,48,128]{3,2,1,0:T(8,128)(2,1)S(1)} %get-tuple-element.26), channel_id=1, source_target_pairs={{0,64},{1,65},{2,66},{3,67},{4,68},{5,69},{6,70},{7,71},{8,72},{9,... | collective-permute-start | bytes 1179656 | tf_op jit(solution)/shard_map/ppermute | solution.py:386
  85.2 11.2 %collective-permute-start.3 = (bf16[4,8,48,128]{3,2,1,0:T(8,128)(2,1)S(1)}, bf16[4,8,48,128]{3,2,1,0:T(8,128)(2,1)S(1)}, u32[]{:S(2)}, u32[]{:S(2)}) collective-permute-start(bf16[4,8,48,128]{3,2,1,0:T(8,128)(2,1)S(1)} %get-tuple-element.27), channel_id=1, source_target_pairs={{0,72},{1,73},{2,74},{3,75},{4,76},{5,77},{6,78},{7,79},{8,64},{9,... | collective-permute-start | bytes 1179656 | tf_op jit(solution)/shard_map/ppermute | solution.py:386
  114.5 3.7 %collective-permute-start.4 = (f32[48,128]{1,0:T(8,128)S(1)}, f32[48,128]{1,0:T(8,128)S(1)}, u32[]{:S(2)}, u32[]{:S(2)}) collective-permute-start(f32[48,128]{1,0:T(8,128)S(1)} %convert_reduce_fusion), channel_id=1, source_target_pairs={{0,32},{32,0},{64,96},{96,64},{128,160},{160,128},{192,224},{224,1... | collective-permute-start | bytes 73736 | tf_op jit(solution)/shard_map/ppermute | solution.py:415
  118.2 4.3 %collective-permute-start.5 = (f32[2,48,128]{2,1,0:T(8,128)S(1)}, f32[2,48,128]{2,1,0:T(8,128)S(1)}, u32[]{:S(2)}, u32[]{:S(2)}) collective-permute-start(f32[2,48,128]{2,1,0:T(8,128)S(1)} %pad_maximum_fusion.refs_0_), channel_id=1, source_target_pairs={{0,64},{32,96},{64,128},{96,160},{128,192},{160,224},{192,0},{224,... | collective-permute-start | bytes 147464 | tf_op jit(solution)/shard_map/ppermute | solution.py:418
  118.2 5.2 %collective-permute-start.6 = (f32[2,48,128]{2,1,0:T(8,128)S(1)}, f32[2,48,128]{2,1,0:T(8,128)S(1)}, u32[]{:S(2)}, u32[]{:S(2)}) collective-permute-start(f32[2,48,128]{2,1,0:T(8,128)S(1)} %pad_maximum_fusion.refs_0_), channel_id=1, source_target_pairs={{0,128},{32,160},{64,192},{96,224},{128,0},{160,32},{192,64},{224,... | collective-permute-start | bytes 147464 | tf_op jit(solution)/shard_map/ppermute | solution.py:418
  120.2 3.5 %collective-permute-start.7 = (f32[2,48,128]{2,1,0:T(8,128)S(1)}, f32[2,48,128]{2,1,0:T(8,128)S(1)}, u32[]{:S(2)}, u32[]{:S(2)}) collective-permute-start(f32[2,48,128]{2,1,0:T(8,128)S(1)} %pad_maximum_fusion.refs_0_), channel_id=1, source_target_pairs={{0,192},{32,224},{64,0},{96,32},{128,64},{160,96},{192,128},{224,1... | collective-permute-start | bytes 147464 | tf_op jit(solution)/shard_map/ppermute | solution.py:418

commit v6 on v5

--- a/solution.py
+++ b/solution.py
@@ -121,18 +121,24 @@
     back_ref[...] = jnp.dot(wss_ref[...], lower(mine_ref), preferred_element_type=F32)
 
 
-def write_half(half, gt_ref, one_ref, two_ref, hidden, d_pre, out_ref):
+def write_half(half, gt_ref, one_ref, two_ref, hidden, d_pre, out_ref, done=None):
     ys, owners, rows, lanes = out_ref.shape
     if half:
         left, right = upper(two_ref), lower(two_ref)
     else:
         left, right = upper(one_ref), gt_ref[...].reshape(hidden.shape)
-    first = lax.dot_general(left, d_pre, LAST, preferred_element_type=F32).astype(BF)
     second = lax.dot_general(hidden, right, LAST, preferred_element_type=F32).astype(BF)
     for y in range(ys):
-        cut = slice(y * lanes, (y + 1) * lanes)
-        out_ref[y, :, :FEATS, :] = first[:, cut].reshape(owners, FEATS, lanes)
-        out_ref[y, :, FEATS:, :] = second[:, cut].reshape(owners, rows - FEATS, lanes)
+        out_ref[y, :, FEATS:, :] = second[:, y * lanes : (y + 1) * lanes].reshape(owners, rows - FEATS, lanes)
+    for part in range(2):
+        span = ys // 2 * lanes
+        first = lax.dot_general(left, d_pre[part * span : (part + 1) * span], LAST, preferred_element_type=F32)
+        first = first.astype(BF)
+        for i in range(ys // 2):
+            cut = first[:, i * lanes : (i + 1) * lanes]
+            out_ref[part * (ys // 2) + i, :, :FEATS, :] = cut.reshape(owners, FEATS, lanes)
+        if done is not None:
+            done(part)
 
 
 def send_kernel(
@@ -145,7 +151,7 @@
     keep_ref,
     wnf_ref,
     wns_ref,
-    send_ref,
+    send_out,
     hidden_out,
     d_pre_out,
     gt_held,
@@ -155,8 +161,10 @@
     wns_held,
     hidden_ref,
     d_pre_ref,
+    send_ref,
     sems,
     out_sems,
+    send_sems,
 ):
     copies = begin(
         [
@@ -190,13 +198,27 @@
     d_pre_ref[...] = ((back + back_held[...]) * slope).astype(BF)
     copies[4].wait()
     leaving = begin([(hidden_ref, hidden_out), (d_pre_ref, d_pre_out)], out_sems)
+    span = send_ref.shape[0] // 2
+    parts = [
+        pltpu.make_async_copy(send_ref.at[pl.ds(i * span, span)], send_out.at[pl.ds(i * span, span)], send_sems.at[i])
+        for i in range(2)
+    ]
     for core in range(2):
 
         @pl.when(core_ref[0] == core)
         def _():
-            write_half(1 - core, gt_held, one_ref, two_ref, hidden_ref[...], d_pre_ref[...], send_ref)
-
-    for copy in leaving:
+            write_half(
+                1 - core,
+                gt_held,
+                one_ref,
+                two_ref,
+                hidden_ref[...],
+                d_pre_ref[...],
+                send_ref,
+                lambda part: parts[part].start(),
+            )
+
+    for copy in leaving + parts:
         copy.wait()
 
 
@@ -347,7 +369,7 @@
         send_kernel,
         "send",
         [SMEM, HBM, VMEM, VMEM, HBM, HBM, VMEM, HBM, HBM],
-        [half, (wide, BF, HBM), (wide, BF, HBM)],
+        [half + (HBM,), (wide, BF, HBM), (wide, BF, HBM)],
         [
             gt,
             pltpu.VMEM(wide, F32),
@@ -356,7 +378,9 @@
             pltpu.VMEM((hidden_width, hidden_width), BF),
             pltpu.VMEM(wide, BF),
             pltpu.VMEM(wide, BF),
+            pltpu.VMEM(*half),
             DMA((5,)),
+            DMA((2,)),
             DMA((2,)),
         ],
         flops=800 << 20,

time: 126 us -> 125 us (level)
  no operation moved by 1% of the time
where the time goes in v6:
time: 125 us
  starting transfers between devices  35.8 us (29%)
  waiting for transfers between devices  34.8 us (28%)
  Pallas kernels  25.5 us (20%)
  blocking collectives  17.8 us (14%)
  local copies, waits for them, and re-layouts  9.53 us (8%)
    pallas_call x9, Pallas kernels, apply(): run(*(pltpu.with_memory_space_constraint(a, pltpu.HBM) if spec is HBM els...  25.5 us
    all_to_all x1, blocking collectives, local(): lax.all_to_all(own.reshape(4 * zs, rows, 128), ('dp', 'feat'), 0, 0, tile...  17.8 us
    all_to_all x1, waiting for transfers between devices, local(): two = exchange(send)  12.4 us
    all_to_all x1, starting transfers between devices, local(): one = exchange(mine)  11.9 us
    ppermute x3, waiting for transfers between devices, trade(): return lax.ppermute(value, ('dp', 'feat'), pairs)  9.37 us
    unnamed x22, local copies, waits for them, and re-layouts  9.36 us
    all_to_all x1, waiting for transfers between devices, local(): one = exchange(mine)  8.55 us
    all_to_all x1, starting transfers between devices, local(): two = exchange(send)  8.37 us
  transfers between devices with their start and end apart: 10, of which 10 were waited for; matrix products, arithmetic and copies ran while one was open for 4% of the time, Pallas kernels for 9%

profile of v6, /device:TPU:1, one launch (start us, length us, event | category | flops | bytes accessed | tf_op | source)
XLA Modules:
  0.0 124.8 jit_solution(16783000497198445033)
XLA Ops:
  0.7 2.1 %prep.1.mine_ref = bf16[32,48,256]{2,1,0:T(8,128)(2,1)} custom-call(bf16[32,8192]{1,0:T(8,128)(2,1)} %x_ref.3, bf16[256,512]{1,0:T(8,128)(2,1)} %g_ref.1), custom_call_target="tpu_custom_call" | custom-call | bytes 1048576 | tf_op jit(solution)/shard_map/prep/pallas_call | solution.py:293
  2.7 11.9 %all-to-all-start = ((bf16[32,48,256]{2,1,0:T(8,128)(2,1)}), bf16[32,48,256]{2,1,0:T(8,128)(2,1)S(1)}, u32[]{:S(2)}, u32[]{:S(2)}) async-start(bf16[32,48,256]{2,1,0:T(8,128)(2,1)} %prep.1.mine_ref), calls=%async_computation | async-start | bytes 1572864 | tf_op jit(solution)/shard_map/all_to_all | solution.py:333
  14.7 8.4 %agg.1 = (bf16[32,48,256]{2,1,0:T(8,128)(2,1)S(1)}, f32[64,128]{1,0:T(8,128)S(1)}, bf16[16,4,128,128]{3,2,1,0:T(8,128)(2,1)S(1)}) custom-call(s32[64,4]{1,0:T(8,128)S(1)} %copy.26.source_ref, s32[64]{0:T(128)S(1)} %copy-done.6, bf16[32,8192]{1,0:T(8,128)(2,1)} %x_ref.3, bf16[64,4,128,128]{3,2,1,0:T(8,128)(2,1)} %tiles_ref.3), custom_call_target="tpu_custom_call" | custom-call | flops 402653184 | bytes 9437184 | tf_op jit(solution)/shard_map/agg/pallas_call | solution.py:293
  23.1 0.9 copy-done
  24.0 1.3 %copy-done.1 = bf16[16,4,128,128]{3,2,1,0:T(8,128)(2,1)} copy-done((bf16[16,4,128,128]{3,2,1,0:T(8,128)(2,1)}, bf16[16,4,128,128]{3,2,1,0:T(8,128)(2,1)S(1)}, u32[]{:S(2)}) %copy-start.1) | copy-done | bytes 2097176
  25.3 8.5 %all-to-all-done.one_ref = bf16[32,48,256]{2,1,0:T(8,128)(2,1)S(1)} async-done(((bf16[32,48,256]{2,1,0:T(8,128)(2,1)}), bf16[32,48,256]{2,1,0:T(8,128)(2,1)S(1)}, u32[]{:S(2)}, u32[]{:S(2)}) %all-to-all-start) | async-done | bytes 786464 | tf_op jit(solution)/shard_map/all_to_all | solution.py:333
  33.9 1.6 %copy-done.2 = bf16[16,4,128,128]{3,2,1,0:T(8,128)(2,1)S(1)} copy-done((bf16[16,4,128,128]{3,2,1,0:T(8,128)(2,1)S(1)}, bf16[16,4,128,128]{3,2,1,0:T(8,128)(2,1)}, u32[]{:S(2)}) %copy-start.2) | copy-done | bytes 2097176
  35.5 5.0 %back.1 = bf16[32,48,256]{2,1,0:T(8,128)(2,1)} custom-call(s32[64,4]{1,0:T(8,128)S(1)} %copy.26.source_ref, s32[64]{0:T(128)S(1)} %copy-done.6, bf16[32,48,256]{2,1,0:T(8,128)(2,1)S(1)} %all-to-all-done.one_ref, f32[64,128]{1,0:T(8,128)S(1)} %get-tuple-element.16.scale_ref, bf16[64,4,128,128]{3,2,1,0:T(8,128)(2,1)} %tiles_ref.3, ...), custom_call_target="tpu_custom_call", output_to_operand_aliasing={{}: (6, {})} | custom-call | flops 134217728 | bytes 9437184 | tf_op jit(solution)/shard_map/back/pallas_call | solution.py:293
  40.5 8.4 %all-to-all-start.1 = ((bf16[32,48,256]{2,1,0:T(8,128)(2,1)}), bf16[32,48,256]{2,1,0:T(8,128)(2,1)S(1)}, u32[]{:S(2)}, u32[]{:S(2)}) async-start(bf16[32,48,256]{2,1,0:T(8,128)(2,1)} %back.1), calls=%async_computation.1 | async-start | bytes 1572864 | tf_op jit(solution)/shard_map/all_to_all | solution.py:354
  48.9 1.5 %copy.27 = bf16[1024,512]{0,1:T(8,128)(2,1)S(1)} copy(bf16[1024,512]{1,0:T(8,128)(2,1)} %param.16) | data formatting | bytes 2097152 | tf_op args[6]
  50.5 2.3 %copy.30 = bf16[1024,512]{0,1:T(8,128)(2,1)} copy(bf16[1024,512]{1,0:T(8,128)(2,1)} %param.17) | data formatting | bytes 2097152 | tf_op args[7]
  52.9 1.7 %early.1 = (f32[512,256]{1,0:T(8,128)S(1)}, f32[512,256]{1,0:T(8,128)S(1)}) custom-call(bf16[32,48,256]{2,1,0:T(8,128)(2,1)} %prep.1.mine_ref, bf16[32,48,256]{2,1,0:T(8,128)(2,1)S(1)} %all-to-all-done.one_ref, bf16[512,1024]{1,0:T(8,128)(2,1)S(1)} %bitcast.27, bf16[512,512]{1,0:T(8,128)(2,1)S(1)} %copy-done.3), custom_call_target="tpu_custom_call" | custom-call | flops 419430400 | bytes 4194304 | tf_op jit(solution)/shard_map/early/pallas_call | solution.py:293
  54.7 0.8 copy-done.4
  56.3 12.4 %all-to-all-done.1.two_ref = bf16[32,48,256]{2,1,0:T(8,128)(2,1)S(1)} async-done(((bf16[32,48,256]{2,1,0:T(8,128)(2,1)}), bf16[32,48,256]{2,1,0:T(8,128)(2,1)S(1)}, u32[]{:S(2)}, u32[]{:S(2)}) %all-to-all-start.1) | async-done | bytes 786464 | tf_op jit(solution)/shard_map/all_to_all | solution.py:354
  68.6 4.3 %send.1 = (bf16[4,32,48,128]{3,2,1,0:T(8,128)(2,1)}, bf16[512,256]{1,0:T(8,128)(2,1)}, bf16[512,256]{1,0:T(8,128)(2,1)}) custom-call(s32[1]{0:T(128)} %bitcast.core_ref, bf16[32,48,256]{2,1,0:T(8,128)(2,1)} %prep.1.mine_ref, bf16[32,48,256]{2,1,0:T(8,128)(2,1)S(1)} %all-to-all-done.one_ref, bf16[32,48,256]{2,1,0:T(8,128)(2,1)S(1)} %all-to-all-done.1.two_ref, ...), custom_call_target="tpu_custom_call" | custom-call | flops 838860800 | bytes 6291456 | tf_op jit(solution)/shard_map/send/pallas_call | solution.py:293
  73.0 4.6 %collective-permute-start = (bf16[4,32,48,128]{3,2,1,0:T(8,128)(2,1)}, bf16[4,32,48,128]{3,2,1,0:T(8,128)(2,1)S(1)}, u32[]{:S(2)}, u32[]{:S(2)}) collective-permute-start(bf16[4,32,48,128]{3,2,1,0:T(8,128)(2,1)} %get-tuple-element.23), channel_id=1, source_target_pairs={{0,32},{32,0},{64,96},{96,64},{128,160},{160,128},{192,224},{224,1... | collective-permute-start | bytes 4718600 | tf_op jit(solution)/shard_map/ppermute | solution.py:390
  77.9 1.7 %keep.1 = bf16[4,32,48,128]{3,2,1,0:T(8,128)(2,1)S(1)} custom-call(s32[1]{0:T(128)} %bitcast.core_ref, bf16[32,48,256]{2,1,0:T(8,128)(2,1)} %prep.1.mine_ref, bf16[32,48,256]{2,1,0:T(8,128)(2,1)S(1)} %all-to-all-done.one_ref, bf16[32,48,256]{2,1,0:T(8,128)(2,1)S(1)} %all-to-all-done.1.two_ref, bf16[512,256]{1,0:T(8,128)(2,1)} %get-tuple-element.21.hidden_ref, ...), custom_call_target="tpu_custom_call" | custom-call | flops 419430400 | bytes 3145728 | tf_op jit(solution)/shard_map/keep/pallas_call | solution.py:293
  79.6 1.2 collective-permute-done
  80.8 0.9 pair.1
  82.3 2.7 %collective-permute-start.2 = (bf16[4,8,48,128]{3,2,1,0:T(8,128)(2,1)S(1)}, bf16[4,8,48,128]{3,2,1,0:T(8,128)(2,1)S(1)}, u32[]{:S(2)}, u32[]{:S(2)}) collective-permute-start(bf16[4,8,48,128]{3,2,1,0:T(8,128)(2,1)S(1)} %get-tuple-element.26), channel_id=1, source_target_pairs={{0,64},{1,65},{2,66},{3,67},{4,68},{5,69},{6,70},{7,71},{8,72},{9,... | collective-permute-start | bytes 1179656 | tf_op jit(solution)/shard_map/ppermute | solution.py:410
  85.1 1.9 %collective-permute-start.3 = (bf16[4,8,48,128]{3,2,1,0:T(8,128)(2,1)S(1)}, bf16[4,8,48,128]{3,2,1,0:T(8,128)(2,1)S(1)}, u32[]{:S(2)}, u32[]{:S(2)}) collective-permute-start(bf16[4,8,48,128]{3,2,1,0:T(8,128)(2,1)S(1)} %get-tuple-element.27), channel_id=1, source_target_pairs={{0,72},{1,73},{2,74},{3,75},{4,76},{5,77},{6,78},{7,79},{8,64},{9,... | collective-permute-start | bytes 1179656 | tf_op jit(solution)/shard_map/ppermute | solution.py:410
  86.9 2.7 %collective-permute-done.1.got_one = bf16[4,8,48,128]{3,2,1,0:T(8,128)(2,1)S(1)} collective-permute-done((bf16[4,8,48,128]{3,2,1,0:T(8,128)(2,1)S(1)}, bf16[4,8,48,128]{3,2,1,0:T(8,128)(2,1)S(1)}, u32[]{:S(2)}, u32[]{:S(2)}) %collective-permute-start.1) | collective-permute-done | bytes 393248 | tf_op jit(solution)/shard_map/ppermute | solution.py:410
  89.6 4.4 %collective-permute-done.2.got_two = bf16[4,8,48,128]{3,2,1,0:T(8,128)(2,1)S(1)} collective-permute-done((bf16[4,8,48,128]{3,2,1,0:T(8,128)(2,1)S(1)}, bf16[4,8,48,128]{3,2,1,0:T(8,128)(2,1)S(1)}, u32[]{:S(2)}, u32[]{:S(2)}) %collective-permute-start.2) | collective-permute-done | bytes 393248 | tf_op jit(solution)/shard_map/ppermute | solution.py:410
  94.0 2.3 %collective-permute-done.3.got_three = bf16[4,8,48,128]{3,2,1,0:T(8,128)(2,1)S(1)} collective-permute-done((bf16[4,8,48,128]{3,2,1,0:T(8,128)(2,1)S(1)}, bf16[4,8,48,128]{3,2,1,0:T(8,128)(2,1)S(1)}, u32[]{:S(2)}, u32[]{:S(2)}) %collective-permute-start.3) | collective-permute-done | bytes 393248 | tf_op jit(solution)/shard_map/ppermute | solution.py:410
  96.5 17.8 %all_to_all.15 = bf16[32,48,128]{2,1,0:T(8,128)(2,1)S(1)} all-to-all(bf16[32,48,128]{2,1,0:T(8,128)(2,1)S(1)} %bitcast.29), channel_id=1, replica_groups={{0,1,2,3,4,5,6,7,24,25,26,27,28,29,30,31,192,193,194,195,196,197,198,19..., dimensions={0} | all-to-all | bytes 786432 | tf_op jit(solution)/shard_map/all_to_all | solution.py:435
  114.4 2.8 %collective-permute-start.4 = (f32[48,128]{1,0:T(8,128)S(1)}, f32[48,128]{1,0:T(8,128)S(1)}, u32[]{:S(2)}, u32[]{:S(2)}) collective-permute-start(f32[48,128]{1,0:T(8,128)S(1)} %convert_reduce_fusion), channel_id=1, source_target_pairs={{0,32},{32,0},{64,96},{96,64},{128,160},{160,128},{192,224},{224,1... | collective-permute-start | bytes 73736 | tf_op jit(solution)/shard_map/ppermute | solution.py:439
  117.2 0.8 collective-permute-done.4
  118.0 2.0 %collective-permute-start.6 = (f32[2,48,128]{2,1,0:T(8,128)S(1)}, f32[2,48,128]{2,1,0:T(8,128)S(1)}, u32[]{:S(2)}, u32[]{:S(2)}) collective-permute-start(f32[2,48,128]{2,1,0:T(8,128)S(1)} %pad_maximum_fusion.refs_0_), channel_id=1, source_target_pairs={{0,128},{32,160},{64,192},{96,224},{128,0},{160,32},{192,64},{224,... | collective-permute-start | bytes 147464 | tf_op jit(solution)/shard_map/ppermute | solution.py:442
  120.1 0.9 collective-permute-start.7
  121.1 1.3 %collective-permute-done.5.refs_1_ = f32[2,48,128]{2,1,0:T(8,128)S(1)} collective-permute-done((f32[2,48,128]{2,1,0:T(8,128)S(1)}, f32[2,48,128]{2,1,0:T(8,128)S(1)}, u32[]{:S(2)}, u32[]{:S(2)}) %collective-permute-start.5) | collective-permute-done | bytes 49184 | tf_op jit(solution)/shard_map/ppermute | solution.py:442
  122.3 0.9 collective-permute-done.6.refs_2_
  123.6 1.2 place.1
  (31 shorter events, 2.8 us)
Async XLA Ops:
  0.6 14.0 %copy-start.7 = (s32[64,4]{0,1:T(4,128)S(1)}, s32[64,4]{0,1:T(4,128)}, u32[]{:S(2)}) copy-start(s32[64,4]{0,1:T(4,128)} %param.12) | copy-start | bytes 3076
  0.6 14.1 %copy-start.6 = (s32[64]{0:T(128)S(1)}, s32[64]{0:T(128)}, u32[]{:S(2)}) copy-start(s32[64]{0:T(128)} %count_ref.3) | copy-start | bytes 772
  2.7 31.1 %all-to-all-start = ((bf16[32,48,256]{2,1,0:T(8,128)(2,1)}), bf16[32,48,256]{2,1,0:T(8,128)(2,1)S(1)}, u32[]{:S(2)}, u32[]{:S(2)}) async-start(bf16[32,48,256]{2,1,0:T(8,128)(2,1)} %prep.1.mine_ref), calls=%async_computation | async-start | bytes 1572864 | tf_op jit(solution)/shard_map/all_to_all | solution.py:333
  23.1 0.9 copy-start
  24.0 1.3 %copy-start.1 = (bf16[16,4,128,128]{3,2,1,0:T(8,128)(2,1)}, bf16[16,4,128,128]{3,2,1,0:T(8,128)(2,1)S(1)}, u32[]{:S(2)}) copy-start(bf16[16,4,128,128]{3,2,1,0:T(8,128)(2,1)S(1)} %get-tuple-element.17.front_ref) | copy-start | bytes 6291460
  33.9 1.6 %copy-start.2 = (bf16[16,4,128,128]{3,2,1,0:T(8,128)(2,1)S(1)}, bf16[16,4,128,128]{3,2,1,0:T(8,128)(2,1)}, u32[]{:S(2)}) copy-start(bf16[16,4,128,128]{3,2,1,0:T(8,128)(2,1)} %copy-done.1) | copy-start | bytes 6291460
  40.5 10.0 %copy-start.8 = (s32[2,16]{1,0:T(2,128)S(1)}, s32[2,16]{1,0:T(2,128)}, u32[]{:S(2)}) copy-start(s32[2,16]{1,0:T(2,128)} %param.14) | copy-start | bytes 388
  40.5 28.2 %all-to-all-start.1 = ((bf16[32,48,256]{2,1,0:T(8,128)(2,1)}), bf16[32,48,256]{2,1,0:T(8,128)(2,1)S(1)}, u32[]{:S(2)}, u32[]{:S(2)}) async-start(bf16[32,48,256]{2,1,0:T(8,128)(2,1)} %back.1), calls=%async_computation.1 | async-start | bytes 1572864 | tf_op jit(solution)/shard_map/all_to_all | solution.py:354
  50.4 2.6 %copy-start.3 = (bf16[512,512]{1,0:T(8,128)(2,1)S(1)}, bf16[512,512]{1,0:T(8,128)(2,1)}, u32[]{:S(2)}) copy-start(bf16[512,512]{1,0:T(8,128)(2,1)} %wss_ref.1) | copy-start | bytes 1572868
  54.7 0.8 copy-start.4
  55.5 0.8 copy-start.5
  73.0 7.8 %collective-permute-start = (bf16[4,32,48,128]{3,2,1,0:T(8,128)(2,1)}, bf16[4,32,48,128]{3,2,1,0:T(8,128)(2,1)S(1)}, u32[]{:S(2)}, u32[]{:S(2)}) collective-permute-start(bf16[4,32,48,128]{3,2,1,0:T(8,128)(2,1)} %get-tuple-element.23), channel_id=1, source_target_pairs={{0,32},{32,0},{64,96},{96,64},{128,160},{160,128},{192,224},{224,1... | collective-permute-start | bytes 4718600 | tf_op jit(solution)/shard_map/ppermute | solution.py:390
  81.7 7.9 %collective-permute-start.1 = (bf16[4,8,48,128]{3,2,1,0:T(8,128)(2,1)S(1)}, bf16[4,8,48,128]{3,2,1,0:T(8,128)(2,1)S(1)}, u32[]{:S(2)}, u32[]{:S(2)}) collective-permute-start(bf16[4,8,48,128]{3,2,1,0:T(8,128)(2,1)S(1)} %get-tuple-element.25), channel_id=1, source_target_pairs={{0,8},{1,9},{2,10},{3,11},{4,12},{5,13},{6,14},{7,15},{8,0},{9,1},... | collective-permute-start | bytes 1179656 | tf_op jit(solution)/shard_map/ppermute | solution.py:410
  82.3 11.7 %collective-permute-start.2 = (bf16[4,8,48,128]{3,2,1,0:T(8,128)(2,1)S(1)}, bf16[4,8,48,128]{3,2,1,0:T(8,128)(2,1)S(1)}, u32[]{:S(2)}, u32[]{:S(2)}) collective-permute-start(bf16[4,8,48,128]{3,2,1,0:T(8,128)(2,1)S(1)} %get-tuple-element.26), channel_id=1, source_target_pairs={{0,64},{1,65},{2,66},{3,67},{4,68},{5,69},{6,70},{7,71},{8,72},{9,... | collective-permute-start | bytes 1179656 | tf_op jit(solution)/shard_map/ppermute | solution.py:410
  85.1 11.2 %collective-permute-start.3 = (bf16[4,8,48,128]{3,2,1,0:T(8,128)(2,1)S(1)}, bf16[4,8,48,128]{3,2,1,0:T(8,128)(2,1)S(1)}, u32[]{:S(2)}, u32[]{:S(2)}) collective-permute-start(bf16[4,8,48,128]{3,2,1,0:T(8,128)(2,1)S(1)} %get-tuple-element.27), channel_id=1, source_target_pairs={{0,72},{1,73},{2,74},{3,75},{4,76},{5,77},{6,78},{7,79},{8,64},{9,... | collective-permute-start | bytes 1179656 | tf_op jit(solution)/shard_map/ppermute | solution.py:410
  114.4 3.7 %collective-permute-start.4 = (f32[48,128]{1,0:T(8,128)S(1)}, f32[48,128]{1,0:T(8,128)S(1)}, u32[]{:S(2)}, u32[]{:S(2)}) collective-permute-start(f32[48,128]{1,0:T(8,128)S(1)} %convert_reduce_fusion), channel_id=1, source_target_pairs={{0,32},{32,0},{64,96},{96,64},{128,160},{160,128},{192,224},{224,1... | collective-permute-start | bytes 73736 | tf_op jit(solution)/shard_map/ppermute | solution.py:439
  118.0 4.3 %collective-permute-start.5 = (f32[2,48,128]{2,1,0:T(8,128)S(1)}, f32[2,48,128]{2,1,0:T(8,128)S(1)}, u32[]{:S(2)}, u32[]{:S(2)}) collective-permute-start(f32[2,48,128]{2,1,0:T(8,128)S(1)} %pad_maximum_fusion.refs_0_), channel_id=1, source_target_pairs={{0,64},{32,96},{64,128},{96,160},{128,192},{160,224},{192,0},{224,... | collective-permute-start | bytes 147464 | tf_op jit(solution)/shard_map/ppermute | solution.py:442
  118.0 5.2 %collective-permute-start.6 = (f32[2,48,128]{2,1,0:T(8,128)S(1)}, f32[2,48,128]{2,1,0:T(8,128)S(1)}, u32[]{:S(2)}, u32[]{:S(2)}) collective-permute-start(f32[2,48,128]{2,1,0:T(8,128)S(1)} %pad_maximum_fusion.refs_0_), channel_id=1, source_target_pairs={{0,128},{32,160},{64,192},{96,224},{128,0},{160,32},{192,64},{224,... | collective-permute-start | bytes 147464 | tf_op jit(solution)/shard_map/ppermute | solution.py:442
  120.1 3.5 %collective-permute-start.7 = (f32[2,48,128]{2,1,0:T(8,128)S(1)}, f32[2,48,128]{2,1,0:T(8,128)S(1)}, u32[]{:S(2)}, u32[]{:S(2)}) collective-permute-start(f32[2,48,128]{2,1,0:T(8,128)S(1)} %pad_maximum_fusion.refs_0_), channel_id=1, source_target_pairs={{0,192},{32,224},{64,0},{96,32},{128,64},{160,96},{192,128},{224,1... | collective-permute-start | bytes 147464 | tf_op jit(solution)/shard_map/ppermute | solution.py:442

commit v7 on v5

--- a/solution.py
+++ b/solution.py
@@ -399,7 +399,7 @@
     own, *sends = call(pair_kernel, "pair", [SMEM, VMEM, VMEM], [four] * 4, size=5 << 20)(
         jnp.stack(slots).reshape(ys * xs).astype(jnp.int32), kept.reshape(parts), other.reshape(parts)
     )
-    got = [trade(sends[m - 1], m) for m in (1, 2, 3)]
+    got = [trade(sends[m - 1], m) for m in (3, 1, 2)]
     (own,) = call(square_kernel, "square", [VMEM] * 4, [four], size=2 << 20)(own, *got)
     lines = (((0, 3), (1, 2)), ((0, 1), (2, 3)))
     groups = [

time: 126 us -> 126 us (level)
  transfers between devices with their start and end apart: 10 -> 10, of which waited for: 10 -> 9; matrix products, arithmetic and copies ran while one was open for 4% -> 4% of each run, Pallas kernels for 9% -> 9%
where the time goes in v7:
time: 126 us; the launch traced here: 125 us
  starting transfers between devices  36 us (29%)
  waiting for transfers between devices  35.1 us (28%)
  Pallas kernels  25.7 us (20%)
  blocking collectives  17.9 us (14%)
  local copies, waits for them, and re-layouts  9.53 us (8%)
    pallas_call x9, Pallas kernels, apply(): run(*(pltpu.with_memory_space_constraint(a, pltpu.HBM) if spec is HBM els...  25.7 us
    all_to_all x1, blocking collectives, local(): lax.all_to_all(own.reshape(4 * zs, rows, 128), ('dp', 'feat'), 0, 0, tile...  17.9 us
    all_to_all x1, waiting for transfers between devices, local(): two = exchange(send)  12.4 us
    all_to_all x1, starting transfers between devices, local(): one = exchange(mine)  11.9 us
    ppermute x3, waiting for transfers between devices, trade(): return lax.ppermute(value, ('dp', 'feat'), pairs)  9.41 us
    unnamed x22, local copies, waits for them, and re-layouts  9.36 us
    all_to_all x1, waiting for transfers between devices, local(): one = exchange(mine)  8.55 us
    all_to_all x1, starting transfers between devices, local(): two = exchange(send)  8.37 us
  transfers between devices with their start and end apart: 10, of which 9 were waited for; matrix products, arithmetic and copies ran while one was open for 4% of the time, Pallas kernels for 9%

profile of v7, /device:TPU:1, one launch (start us, length us, event | category | flops | bytes accessed | tf_op | source)
XLA Modules:
  0.0 125.5 jit_solution(13144922745521961653)
XLA Ops:
  0.7 2.1 %prep.1.mine_ref = bf16[32,48,256]{2,1,0:T(8,128)(2,1)} custom-call(bf16[32,8192]{1,0:T(8,128)(2,1)} %x_ref.3, bf16[256,512]{1,0:T(8,128)(2,1)} %g_ref.1), custom_call_target="tpu_custom_call" | custom-call | bytes 1048576 | tf_op jit(solution)/shard_map/prep/pallas_call | solution.py:271
  2.7 11.9 %all-to-all-start = ((bf16[32,48,256]{2,1,0:T(8,128)(2,1)}), bf16[32,48,256]{2,1,0:T(8,128)(2,1)S(1)}, u32[]{:S(2)}, u32[]{:S(2)}) async-start(bf16[32,48,256]{2,1,0:T(8,128)(2,1)} %prep.1.mine_ref), calls=%async_computation | async-start | bytes 1572864 | tf_op jit(solution)/shard_map/all_to_all | solution.py:311
  14.7 8.4 %agg.1 = (bf16[32,48,256]{2,1,0:T(8,128)(2,1)S(1)}, f32[64,128]{1,0:T(8,128)S(1)}, bf16[16,4,128,128]{3,2,1,0:T(8,128)(2,1)S(1)}) custom-call(s32[64,4]{1,0:T(8,128)S(1)} %copy.26.source_ref, s32[64]{0:T(128)S(1)} %copy-done.6, bf16[32,8192]{1,0:T(8,128)(2,1)} %x_ref.3, bf16[64,4,128,128]{3,2,1,0:T(8,128)(2,1)} %tiles_ref.3), custom_call_target="tpu_custom_call" | custom-call | flops 402653184 | bytes 9437184 | tf_op jit(solution)/shard_map/agg/pallas_call | solution.py:271
  23.1 0.9 copy-done
  24.0 1.3 %copy-done.1 = bf16[16,4,128,128]{3,2,1,0:T(8,128)(2,1)} copy-done((bf16[16,4,128,128]{3,2,1,0:T(8,128)(2,1)}, bf16[16,4,128,128]{3,2,1,0:T(8,128)(2,1)S(1)}, u32[]{:S(2)}) %copy-start.1) | copy-done | bytes 2097176
  25.3 8.6 %all-to-all-done.one_ref = bf16[32,48,256]{2,1,0:T(8,128)(2,1)S(1)} async-done(((bf16[32,48,256]{2,1,0:T(8,128)(2,1)}), bf16[32,48,256]{2,1,0:T(8,128)(2,1)S(1)}, u32[]{:S(2)}, u32[]{:S(2)}) %all-to-all-start) | async-done | bytes 786464 | tf_op jit(solution)/shard_map/all_to_all | solution.py:311
  33.9 1.6 %copy-done.2 = bf16[16,4,128,128]{3,2,1,0:T(8,128)(2,1)S(1)} copy-done((bf16[16,4,128,128]{3,2,1,0:T(8,128)(2,1)S(1)}, bf16[16,4,128,128]{3,2,1,0:T(8,128)(2,1)}, u32[]{:S(2)}) %copy-start.2) | copy-done | bytes 2097176
  35.5 5.0 %back.1 = bf16[32,48,256]{2,1,0:T(8,128)(2,1)} custom-call(s32[64,4]{1,0:T(8,128)S(1)} %copy.26.source_ref, s32[64]{0:T(128)S(1)} %copy-done.6, bf16[32,48,256]{2,1,0:T(8,128)(2,1)S(1)} %all-to-all-done.one_ref, f32[64,128]{1,0:T(8,128)S(1)} %get-tuple-element.16.scale_ref, bf16[64,4,128,128]{3,2,1,0:T(8,128)(2,1)} %tiles_ref.3, ...), custom_call_target="tpu_custom_call", output_to_operand_aliasing={{}: (6, {})} | custom-call | flops 134217728 | bytes 9437184 | tf_op jit(solution)/shard_map/back/pallas_call | solution.py:271
  40.5 8.4 %all-to-all-start.1 = ((bf16[32,48,256]{2,1,0:T(8,128)(2,1)}), bf16[32,48,256]{2,1,0:T(8,128)(2,1)S(1)}, u32[]{:S(2)}, u32[]{:S(2)}) async-start(bf16[32,48,256]{2,1,0:T(8,128)(2,1)} %back.1), calls=%async_computation.1 | async-start | bytes 1572864 | tf_op jit(solution)/shard_map/all_to_all | solution.py:332
  48.9 1.5 %copy.27 = bf16[1024,512]{0,1:T(8,128)(2,1)S(1)} copy(bf16[1024,512]{1,0:T(8,128)(2,1)} %param.16) | data formatting | bytes 2097152 | tf_op args[6]
  50.5 2.3 %copy.30 = bf16[1024,512]{0,1:T(8,128)(2,1)} copy(bf16[1024,512]{1,0:T(8,128)(2,1)} %param.17) | data formatting | bytes 2097152 | tf_op args[7]
  52.9 1.7 %early.1 = (f32[512,256]{1,0:T(8,128)S(1)}, f32[512,256]{1,0:T(8,128)S(1)}) custom-call(bf16[32,48,256]{2,1,0:T(8,128)(2,1)} %prep.1.mine_ref, bf16[32,48,256]{2,1,0:T(8,128)(2,1)S(1)} %all-to-all-done.one_ref, bf16[512,1024]{1,0:T(8,128)(2,1)S(1)} %bitcast.27, bf16[512,512]{1,0:T(8,128)(2,1)S(1)} %copy-done.3), custom_call_target="tpu_custom_call" | custom-call | flops 419430400 | bytes 4194304 | tf_op jit(solution)/shard_map/early/pallas_call | solution.py:271
  54.7 0.8 copy-done.4
  55.5 0.8 copy-done.5
  56.3 12.4 %all-to-all-done.1.two_ref = bf16[32,48,256]{2,1,0:T(8,128)(2,1)S(1)} async-done(((bf16[32,48,256]{2,1,0:T(8,128)(2,1)}), bf16[32,48,256]{2,1,0:T(8,128)(2,1)S(1)}, u32[]{:S(2)}, u32[]{:S(2)}) %all-to-all-start.1) | async-done | bytes 786464 | tf_op jit(solution)/shard_map/all_to_all | solution.py:332
  68.6 4.5 %send.1 = (bf16[4,32,48,128]{3,2,1,0:T(8,128)(2,1)}, bf16[512,256]{1,0:T(8,128)(2,1)}, bf16[512,256]{1,0:T(8,128)(2,1)}) custom-call(s32[1]{0:T(128)} %bitcast.core_ref, bf16[32,48,256]{2,1,0:T(8,128)(2,1)} %prep.1.mine_ref, bf16[32,48,256]{2,1,0:T(8,128)(2,1)S(1)} %all-to-all-done.one_ref, bf16[32,48,256]{2,1,0:T(8,128)(2,1)S(1)} %all-to-all-done.1.two_ref, ...), custom_call_target="tpu_custom_call" | custom-call | flops 838860800 | bytes 6291456 | tf_op jit(solution)/shard_map/send/pallas_call | solution.py:271
  73.1 4.6 %collective-permute-start = (bf16[4,32,48,128]{3,2,1,0:T(8,128)(2,1)}, bf16[4,32,48,128]{3,2,1,0:T(8,128)(2,1)S(1)}, u32[]{:S(2)}, u32[]{:S(2)}) collective-permute-start(bf16[4,32,48,128]{3,2,1,0:T(8,128)(2,1)} %get-tuple-element.23), channel_id=1, source_target_pairs={{0,32},{32,0},{64,96},{96,64},{128,160},{160,128},{192,224},{224,1... | collective-permute-start | bytes 4718600 | tf_op jit(solution)/shard_map/ppermute | solution.py:366
  78.1 1.7 %keep.1 = bf16[4,32,48,128]{3,2,1,0:T(8,128)(2,1)S(1)} custom-call(s32[1]{0:T(128)} %bitcast.core_ref, bf16[32,48,256]{2,1,0:T(8,128)(2,1)} %prep.1.mine_ref, bf16[32,48,256]{2,1,0:T(8,128)(2,1)S(1)} %all-to-all-done.one_ref, bf16[32,48,256]{2,1,0:T(8,128)(2,1)S(1)} %all-to-all-done.1.two_ref, bf16[512,256]{1,0:T(8,128)(2,1)} %get-tuple-element.21.hidden_ref, ...), custom_call_target="tpu_custom_call" | custom-call | flops 419430400 | bytes 3145728 | tf_op jit(solution)/shard_map/keep/pallas_call | solution.py:271
  79.8 1.2 collective-permute-done
  81.0 0.9 pair.1
  81.9 3.1 %collective-permute-start.1 = (bf16[4,8,48,128]{3,2,1,0:T(8,128)(2,1)S(1)}, bf16[4,8,48,128]{3,2,1,0:T(8,128)(2,1)S(1)}, u32[]{:S(2)}, u32[]{:S(2)}) collective-permute-start(bf16[4,8,48,128]{3,2,1,0:T(8,128)(2,1)S(1)} %get-tuple-element.25), channel_id=1, source_target_pairs={{0,72},{1,73},{2,74},{3,75},{4,76},{5,77},{6,78},{7,79},{8,64},{9,... | collective-permute-start | bytes 1179656 | tf_op jit(solution)/shard_map/ppermute | solution.py:386
  84.9 2.2 %collective-permute-start.2 = (bf16[4,8,48,128]{3,2,1,0:T(8,128)(2,1)S(1)}, bf16[4,8,48,128]{3,2,1,0:T(8,128)(2,1)S(1)}, u32[]{:S(2)}, u32[]{:S(2)}) collective-permute-start(bf16[4,8,48,128]{3,2,1,0:T(8,128)(2,1)S(1)} %get-tuple-element.26), channel_id=1, source_target_pairs={{0,8},{1,9},{2,10},{3,11},{4,12},{5,13},{6,14},{7,15},{8,0},{9,1},... | collective-permute-start | bytes 1179656 | tf_op jit(solution)/shard_map/ppermute | solution.py:386
  87.1 4.9 %collective-permute-done.1.got_one = bf16[4,8,48,128]{3,2,1,0:T(8,128)(2,1)S(1)} collective-permute-done((bf16[4,8,48,128]{3,2,1,0:T(8,128)(2,1)S(1)}, bf16[4,8,48,128]{3,2,1,0:T(8,128)(2,1)S(1)}, u32[]{:S(2)}, u32[]{:S(2)}) %collective-permute-start.1) | collective-permute-done | bytes 393248 | tf_op jit(solution)/shard_map/ppermute | solution.py:386
  92.0 4.5 %collective-permute-done.2.got_two = bf16[4,8,48,128]{3,2,1,0:T(8,128)(2,1)S(1)} collective-permute-done((bf16[4,8,48,128]{3,2,1,0:T(8,128)(2,1)S(1)}, bf16[4,8,48,128]{3,2,1,0:T(8,128)(2,1)S(1)}, u32[]{:S(2)}, u32[]{:S(2)}) %collective-permute-start.2) | collective-permute-done | bytes 393248 | tf_op jit(solution)/shard_map/ppermute | solution.py:386
  96.7 17.9 %all_to_all.15 = bf16[32,48,128]{2,1,0:T(8,128)(2,1)S(1)} all-to-all(bf16[32,48,128]{2,1,0:T(8,128)(2,1)S(1)} %bitcast.29), channel_id=1, replica_groups={{0,1,2,3,4,5,6,7,24,25,26,27,28,29,30,31,192,193,194,195,196,197,198,19..., dimensions={0} | all-to-all | bytes 786432 | tf_op jit(solution)/shard_map/all_to_all | solution.py:411
  114.7 3.1 %collective-permute-start.4 = (f32[48,128]{1,0:T(8,128)S(1)}, f32[48,128]{1,0:T(8,128)S(1)}, u32[]{:S(2)}, u32[]{:S(2)}) collective-permute-start(f32[48,128]{1,0:T(8,128)S(1)} %convert_reduce_fusion), channel_id=1, source_target_pairs={{0,32},{32,0},{64,96},{96,64},{128,160},{160,128},{192,224},{224,1... | collective-permute-start | bytes 73736 | tf_op jit(solution)/shard_map/ppermute | solution.py:415
  117.8 0.8 collective-permute-done.4
  118.7 1.9 %collective-permute-start.6 = (f32[2,48,128]{2,1,0:T(8,128)S(1)}, f32[2,48,128]{2,1,0:T(8,128)S(1)}, u32[]{:S(2)}, u32[]{:S(2)}) collective-permute-start(f32[2,48,128]{2,1,0:T(8,128)S(1)} %pad_maximum_fusion.refs_0_), channel_id=1, source_target_pairs={{0,128},{32,160},{64,192},{96,224},{128,0},{160,32},{192,64},{224,... | collective-permute-start | bytes 147464 | tf_op jit(solution)/shard_map/ppermute | solution.py:418
  120.6 0.9 collective-permute-start.7
  121.5 1.5 %collective-permute-done.5.refs_1_ = f32[2,48,128]{2,1,0:T(8,128)S(1)} collective-permute-done((f32[2,48,128]{2,1,0:T(8,128)S(1)}, f32[2,48,128]{2,1,0:T(8,128)S(1)}, u32[]{:S(2)}, u32[]{:S(2)}) %collective-permute-start.5) | collective-permute-done | bytes 49184 | tf_op jit(solution)/shard_map/ppermute | solution.py:418
  123.4 0.8 collective-permute-done.7.refs_3_
  124.2 1.2 place.1
  (31 shorter events, 1.5 us)
Async XLA Ops:
  0.6 14.0 %copy-start.7 = (s32[64,4]{0,1:T(4,128)S(1)}, s32[64,4]{0,1:T(4,128)}, u32[]{:S(2)}) copy-start(s32[64,4]{0,1:T(4,128)} %param.12) | copy-start | bytes 3076
  0.6 14.1 %copy-start.6 = (s32[64]{0:T(128)S(1)}, s32[64]{0:T(128)}, u32[]{:S(2)}) copy-start(s32[64]{0:T(128)} %count_ref.3) | copy-start | bytes 772
  2.7 31.1 %all-to-all-start = ((bf16[32,48,256]{2,1,0:T(8,128)(2,1)}), bf16[32,48,256]{2,1,0:T(8,128)(2,1)S(1)}, u32[]{:S(2)}, u32[]{:S(2)}) async-start(bf16[32,48,256]{2,1,0:T(8,128)(2,1)} %prep.1.mine_ref), calls=%async_computation | async-start | bytes 1572864 | tf_op jit(solution)/shard_map/all_to_all | solution.py:311
  23.1 0.9 copy-start
  24.0 1.3 %copy-start.1 = (bf16[16,4,128,128]{3,2,1,0:T(8,128)(2,1)}, bf16[16,4,128,128]{3,2,1,0:T(8,128)(2,1)S(1)}, u32[]{:S(2)}) copy-start(bf16[16,4,128,128]{3,2,1,0:T(8,128)(2,1)S(1)} %get-tuple-element.17.front_ref) | copy-start | bytes 6291460
  33.9 1.6 %copy-start.2 = (bf16[16,4,128,128]{3,2,1,0:T(8,128)(2,1)S(1)}, bf16[16,4,128,128]{3,2,1,0:T(8,128)(2,1)}, u32[]{:S(2)}) copy-start(bf16[16,4,128,128]{3,2,1,0:T(8,128)(2,1)} %copy-done.1) | copy-start | bytes 6291460
  40.5 10.0 %copy-start.8 = (s32[2,16]{1,0:T(2,128)S(1)}, s32[2,16]{1,0:T(2,128)}, u32[]{:S(2)}) copy-start(s32[2,16]{1,0:T(2,128)} %param.14) | copy-start | bytes 388
  40.5 28.2 %all-to-all-start.1 = ((bf16[32,48,256]{2,1,0:T(8,128)(2,1)}), bf16[32,48,256]{2,1,0:T(8,128)(2,1)S(1)}, u32[]{:S(2)}, u32[]{:S(2)}) async-start(bf16[32,48,256]{2,1,0:T(8,128)(2,1)} %back.1), calls=%async_computation.1 | async-start | bytes 1572864 | tf_op jit(solution)/shard_map/all_to_all | solution.py:332
  50.3 2.6 %copy-start.3 = (bf16[512,512]{1,0:T(8,128)(2,1)S(1)}, bf16[512,512]{1,0:T(8,128)(2,1)}, u32[]{:S(2)}) copy-start(bf16[512,512]{1,0:T(8,128)(2,1)} %wss_ref.1) | copy-start | bytes 1572868
  54.7 0.8 copy-start.4
  55.5 0.8 copy-start.5
  73.1 7.8 %collective-permute-start = (bf16[4,32,48,128]{3,2,1,0:T(8,128)(2,1)}, bf16[4,32,48,128]{3,2,1,0:T(8,128)(2,1)S(1)}, u32[]{:S(2)}, u32[]{:S(2)}) collective-permute-start(bf16[4,32,48,128]{3,2,1,0:T(8,128)(2,1)} %get-tuple-element.23), channel_id=1, source_target_pairs={{0,32},{32,0},{64,96},{96,64},{128,160},{160,128},{192,224},{224,1... | collective-permute-start | bytes 4718600 | tf_op jit(solution)/shard_map/ppermute | solution.py:366
  81.9 10.1 %collective-permute-start.1 = (bf16[4,8,48,128]{3,2,1,0:T(8,128)(2,1)S(1)}, bf16[4,8,48,128]{3,2,1,0:T(8,128)(2,1)S(1)}, u32[]{:S(2)}, u32[]{:S(2)}) collective-permute-start(bf16[4,8,48,128]{3,2,1,0:T(8,128)(2,1)S(1)} %get-tuple-element.25), channel_id=1, source_target_pairs={{0,72},{1,73},{2,74},{3,75},{4,76},{5,77},{6,78},{7,79},{8,64},{9,... | collective-permute-start | bytes 1179656 | tf_op jit(solution)/shard_map/ppermute | solution.py:386
  84.9 11.6 %collective-permute-start.2 = (bf16[4,8,48,128]{3,2,1,0:T(8,128)(2,1)S(1)}, bf16[4,8,48,128]{3,2,1,0:T(8,128)(2,1)S(1)}, u32[]{:S(2)}, u32[]{:S(2)}) collective-permute-start(bf16[4,8,48,128]{3,2,1,0:T(8,128)(2,1)S(1)} %get-tuple-element.26), channel_id=1, source_target_pairs={{0,8},{1,9},{2,10},{3,11},{4,12},{5,13},{6,14},{7,15},{8,0},{9,1},... | collective-permute-start | bytes 1179656 | tf_op jit(solution)/shard_map/ppermute | solution.py:386
  87.1 9.4 %collective-permute-start.3 = (bf16[4,8,48,128]{3,2,1,0:T(8,128)(2,1)S(1)}, bf16[4,8,48,128]{3,2,1,0:T(8,128)(2,1)S(1)}, u32[]{:S(2)}, u32[]{:S(2)}) collective-permute-start(bf16[4,8,48,128]{3,2,1,0:T(8,128)(2,1)S(1)} %get-tuple-element.27), channel_id=1, source_target_pairs={{0,64},{1,65},{2,66},{3,67},{4,68},{5,69},{6,70},{7,71},{8,72},{9,... | collective-permute-start | bytes 1179656 | tf_op jit(solution)/shard_map/ppermute | solution.py:386
  114.7 4.0 %collective-permute-start.4 = (f32[48,128]{1,0:T(8,128)S(1)}, f32[48,128]{1,0:T(8,128)S(1)}, u32[]{:S(2)}, u32[]{:S(2)}) collective-permute-start(f32[48,128]{1,0:T(8,128)S(1)} %convert_reduce_fusion), channel_id=1, source_target_pairs={{0,32},{32,0},{64,96},{96,64},{128,160},{160,128},{192,224},{224,1... | collective-permute-start | bytes 73736 | tf_op jit(solution)/shard_map/ppermute | solution.py:415
  118.7 4.3 %collective-permute-start.5 = (f32[2,48,128]{2,1,0:T(8,128)S(1)}, f32[2,48,128]{2,1,0:T(8,128)S(1)}, u32[]{:S(2)}, u32[]{:S(2)}) collective-permute-start(f32[2,48,128]{2,1,0:T(8,128)S(1)} %pad_maximum_fusion.refs_0_), channel_id=1, source_target_pairs={{0,64},{32,96},{64,128},{96,160},{128,192},{160,224},{192,0},{224,... | collective-permute-start | bytes 147464 | tf_op jit(solution)/shard_map/ppermute | solution.py:418
  118.7 4.7 %collective-permute-start.6 = (f32[2,48,128]{2,1,0:T(8,128)S(1)}, f32[2,48,128]{2,1,0:T(8,128)S(1)}, u32[]{:S(2)}, u32[]{:S(2)}) collective-permute-start(f32[2,48,128]{2,1,0:T(8,128)S(1)} %pad_maximum_fusion.refs_0_), channel_id=1, source_target_pairs={{0,128},{32,160},{64,192},{96,224},{128,0},{160,32},{192,64},{224,... | collective-permute-start | bytes 147464 | tf_op jit(solution)/shard_map/ppermute | solution.py:418
  120.6 3.7 %collective-permute-start.7 = (f32[2,48,128]{2,1,0:T(8,128)S(1)}, f32[2,48,128]{2,1,0:T(8,128)S(1)}, u32[]{:S(2)}, u32[]{:S(2)}) collective-permute-start(f32[2,48,128]{2,1,0:T(8,128)S(1)} %pad_maximum_fusion.refs_0_), channel_id=1, source_target_pairs={{0,192},{32,224},{64,0},{96,32},{128,64},{160,96},{192,128},{224,1... | collective-permute-start | bytes 147464 | tf_op jit(solution)/shard_map/ppermute | solution.py:418
